TPU v7x, 256 devices: a whole 4x4x8 slice. The times are simulated.
256 devices in a mesh: samp: 32 (over z, y), par: 8 (over x, core).
Axes of the slice: x: 4, y: 4, z: 8, core: 2. Of those that a mesh axis runs over, the one named last changes fastest.
Arguments:
- activations: bfloat16 [256, 16, 64, 576], P('samp', 'par'), may hold values from -17 to 17
- cotangents: bfloat16 [256, 16, 64, 576], P('samp', 'par'), may hold values from -0.34999167 to 0.34999167
- spin_bits: int32 [256, 576], P('samp'), may hold values from 0 to 1
- offdiag_energy: float32 [256], P('samp'), may hold values from -24 to 24
Outputs:
- update: float32 [16, 36864], P('par', 'samp')
- coefficients: float32 [256], P('samp')
Inputs may be any that keep to these rules, and one draw needn't show every extreme that they name: `spin_bits`: 1 marks an up spin, 0 a down spin.
All inputs are finite; a program needn't handle non-finite values.
Results may differ from a plain program's by a relative error of at most 0.0078.
The roundings to bfloat16 on the way count: a program that leaves them out, or rounds other values in their place, can miss the bound.
Values may be sent and summed in bfloat16 or wider, within the bound.
A program may use at most 128 MiB of HBM per device.

v0:
```python
import math

import jax
import jax.numpy as jnp
from jax import lax
from jax.sharding import PartitionSpec as P

CH = 64
KK = 9
LAT = 24


def shifted(values_in, row_step, col_step):
    grid = values_in.reshape(values_in.shape[:-1] + (LAT, LAT))
    grid = jnp.roll(grid, (-row_step, -col_step), axis=(-2, -1))
    return grid.reshape(values_in.shape)


def diagonal_energy(spin_bits):
    spin = (2 * spin_bits - 1).astype(jnp.float32).reshape(-1, LAT, LAT)
    nearest = spin * jnp.roll(spin, -1, 1) + spin * jnp.roll(spin, -1, 2)
    diagonal = spin * jnp.roll(spin, (-1, -1), (1, 2)) + spin * jnp.roll(spin, (-1, 1), (1, 2))
    return 0.25 * jnp.sum(nearest + 0.5 * diagonal, axis=(1, 2))


def conv_jacobian(layer_acts, layer_cots):
    pieces = []
    for row_step in (-1, 0, 1):
        for col_step in (-1, 0, 1):
            moved = shifted(layer_acts, row_step, col_step)
            pieces.append(
                jnp.einsum("nix,nox->nio", moved, layer_cots, preferred_element_type=jnp.float32)
            )
    stacked = jnp.stack(pieces, 1)
    return stacked.reshape(stacked.shape[0], KK * CH * CH).astype(jnp.bfloat16)


def on_device(activations, cotangents, spin_bits, offdiag_energy):
    local_rows = activations.shape[0]
    layer_count = activations.shape[1]
    jac_local = jnp.stack(
        [
            conv_jacobian(activations[:, layer], cotangents[:, layer])
            for layer in range(layer_count)
        ],
        1,
    )
    regrouped = lax.all_to_all(jac_local, "samp", split_axis=2, concat_axis=0, tiled=True)
    total_rows = regrouped.shape[0]
    jac_wide = regrouped.astype(jnp.float32)
    mean_col = jnp.mean(jac_wide, axis=0)
    centered = ((jac_wide - mean_col) / math.sqrt(total_rows)).astype(jnp.bfloat16)
    flattened = centered.reshape(total_rows, -1)
    row_block = lax.psum_scatter(
        lax.dot_general(
            flattened, flattened, (((1,), (1,)), ((), ())), preferred_element_type=jnp.float32
        ),
        ("samp", "par"),
        scatter_dimension=0,
        tiled=True,
    )
    gram_matrix = lax.all_gather(row_block, ("samp", "par"), axis=0, tiled=True)
    energy = diagonal_energy(spin_bits) + offdiag_energy
    energy_sum = lax.psum(jnp.sum(energy), "samp")
    mean_energy = energy_sum / total_rows
    residual_local = -(energy - mean_energy) / math.sqrt(total_rows)
    residual_energy = lax.all_gather(residual_local, "samp", axis=0, tiled=True)
    shift_value = 0.01 * jnp.trace(gram_matrix) / total_rows
    system = gram_matrix + shift_value * jnp.eye(total_rows, dtype=jnp.float32)
    factor = jnp.linalg.cholesky(system)
    solution = jax.scipy.linalg.cho_solve((factor, True), residual_energy)
    raw_step = jnp.einsum(
        "n,ncw->cw", solution, centered.astype(jnp.float32), precision=lax.Precision.HIGHEST
    )
    entry_count = layer_count * lax.axis_size("par") * KK * CH * CH
    square_total = lax.psum(jnp.sum(raw_step * raw_step), ("samp", "par"))
    step_scale = jnp.sqrt(square_total / entry_count + 1e-06)
    update = raw_step / step_scale
    own_coeffs = lax.dynamic_slice_in_dim(
        solution, lax.axis_index("samp") * local_rows, local_rows, 0
    )
    return (update, own_coeffs)


def solution(mesh):
    in_specs = (
        P("samp", "par", None, None),
        P("samp", "par", None, None),
        P("samp", None),
        P("samp"),
    )
    out_specs = (P("par", "samp"), P("samp"))
    return jax.shard_map(
        on_device, mesh=mesh, in_specs=in_specs, out_specs=out_specs, check_vma=False
    )
```

profile of v0, /device:TPU:1, one launch (start us, length us, event | category | flops | bytes accessed | tf_op | source)
XLA Modules:
  0.0 735.2 jit_solution(10449382472209300800)
XLA Ops:
  7.2 1.4 slice_bitcast_fusion.1
  9.6 2.5 fusion.9
  12.2 1.3 fusion.90
  13.5 1.9 pad_maximum_fusion
  15.3 1.9 fusion.137
  19.1 1.3 fusion.86
  20.4 2.5 fusion.5
  22.9 1.9 pad_maximum_fusion.2
  24.8 2.0 fusion.141
  32.6 1.0 pad_maximum_fusion.6
  40.2 1.1 copy.120
  41.3 3.1 convert_element_type.48
  44.4 1.6 pad_maximum_fusion.10
  49.7 1.2 pad_maximum_fusion.12
  58.2 28.0 %copy.133 = bf16[8,2,36864]{0,1,2:T(2,128)(2,1)} copy(bf16[8,2,36864]{2,0,1:T(8,128)(2,1)S(1)} %pad_maximum_fusion.16) | data formatting | bytes 2359296 | tf_op jit(solution)/shard_map/stack | solution.py:41
  86.2 22.3 %reshape.211 = bf16[32,2,9216]{2,1,0:T(2,128)(2,1)} reshape(bf16[36864,2,8]{2,1,0:T(2,128)(2,1)} %bitcast.290) | data formatting | bytes 2359296
  108.5 12.2 %all-to-all-start = ((bf16[32,2,9216]{2,1,0:T(2,128)(2,1)}), bf16[32,2,9216]{2,1,0:T(2,128)(2,1)S(1)}, u32[]{:S(2)}, u32[]{:S(2)}) async-start(bf16[32,2,9216]{2,1,0:T(2,128)(2,1)} %reshape.211), calls=%async_computation | async-start | bytes 2359296 | tf_op jit(solution)/shard_map/all_to_all | solution.py:48
  122.4 73.8 %psum.14 = f32[]{:T(128)} all-reduce(f32[]{:T(128)} %fusion.133), channel_id=1, replica_groups=mesh['samp'=32,'par'=8] {'samp'}, use_global_device_ids=true, to_apply=%region_9.10 | all-reduce | flops 1 | bytes 8 | tf_op jit(solution)/shard_map/psum | solution.py:64
  198.1 23.2 %reshape.212 = bf16[36864,2,8]{2,1,0:T(2,128)(2,1)} reshape(bf16[32,2,9216]{2,1,0:T(2,128)(2,1)S(1)} %all-to-all-done) | data formatting | bytes 2359296
  221.3 33.9 %copy.134 = bf16[8,2,36864]{2,0,1:T(8,128)(2,1)S(1)} copy(bf16[8,2,36864]{0,1,2:T(2,128)(2,1)} %bitcast.291) | data formatting | bytes 2359296 | tf_op jit(solution)/shard_map/all_to_all | solution.py:48
  256.2 1.4 fusion.16
  257.8 57.9 %all-reduce.1 = f32[256]{0:T(256)S(1)} all-reduce(f32[256]{0:T(256)S(1)} %multiply_dynamic-update-slice_fusion), channel_id=1, replica_groups=mesh['samp'=32,'par'=8] {'samp'}, use_global_device_ids=true, to_apply=%add.1 | all-reduce | flops 256 | bytes 2048
  315.7 208.0 %all-reduce.5.cloned.1.call-done = f32[256,256]{1,0:T(8,128)} async-done(((f32[256,256]{1,0:T(8,128)}), f32[256,256]{1,0:T(8,128)}) %all-reduce.5.cloned.1.call-update) | async-done | bytes 262160
  524.4 62.4 %all-gather = f32[256,1,256]{2,1,0:T(1,128)S(1)} all-gather(f32[1,1,256]{2,1,0:T(1,128)S(1)} %dynamic-slice_bitcast_fusion), channel_id=1, replica_groups=mesh['samp'=32,'par'=8] {'samp','par'}, dimensions={0}, use_global_device_ids=true | all-gather | bytes 263168 | tf_op jit(solution)/shard_map/all_gather | solution.py:62
  588.5 11.7 %cholesky.49 = f32[128,128]{1,0:T(8,128)S(1)} custom-call(f32[128,128]{1,0:T(8,128)S(1)} %cholesky.115), custom_call_target="Cholesky" | custom-call | tf_op jit(solution)/shard_map/jit(cholesky)/cholesky | solution.py:70
  600.2 9.8 %custom-call.18 = f32[1,128,128]{1,2,0:T(8,128)S(1)} custom-call(f32[1,128,128]{2,1,0:T(8,128)S(1)} %get-tuple-element.79), custom_call_target="InvertDiagBlocksLowerTriangular" | custom-call | tf_op jit(solution)/shard_map/jit(cholesky)/cholesky | solution.py:70
  610.5 11.7 %cholesky.103 = f32[128,128]{1,0:T(8,128)S(1)} custom-call(f32[128,128]{1,0:T(8,128)S(1)} %convolution_subtract_fusion), custom_call_target="Cholesky" | custom-call | tf_op jit(solution)/shard_map/jit(cholesky)/cholesky | solution.py:70
  625.3 4.4 while.1
  626.1 1.4 dynamic-slice.11
  628.2 1.4 dynamic-slice.11
  629.7 19.7 %custom-call.19 = f32[2,128,128]{1,2,0:T(8,128)S(1)} custom-call(f32[2,128,128]{2,1,0:T(8,128)S(1)} %get-tuple-element.9), custom_call_target="InvertDiagBlocksLowerTriangular" | custom-call | tf_op jit(solution)/shard_map/jit(_cho_solve)/triangular_solve | solution.py:71
  652.6 74.2 %psum.15 = f32[]{:T(128)} all-reduce(f32[]{:T(128)} %fusion.124), channel_id=1, replica_groups=mesh['samp'=32,'par'=8] {'samp','par'}, use_global_device_ids=true, to_apply=%region_11.12 | all-reduce | flops 1 | bytes 8 | tf_op jit(solution)/shard_map/psum | solution.py:76
  (166 shorter events, 38.2 us)
Async XLA Ops:
  24.8 2.8 copy-start.5
  24.8 2.8 copy-start.23
  27.6 1.3 copy-start.30
  28.2 1.4 copy-start.16
  29.4 1.3 copy-start.4
  29.5 1.3 copy-start.22
  30.7 1.3 copy-start.9
  31.2 1.4 copy-start.8
  31.2 1.4 copy-start.26
  31.2 1.3 copy-start.27
  33.6 1.3 copy-start.11
  35.4 1.3 copy-start.1
  35.4 1.3 copy-start.20
  37.2 1.3 copy-start.14
  37.8 1.4 copy-start
  37.8 1.4 copy-start.19
  41.3 3.1 copy-start.3
  44.4 1.6 copy-start.31
  46.0 1.3 copy-start.15
  46.5 1.4 copy-start.2
  46.5 1.4 copy-start.21
  47.9 1.3 copy-start.7
  48.3 1.4 copy-start.6
  48.3 1.4 copy-start.24
  48.3 1.3 copy-start.25
  50.9 1.3 copy-start.12
  54.1 1.3 copy-start.13
  54.6 1.3 copy-start.17
  108.5 12.3 %copy-start.28 = (s32[8,576]{1,0:T(8,128)S(1)}, s32[8,576]{1,0:T(8,128)}, u32[]{:S(2)}) copy-start(s32[8,576]{1,0:T(8,128)} %param.6) | copy-start | bytes 55300
  108.5 89.6 %all-to-all-start = ((bf16[32,2,9216]{2,1,0:T(2,128)(2,1)}), bf16[32,2,9216]{2,1,0:T(2,128)(2,1)S(1)}, u32[]{:S(2)}, u32[]{:S(2)}) async-start(bf16[32,2,9216]{2,1,0:T(2,128)(2,1)} %reshape.211), calls=%async_computation | async-start | bytes 2359296 | tf_op jit(solution)/shard_map/all_to_all | solution.py:48
  120.7 76.1 %copy-start.32 = (u32[256]{0:T(256)S(1)}, u32[256]{0:T(256)}, u32[]{:S(2)}) copy-start(u32[256]{0:T(256)} %constant.156) | copy-start | bytes 3076
  120.8 402.9 %all-reduce.5.cloned.1.call-start = ((), (), s32[]{:S(2)}) async-start(), calls=%async_computation.1 | async-start | bytes 524288
  (3 other events, 3.0 us)
Sparse Core Ops, SparseCore 0:
  257.8 265.8 all-reduce.4
where the time goes:
time: 741 us; the launch traced here: 735 us
  blocking collectives  268 us (36%)
  waiting for transfers between devices  208 us (28%)
  local copies, waits for them, and re-layouts  136 us (18%)
  other arithmetic  77.9 us (11%)
  between operations  18.9 us (3%)
  matrix products  13.2 us (2%)
  starting transfers between devices  12.2 us (2%)
    unnamed x2, waiting for transfers between devices  208 us
    psum x1, blocking collectives, on_device(): square_total = lax.psum(jnp.sum(raw_step * raw_step), ('samp', 'par'))  74.2 us
    psum x1, blocking collectives, on_device(): energy_sum = lax.psum(jnp.sum(energy), 'samp')  73.8 us
    all_gather x1, blocking collectives, on_device(): gram_matrix = lax.all_gather(row_block, ('samp', 'par'), axis=0, tiled=True)  62.4 us
    unnamed x1, blocking collectives  57.9 us
    unnamed x72, local copies, waits for them, and re-layouts  56.4 us
    another operation x7, other arithmetic, on_device(): factor = jnp.linalg.cholesky(system)  34.6 us
    all_to_all x1, local copies, waits for them, and re-layouts, on_device(): lax.all_to_all(jac_local, 'samp', split_axis=2, concat_axis=0, tiled=True)  33.9 us
  transfers between devices with their start and end apart: 2, of which 1 were waited for; matrix products, arithmetic and copies ran while one was open for 0% of the time, Pallas kernels for 0%

commit v1 on v0

v1 whole, which is shorter than its diff:
```python
import math

import jax
import jax.numpy as jnp
from jax import lax
from jax.experimental import pallas as pl
from jax.experimental.pallas import tpu as pltpu
from jax.sharding import PartitionSpec as P

CH = 64
KK = 9
LAT = 24
SITES = LAT * LAT
NSAMP = 32
NPAR = 8
NZ = 8
NY = 4
LOCAL = 8
NS = NSAMP * LOCAL
ROWS = KK * CH // NSAMP
CHUNK = ROWS * LOCAL
WIDTH = ROWS * 128
PADK = 640
LAYERS = 2
ENTRIES = 16 * KK * CH * CH
MESH = pl.DeviceIdType.MESH
VMEM_LIMIT = 56 * 1024 * 1024
HIGHEST = lax.Precision.HIGHEST
VMEM = pltpu.VMEM


def rolled(value, amount):
    amount = amount % SITES
    if amount == 0:
        return value
    return jnp.concatenate([value[:, amount:], value[:, :amount]], axis=1)


def column_shift(value, col_step):
    if col_step == 0:
        return value
    column = lax.broadcasted_iota(jnp.int32, value.shape, 1) % LAT
    edge = LAT - 1 if col_step > 0 else 0
    return jnp.where(column == edge, rolled(value, col_step - LAT * col_step), rolled(value, col_step))


def samp_partner(z, y, step):
    high = step % NZ
    hop = lax.select(high % 2 == 1, (high + 1) // 2, NZ - high // 2)
    return ((z + hop) % NZ) * NY + (y + step // NZ) % NY


def diagonal_energy(spin_bits):
    spin = (2 * spin_bits - 1).astype(jnp.float32)
    right = column_shift(spin, 1)
    left = column_shift(spin, -1)
    pairs = spin * rolled(spin, LAT) + spin * right
    corners = spin * rolled(right, LAT) + spin * rolled(left, LAT)
    diag = 0.25 * jnp.sum(pairs + 0.5 * corners, axis=1, keepdims=True)
    wide = jnp.broadcast_to(diag, (LOCAL, 128))
    here = lax.broadcasted_iota(jnp.int32, (LOCAL, 128), 0) == lax.broadcasted_iota(
        jnp.int32, (LOCAL, 128), 1
    )
    return jnp.sum(jnp.where(here, wide, 0.0), axis=0, keepdims=True)


WAVES = 4
PER_WAVE = LOCAL // WAVES
CHIPS = 16
TAIL = 48


def main_kernel(
    act_hbm, cot_hbm, spin_ref, off_ref,
    gram_ref, cent_hbm, energies_ref,
    act_ref, cot_ref, lhs, rhs, wide_rows, send_ref, recv_ref, wide_recv, cent_ref,
    energy_ref, half_ref, first, mine, second,
    act_sem, cot_sem, cent_sem, send_sem, recv_sem, esend_sem, erecv_sem,
    core_sem, s1, r1, s2, r2, s3, r3, s4, r4,
):
    samp = lax.axis_index("samp")
    par = lax.axis_index("par")
    z, y = samp // NY, samp % NY
    x, core = par // 2, par % 2
    chip = y * 4 + x
    sibling = (samp, x * 2 + 1 - core)

    def act_copy(n):
        return pltpu.make_async_copy(act_hbm.at[n], act_ref.at[n], act_sem.at[n])

    def cot_copy(n):
        return pltpu.make_async_copy(cot_hbm.at[n], cot_ref.at[n], cot_sem.at[n])

    for n in range(LOCAL):
        act_copy(n).start()
        cot_copy(n).start()

    def chip_at(step):
        other = (chip + step) % CHIPS
        return other, (z * NY + other // 4, (other % 4) * 2 + core)

    def column_at(step):
        other = (z + step) % NZ
        return other, (other * NY + y, par)

    barrier = pltpu.get_barrier_semaphore()

    def greet(step, carry):
        other = samp_partner(z, y, step)
        pl.semaphore_signal(barrier, inc=1, device_id=(other, par), device_id_type=MESH)
        return carry

    lax.fori_loop(1, NSAMP, greet, 0)

    def greet_chip(step, carry):
        across = (x + 1 + step % 3) % 4
        down = (y + step // 3) % NY
        pl.semaphore_signal(
            barrier, inc=1, device_id=(z * NY + down, across * 2 + core), device_id_type=MESH
        )
        return carry

    lax.fori_loop(0, 12, greet_chip, 0)
    pl.semaphore_signal(barrier, inc=1, device_id=sibling, device_id_type=MESH)

    rhs[...] = jnp.zeros_like(rhs)
    for layer in range(LAYERS):
        edge = layer * PADK + SITES - CH
        lhs[:, :, edge : edge + 128] = jnp.zeros((PER_WAVE, KK * CH, 128), jnp.bfloat16)

    def compute(wave):
        for slot in range(PER_WAVE):
            sample = wave * PER_WAVE + slot
            act_copy(sample).wait()
            cot_copy(sample).wait()
            for layer in range(LAYERS):
                base = layer * PADK
                act = act_ref[sample, layer]
                rhs[slot, layer * CH : (layer + 1) * CH, base : base + SITES] = cot_ref[sample, layer]
                for col_step in (-1, 0, 1):
                    moved = column_shift(act, col_step)
                    for row_step in (-1, 0, 1):
                        tap = 3 * (row_step + 1) + col_step + 1
                        lhs[slot, tap * CH : (tap + 1) * CH, base : base + SITES] = rolled(
                            moved, LAT * row_step
                        )
            out = lax.dot_general(
                lhs[slot], rhs[slot], (((1,), (1,)), ((), ())), preferred_element_type=jnp.float32
            )
            for dest in range(NSAMP):
                wide_rows[dest, pl.ds(sample * ROWS, ROWS), :] = out[dest * ROWS : (dest + 1) * ROWS]

    def wave_copy(other, low, rows):
        return pltpu.make_async_remote_copy(
            src_ref=send_ref.at[other, pl.ds(low, rows)],
            dst_ref=recv_ref.at[samp, pl.ds(low, rows)],
            send_sem=send_sem.at[other],
            recv_sem=recv_sem.at[samp],
            device_id=(other, par),
            device_id_type=MESH,
        )

    def send_wave(low, rows):
        def body(step, carry):
            other = samp_partner(z, y, step)
            send_ref[other, pl.ds(low, rows), :] = wide_rows[other, pl.ds(low, rows), :].astype(
                jnp.bfloat16
            )
            wave_copy(other, low, rows).start()
            return carry

        lax.fori_loop(1, NSAMP, body, 0)

    compute(0)
    pl.semaphore_wait(barrier, NSAMP - 1 + 12 + 1)
    send_wave(0, 32)

    def later(wave, carry):
        compute(wave)

        @pl.when(wave < WAVES - 1)
        def _():
            send_wave(pl.multiple_of(wave * 32, 32), 32)

        @pl.when(wave == WAVES - 1)
        def _():
            send_wave(96, TAIL)

        return carry

    lax.fori_loop(1, WAVES, later, 0)

    flat = diagonal_energy(spin_ref[...])
    energy_ref[...] = jnp.zeros_like(energy_ref)
    energy_ref[:, :LOCAL] = flat[:, :LOCAL] + off_ref[...]

    def energy_copy(other, source):
        return pltpu.make_async_remote_copy(
            src_ref=energy_ref,
            dst_ref=energies_ref.at[source],
            send_sem=esend_sem.at[other],
            recv_sem=erecv_sem.at[source],
            device_id=(other, par),
            device_id_type=MESH,
        )

    def send_energy(step, carry):
        energy_copy(samp_partner(z, y, step), samp).start()
        return carry

    lax.fori_loop(1, NSAMP, send_energy, 0)
    energies_ref[samp] = energy_ref[...]
    wide_recv[pl.ds(pl.multiple_of(samp * CHUNK, CHUNK), CHUNK), :] = (
        wide_rows[samp].astype(jnp.bfloat16).astype(jnp.float32)
    )

    def arrive(step, carry):
        other = samp_partner(z, y, step)
        pltpu.make_async_remote_copy(
            src_ref=send_ref.at[other],
            dst_ref=recv_ref.at[other],
            send_sem=send_sem.at[other],
            recv_sem=recv_sem.at[other],
            device_id=(other, par),
            device_id_type=MESH,
        ).wait_recv()
        wide_recv[pl.ds(pl.multiple_of(other * CHUNK, CHUNK), CHUNK), :] = recv_ref[other].astype(
            jnp.float32
        )
        return carry

    lax.fori_loop(1, NSAMP, arrive, 0)

    def centre(row, carry):
        part = jnp.stack(
            [wide_recv[pl.ds(src * CHUNK + row, LOCAL, stride=ROWS), :] for src in range(NSAMP)]
        )
        mean = jnp.sum(jnp.sum(part, axis=0), axis=0, keepdims=True) / NS
        cent = ((part - mean) / math.sqrt(NS)).reshape(NS, 128)
        cent_ref[:, pl.ds(pl.multiple_of(row * 128, 128), 128)] = cent.astype(jnp.bfloat16)
        return carry

    lax.fori_loop(0, ROWS, centre, 0)
    cent_copy = pltpu.make_async_copy(cent_ref, cent_hbm, cent_sem)
    cent_copy.start()

    def gram_rows(low):
        return lax.dot_general(
            cent_ref[pl.ds(low, 128), :], cent_ref[...], (((1,), (1,)), ((), ())),
            preferred_element_type=jnp.float32,
        )

    mine_low = pl.multiple_of(core * 128, 128)
    core_copy = pltpu.make_async_remote_copy(
        src_ref=half_ref.at[0],
        dst_ref=half_ref.at[1],
        send_sem=core_sem.at[0],
        recv_sem=core_sem.at[1],
        device_id=sibling,
        device_id_type=MESH,
    )
    half_ref[0] = gram_rows(pl.multiple_of((1 - core) * 128, 128))
    core_copy.start()
    half_ref[2] = gram_rows(mine_low)
    core_copy.wait_recv()
    half_ref[2] = half_ref[2] + half_ref[1]

    def rows_of(index):
        return pl.ds(pl.multiple_of(index * 8, 8), 8)

    def gram_block(index):
        return gram_ref.at[pl.ds(pl.multiple_of(mine_low + index * 8, 8), 8)]

    def copy_one(step, landed):
        other, device = chip_at(step)
        return pltpu.make_async_remote_copy(
            src_ref=half_ref.at[2, rows_of(other)],
            dst_ref=first.at[other if landed else chip],
            send_sem=s1.at[other],
            recv_sem=r1.at[other if landed else chip],
            device_id=device,
            device_id_type=MESH,
        )

    def copy_two(step, landed):
        other, device = column_at(step)
        return pltpu.make_async_remote_copy(
            src_ref=mine,
            dst_ref=second.at[other if landed else z],
            send_sem=s2.at[other],
            recv_sem=r2.at[other if landed else z],
            device_id=device,
            device_id_type=MESH,
        )

    def copy_three(step, landed):
        other, device = chip_at(step)
        return pltpu.make_async_remote_copy(
            src_ref=gram_block(chip),
            dst_ref=gram_block(other if landed else chip),
            send_sem=s3.at[other],
            recv_sem=r3.at[other if landed else chip],
            device_id=device,
            device_id_type=MESH,
        )

    def copy_four(index, landed):
        low = (1 - core) * 128 if landed else mine_low
        block = gram_ref.at[pl.ds(pl.multiple_of(low + index * 8, 8), 8)]
        return pltpu.make_async_remote_copy(
            src_ref=block,
            dst_ref=block,
            send_sem=s4.at[index],
            recv_sem=r4.at[index],
            device_id=sibling,
            device_id_type=MESH,
        )

    def run(copy, count):
        def start(step, carry):
            copy(step, False).start()
            return carry

        lax.fori_loop(1, count, start, 0)

    def settle(copy, count):
        def wait(step, carry):
            copy(step, True).wait_recv()
            return carry

        lax.fori_loop(1, count, wait, 0)

    def drain(copy, low, count):
        def wait(step, carry):
            copy(step, False).wait_send()
            return carry

        lax.fori_loop(low, count, wait, 0)

    run(copy_one, CHIPS)
    first[chip] = half_ref[2, rows_of(chip), :]
    settle(copy_one, CHIPS)
    own = jnp.sum(first[...], axis=0)
    mine[...] = own
    run(copy_two, NZ)
    second[z] = own
    settle(copy_two, NZ)
    gram_ref[pl.ds(pl.multiple_of(mine_low + chip * 8, 8), 8), :] = jnp.sum(second[...], axis=0)
    run(copy_three, CHIPS)
    copy_four(chip, False).start()

    def forward(step, carry):
        copy_three(step, True).wait_recv()
        copy_four(chip_at(step)[0], False).start()
        return carry

    lax.fori_loop(1, CHIPS, forward, 0)

    def wait_sent(step, carry):
        other = samp_partner(z, y, step)
        pltpu.make_async_remote_copy(
            src_ref=send_ref.at[other],
            dst_ref=recv_ref.at[samp],
            send_sem=send_sem.at[other],
            recv_sem=recv_sem.at[samp],
            device_id=(other, par),
            device_id_type=MESH,
        ).wait_send()
        energy_copy(other, samp).wait_send()
        energy_copy(other, other).wait_recv()
        return carry

    lax.fori_loop(1, NSAMP, wait_sent, 0)
    core_copy.wait_send()
    drain(copy_one, 1, CHIPS)
    drain(copy_two, 1, NZ)
    drain(copy_three, 1, CHIPS)

    def arrive_four(index, carry):
        copy_four(index, True).wait_recv()
        return carry

    lax.fori_loop(0, CHIPS, arrive_four, 0)
    drain(copy_four, 0, CHIPS)
    cent_copy.wait()


def main_call(activations, cotangents, spin_bits, off_row):
    whole = pl.BlockSpec(memory_space=VMEM)
    anywhere = pl.BlockSpec(memory_space=pl.ANY)
    dma = pltpu.SemaphoreType.DMA
    return pl.pallas_call(
        main_kernel,
        in_specs=[anywhere, anywhere, whole, whole],
        out_specs=[whole, anywhere, whole],
        out_shape=[
            jax.ShapeDtypeStruct((NS, NS), jnp.float32),
            jax.ShapeDtypeStruct((NS, WIDTH), jnp.bfloat16),
            jax.ShapeDtypeStruct((NSAMP, 1, 128), jnp.float32),
        ],
        scratch_shapes=[
            VMEM((LOCAL, LAYERS, CH, SITES), jnp.bfloat16),
            VMEM((LOCAL, LAYERS, CH, SITES), jnp.bfloat16),
            VMEM((PER_WAVE, KK * CH, LAYERS * PADK), jnp.bfloat16),
            VMEM((PER_WAVE, LAYERS * CH, LAYERS * PADK), jnp.bfloat16),
            VMEM((NSAMP, CHUNK, 128), jnp.float32),
            VMEM((NSAMP, CHUNK, 128), jnp.bfloat16),
            VMEM((NSAMP, CHUNK, 128), jnp.bfloat16),
            VMEM((NSAMP * CHUNK, 128), jnp.float32),
            VMEM((NS, WIDTH), jnp.bfloat16),
            VMEM((1, 128), jnp.float32),
            VMEM((3, 128, NS), jnp.float32),
            VMEM((CHIPS, 8, NS), jnp.float32),
            VMEM((8, NS), jnp.float32),
            VMEM((NZ, 8, NS), jnp.float32),
            dma((LOCAL,)),
            dma((LOCAL,)),
            dma,
            dma((NSAMP,)),
            dma((NSAMP,)),
            dma((NSAMP,)),
            dma((NSAMP,)),
            dma((2,)),
            dma((CHIPS,)),
            dma((CHIPS,)),
            dma((NZ,)),
            dma((NZ,)),
            dma((CHIPS,)),
            dma((CHIPS,)),
            dma((CHIPS,)),
            dma((CHIPS,)),
        ],
        compiler_params=pltpu.CompilerParams(
            collective_id=0, has_side_effects=True, vmem_limit_bytes=VMEM_LIMIT
        ),
    )(activations, cotangents, spin_bits, off_row)


BLOCK = 64
PANEL = 8


def spread(value, row, col):
    return jnp.broadcast_to(value[row : row + 1, col : col + 1], (8, 128))


def invert_block(diag):
    eye = lax.broadcasted_iota(jnp.int32, (BLOCK, BLOCK), 0) == lax.broadcasted_iota(
        jnp.int32, (BLOCK, BLOCK), 1
    )
    wide = jnp.concatenate([diag, jnp.where(eye, 1.0, 0.0)], axis=1)
    tiles = [wide[8 * q : 8 * q + 8] for q in range(BLOCK // 8)]
    sub = lax.broadcasted_iota(jnp.int32, (8, 128), 0)
    for panel in range(BLOCK // PANEL):
        tile = tiles[panel]
        base = panel * PANEL
        low = {
            (i, j): spread(tile, i, base + j) for i in range(PANEL) for j in range(i + 1)
        }
        rows = [jnp.broadcast_to(tile[i : i + 1], (8, 128)) for i in range(PANEL)]
        factor = {}
        inverse = []
        for j in range(PANEL):
            recip = 1.0 / low[j, j]
            inverse.append(recip)
            for i in range(j + 1, PANEL):
                factor[i, j] = low[i, j] * recip
            for i in range(j + 1, PANEL):
                rows[i] = rows[i] - factor[i, j] * rows[j]
                for m in range(j + 1, i + 1):
                    low[i, m] = low[i, m] - factor[i, j] * low[m, j]
        solved = [None] * PANEL
        for i in reversed(range(PANEL)):
            total = rows[i] * inverse[i]
            for j in range(i + 1, PANEL):
                total = total - factor[j, i] * solved[j]
            solved[i] = total
        for q in range(BLOCK // 8):
            if q == panel:
                continue
            old = tiles[q]
            terms = [
                jnp.broadcast_to(old[:, base + i : base + i + 1], (8, 128)) * solved[i]
                for i in range(PANEL)
            ]
            while len(terms) > 1:
                terms = [terms[a] + terms[a + 1] for a in range(0, len(terms), 2)]
            tiles[q] = old - terms[0]
        joined = solved[0]
        for i in range(1, PANEL):
            joined = jnp.where(sub == i, solved[i], joined)
        tiles[panel] = joined
    return jnp.concatenate(tiles, axis=0)[:, BLOCK:]


def solve_kernel(gram_ref, energies_ref, cent_ref, update_ref, coeff_ref, work, held):
    rows_iota = lax.broadcasted_iota(jnp.int32, (NS, NS), 0)
    cols_iota = lax.broadcasted_iota(jnp.int32, (NS, NS), 1)
    gram = gram_ref[...]
    diagonal = rows_iota == cols_iota
    trace = jnp.sum(jnp.where(diagonal, gram, 0.0), keepdims=True)
    shift = 0.01 * trace / NS
    pieces = jnp.broadcast_to(energies_ref[...], (NSAMP, LOCAL, 128)).reshape(NS, 128)
    lane = lax.broadcasted_iota(jnp.int32, (NS, 128), 1)
    row = lax.broadcasted_iota(jnp.int32, (NS, 128), 0)
    energy = jnp.sum(jnp.where(lane == row % LOCAL, pieces, 0.0), axis=1, keepdims=True)
    mean = jnp.sum(energy, axis=0, keepdims=True) / NS
    residual = -(energy - mean) / math.sqrt(NS)
    work[:, :NS] = gram + jnp.where(diagonal, shift, 0.0)
    work[:, NS:] = jnp.broadcast_to(residual, (NS, 128))

    def step(index, carry):
        own = pl.ds(pl.multiple_of(index * BLOCK, BLOCK), BLOCK)
        panel = work[own, :]
        inverse = invert_block(panel[:, :BLOCK])
        solved = jnp.dot(inverse, panel, precision=HIGHEST, preferred_element_type=jnp.float32)
        held[...] = work[...] - jnp.dot(
            work[:, :BLOCK], solved, precision=HIGHEST, preferred_element_type=jnp.float32
        )
        held[own, :] = solved
        work[:, : NS - BLOCK] = held[:, BLOCK:NS]
        work[:, NS - BLOCK : NS] = held[:, :BLOCK]
        work[:, NS:] = held[:, NS:]
        return carry

    lax.fori_loop(0, NS // BLOCK, step, 0)
    coeff = work[:, NS:]
    held[:, NS:] = coeff
    coeff_ref[...] = held[pl.ds(pl.multiple_of(lax.axis_index("samp") * LOCAL, LOCAL), LOCAL), NS:]
    image = jnp.zeros((8, 128), jnp.float32)
    both = jnp.concatenate([coeff, coeff], axis=1)
    weighted = jnp.sum(gram * both, axis=0, keepdims=True)
    across = jnp.sum(jnp.where(diagonal, both, 0.0), axis=0, keepdims=True)
    square_total = jnp.sum(weighted * across, keepdims=True)
    scale = lax.rsqrt(square_total / ENTRIES + 1e-06)
    first = lax.broadcasted_iota(jnp.int32, (1, 128), 1) < CH
    for pair in range(ROWS // 2):
        parts = []
        for half in range(2):
            column = 128 * (2 * pair + half)
            cent = cent_ref[:, column : column + 128].astype(jnp.float32)
            parts.append(jnp.sum(cent * coeff, axis=0, keepdims=True) * scale)
        turned = [jnp.concatenate([item[:, CH:], item[:, :CH]], axis=1) for item in parts]
        update_ref[0:1, 128 * pair : 128 * pair + 128] = jnp.where(first, parts[0], turned[1])
        update_ref[1:2, 128 * pair : 128 * pair + 128] = jnp.where(first, turned[0], parts[1])


def solve_call(gram, energies, cent):
    whole = pl.BlockSpec(memory_space=VMEM)
    return pl.pallas_call(
        solve_kernel,
        in_specs=[whole] * 3,
        out_specs=[whole, whole],
        out_shape=[
            jax.ShapeDtypeStruct((LAYERS, ROWS * CH), jnp.float32),
            jax.ShapeDtypeStruct((LOCAL, 128), jnp.float32),
        ],
        scratch_shapes=[VMEM((NS, NS + 128), jnp.float32), VMEM((NS, NS + 128), jnp.float32)],
        compiler_params=pltpu.CompilerParams(vmem_limit_bytes=VMEM_LIMIT),
    )(gram, energies, cent)


def on_device(activations, cotangents, spin_bits, offdiag_energy):
    gram, cent, energies = main_call(
        activations, cotangents, spin_bits, offdiag_energy.reshape(1, LOCAL)
    )
    update, coeff = solve_call(gram, energies, cent)
    return update, coeff[:, 0]


def solution(mesh):
    in_specs = (
        P("samp", "par", None, None),
        P("samp", "par", None, None),
        P("samp", None),
        P("samp"),
    )
    out_specs = (P("par", "samp"), P("samp"))
    return jax.shard_map(
        on_device, mesh=mesh, in_specs=in_specs, out_specs=out_specs, check_vma=False
    )
```

time: 741 us -> 85.5 us (0.12)
  blocking collectives: 268 us -> 0 us
  waiting for transfers between devices: 208 us -> 0 us
  local copies, waits for them, and re-layouts: 136 us -> 1.31 us
  Pallas kernels: 0 us -> 83.4 us
  other arithmetic: 77.9 us -> 0 us
  between operations: 18.9 us -> 0.64 us
  matrix products: 13.2 us -> 0 us
  starting transfers between devices: 12.2 us -> 0 us
    unnamed x2 -> x0, waiting for transfers between devices: 208 us -> none
    psum x2 -> x0, blocking collectives: 148 us -> none  [the longest x1 74.2 us: on_device(): square_total = lax.psum(jnp.sum(raw_step * raw_step), ('samp', 'par'))]
    pallas_call x0 -> x2, Pallas kernels: none -> 83.4 us  [the longest x1 65.1 us: main_call(): pl.pallas_call(main_kernel, in_specs=[anywhere, anywhere, whole, whole],...]
    all_gather x1 -> x0, blocking collectives: 62.4 us -> none  [on_device(): gram_matrix = lax.all_gather(row_block, ('samp', 'par'), axis=0, tiled=True)]
    unnamed x1 -> x0, blocking collectives: 57.9 us -> none
    unnamed x72 -> x0, local copies, waits for them, and re-layouts: 56.4 us -> none
    another operation x11 -> x0, other arithmetic: 54.4 us -> none  [the longest x7 34.6 us: on_device(): factor = jnp.linalg.cholesky(system)]
    all_to_all x1 -> x0, local copies, waits for them, and re-layouts: 33.9 us -> none  [on_device(): lax.all_to_all(jac_local, 'samp', split_axis=2, concat_axis=0, tiled=True)]
  transfers between devices with their start and end apart: 2 -> 0, of which waited for: 1 -> 0; matrix products, arithmetic and copies ran while one was open for 0% -> 0% of each run, Pallas kernels for 0% -> 0%
where the time goes in v1:
time: 85.5 us; the launch traced here: 85.3 us
  Pallas kernels  83.4 us (98%)
  local copies, waits for them, and re-layouts  1.31 us (2%)
    pallas_call x1, Pallas kernels, main_call(): pl.pallas_call(main_kernel, in_specs=[anywhere, anywhere, whole, whole],...  65.1 us
    pallas_call x1, Pallas kernels, solve_call(): pl.pallas_call(solve_kernel, in_specs=[whole] * 3, out_specs=[whole, whol...  18.2 us

profile of v1, /device:TPU:1, one launch (start us, length us, event | category | flops | bytes accessed | tf_op | source)
XLA Modules:
  0.0 85.3 jit_solution(15342658304740377331)
XLA Ops:
  0.6 65.1 %shard_map.59 = (f32[256,256]{1,0:T(8,128)}, bf16[256,2304]{1,0:T(8,128)(2,1)}, f32[32,1,128]{2,1,0:T(1,128)}) custom-call(bf16[8,2,64,576]{3,2,1,0:T(8,128)(2,1)} %act_hbm.1, bf16[8,2,64,576]{3,2,1,0:T(8,128)(2,1)} %cot_hbm.1, s32[8,576]{1,0:T(8,128)} %spin_ref.1, f32[1,8]{1,0:T(1,128)} %bitcast.1), custom_call_target="tpu_custom_call" | custom-call | tf_op jit(solution)/shard_map/pallas_call | solution.py:392
  65.8 18.2 %shard_map.60 = (f32[2,1152]{1,0:T(2,128)}, f32[8,128]{1,0:T(8,128)}) custom-call(f32[256,256]{1,0:T(8,128)} %get-tuple-element.7.gram_ref, f32[32,1,128]{2,1,0:T(1,128)} %get-tuple-element.8.energies_ref, bf16[256,2304]{1,0:T(8,128)(2,1)} %get-tuple-element.9.cent_ref), custom_call_target="tpu_custom_call" | custom-call | tf_op jit(solution)/shard_map/pallas_call | solution.py:550
  84.0 1.3 %slice_reduce_fusion = f32[8]{0:T(128)} fusion(f32[8,128]{1,0:T(8,128)} %get-tuple-element.11), kind=kLoop, calls=%fused_computation | loop fusion | bytes 64 | tf_op jit(solution)/shard_map/slice | solution.py:568

commit v2 on v1

v2 whole, which is shorter than its diff:
```python
import math

import jax
import jax.numpy as jnp
from jax import lax
from jax.experimental import pallas as pl
from jax.experimental.pallas import tpu as pltpu
from jax.sharding import PartitionSpec as P

CH = 64
KK = 9
LAT = 24
SITES = LAT * LAT
NSAMP = 32
NPAR = 8
NZ = 8
NY = 4
LOCAL = 8
NS = NSAMP * LOCAL
ROWS = KK * CH // NSAMP
CHUNK = ROWS * LOCAL
WIDTH = ROWS * 128
PADK = 640
LAYERS = 2
ENTRIES = 16 * KK * CH * CH
MESH = pl.DeviceIdType.MESH
VMEM_LIMIT = 56 * 1024 * 1024
HIGHEST = lax.Precision.HIGHEST
VMEM = pltpu.VMEM


def rolled(value, amount):
    amount = amount % SITES
    if amount == 0:
        return value
    return jnp.concatenate([value[:, amount:], value[:, :amount]], axis=1)


def column_shift(value, col_step):
    if col_step == 0:
        return value
    column = lax.broadcasted_iota(jnp.int32, value.shape, 1) % LAT
    edge = LAT - 1 if col_step > 0 else 0
    return jnp.where(column == edge, rolled(value, col_step - LAT * col_step), rolled(value, col_step))


def wrap(value, size):
    return lax.select(value >= size, value - size, value)


STEPS = [(down, hop) for down in range(NY) for hop in (1, 7, 2, 6, 3, 5, 4, 0) if (down, hop) != (0, 0)]


def diagonal_energy(spin_bits):
    spin = (2 * spin_bits - 1).astype(jnp.float32)
    right = column_shift(spin, 1)
    left = column_shift(spin, -1)
    pairs = spin * rolled(spin, LAT) + spin * right
    corners = spin * rolled(right, LAT) + spin * rolled(left, LAT)
    diag = 0.25 * jnp.sum(pairs + 0.5 * corners, axis=1, keepdims=True)
    wide = jnp.broadcast_to(diag, (LOCAL, 128))
    here = lax.broadcasted_iota(jnp.int32, (LOCAL, 128), 0) == lax.broadcasted_iota(
        jnp.int32, (LOCAL, 128), 1
    )
    return jnp.sum(jnp.where(here, wide, 0.0), axis=0, keepdims=True)


WAVES = 4
PER_WAVE = LOCAL // WAVES
CHIPS = 16
TAIL = 48


def main_kernel(
    act_hbm, cot_hbm, spin_ref, off_ref,
    gram_ref, cent_hbm, energies_ref,
    act_ref, cot_ref, lhs, rhs, wide_rows, send_ref, recv_ref, wide_recv, cent_ref,
    energy_ref, half_ref, first, mine, second,
    act_sem, cot_sem, cent_sem, send_sem, recv_sem, esem, core_sem, sem1, sem2, sem3, sem4,
):
    samp = lax.axis_index("samp")
    par = lax.axis_index("par")
    z, y = samp // NY, samp % NY
    x, core = par // 2, par % 2
    chip = y * 4 + x
    slot_here = y * NZ + z
    sibling = (samp, x * 2 + 1 - core)
    zs = [wrap(z + hop, NZ) for hop in range(NZ)]
    ys = [wrap(y + down, NY) for down in range(NY)]
    xs = [wrap(x + across, 4) for across in range(4)]
    partners = [(down, zs[hop] * NY + ys[down]) for down, hop in STEPS]
    chips = [
        (ys[down] * 4 + xs[across], (z * NY + ys[down], xs[across] * 2 + core))
        for down in range(NY)
        for across in range(4)
        if (down, across) != (0, 0)
    ]

    def act_copy(n):
        return pltpu.make_async_copy(act_hbm.at[n], act_ref.at[n], act_sem.at[n])

    def cot_copy(n):
        return pltpu.make_async_copy(cot_hbm.at[n], cot_ref.at[n], cot_sem.at[n])

    for n in range(LOCAL):
        act_copy(n).start()
        cot_copy(n).start()

    def remote(source, target, send, recv, device):
        return pltpu.make_async_remote_copy(
            src_ref=source,
            dst_ref=target,
            send_sem=send,
            recv_sem=recv,
            device_id=device,
            device_id_type=MESH,
        )

    barrier = pltpu.get_barrier_semaphore()
    greeted = 0
    for _, other in partners:
        pl.semaphore_signal(barrier, inc=1, device_id=(other, par), device_id_type=MESH)
        greeted += 1
    for down in range(NY):
        for across in range(1, 4):
            device = (z * NY + ys[down], xs[across] * 2 + core)
            pl.semaphore_signal(barrier, inc=1, device_id=device, device_id_type=MESH)
            greeted += 1
    pl.semaphore_signal(barrier, inc=1, device_id=sibling, device_id_type=MESH)
    greeted += 1

    rhs[...] = jnp.zeros_like(rhs)
    for layer in range(LAYERS):
        edge = layer * PADK + SITES - CH
        lhs[:, :, edge : edge + 128] = jnp.zeros((PER_WAVE, KK * CH, 128), jnp.bfloat16)

    def compute(wave):
        for slot in range(PER_WAVE):
            sample = wave * PER_WAVE + slot
            act_copy(sample).wait()
            cot_copy(sample).wait()
            for layer in range(LAYERS):
                base = layer * PADK
                act = act_ref[sample, layer]
                rhs[slot, layer * CH : (layer + 1) * CH, base : base + SITES] = cot_ref[sample, layer]
                for col_step in (-1, 0, 1):
                    moved = column_shift(act, col_step)
                    for row_step in (-1, 0, 1):
                        tap = 3 * (row_step + 1) + col_step + 1
                        lhs[slot, tap * CH : (tap + 1) * CH, base : base + SITES] = rolled(
                            moved, LAT * row_step
                        )
            out = lax.dot_general(
                lhs[slot], rhs[slot], (((1,), (1,)), ((), ())), preferred_element_type=jnp.float32
            )
            for dest in range(NSAMP):
                wide_rows[dest, pl.ds(sample * ROWS, ROWS), :] = out[dest * ROWS : (dest + 1) * ROWS]

    def send_wave(low, rows):
        for down, other in partners:
            send_ref[other, pl.ds(low, rows), :] = wide_rows[other, pl.ds(low, rows), :].astype(
                jnp.bfloat16
            )
            remote(
                send_ref.at[other, pl.ds(low, rows)],
                recv_ref.at[slot_here, pl.ds(low, rows)],
                send_sem,
                recv_sem.at[down],
                (other, par),
            ).start()

    compute(0)
    pl.semaphore_wait(barrier, greeted)
    send_wave(0, 32)

    def later(wave, carry):
        compute(wave)

        @pl.when(wave < WAVES - 1)
        def _():
            send_wave(pl.multiple_of(wave * 32, 32), 32)

        @pl.when(wave == WAVES - 1)
        def _():
            send_wave(96, TAIL)

        return carry

    lax.fori_loop(1, WAVES, later, 0)

    flat = diagonal_energy(spin_ref[...])
    energy_ref[...] = jnp.zeros_like(energy_ref)
    energy_ref[:, :LOCAL] = flat[:, :LOCAL] + off_ref[...]
    for _, other in partners:
        remote(energy_ref, energies_ref.at[samp], esem.at[0], esem.at[1], (other, par)).start()
    energies_ref[samp] = energy_ref[...]
    recv_ref[slot_here] = wide_rows[samp].astype(jnp.bfloat16)

    group = NZ * CHUNK
    for down in range(NY):
        low = wrap(y + NY - down, NY) * NZ
        taken = recv_ref.at[pl.ds(0, NZ - 1)] if down == 0 else recv_ref.at[pl.ds(low, NZ)]
        remote(taken, taken, send_sem, recv_sem.at[down], sibling).wait_recv()
        start = pl.multiple_of(low * CHUNK, group)
        wide_recv[pl.ds(start, group), :] = (
            recv_ref[pl.ds(low, NZ)].astype(jnp.float32).reshape(group, 128)
        )

    def centre(row, carry):
        part = jnp.stack(
            [
                wide_recv[pl.ds(((src % NY) * NZ + src // NY) * CHUNK + row, LOCAL, stride=ROWS), :]
                for src in range(NSAMP)
            ]
        )
        mean = jnp.sum(jnp.sum(part, axis=0), axis=0, keepdims=True) / NS
        cent = ((part - mean) / math.sqrt(NS)).reshape(NS, 128)
        cent_ref[:, pl.ds(pl.multiple_of(row * 128, 128), 128)] = cent.astype(jnp.bfloat16)
        return carry

    lax.fori_loop(0, ROWS, centre, 0)
    cent_copy = pltpu.make_async_copy(cent_ref, cent_hbm, cent_sem)
    cent_copy.start()

    def gram_rows(low):
        return lax.dot_general(
            cent_ref[pl.ds(low, 128), :], cent_ref[...], (((1,), (1,)), ((), ())),
            preferred_element_type=jnp.float32,
        )

    low_here = pl.multiple_of(core * 128, 128)
    core_copy = remote(half_ref.at[0], half_ref.at[1], core_sem.at[0], core_sem.at[1], sibling)
    half_ref[0] = gram_rows(pl.multiple_of((1 - core) * 128, 128))
    core_copy.start()
    half_ref[2] = gram_rows(low_here)
    core_copy.wait_recv()
    half_ref[2] = half_ref[2] + half_ref[1]

    def rows_of(index):
        return pl.ds(pl.multiple_of(index * 8, 8), 8)

    for other, device in chips:
        remote(
            half_ref.at[2, rows_of(other)], first.at[chip], sem1.at[0], sem1.at[1], device
        ).start()
    first[chip] = half_ref[2, rows_of(chip), :]
    chip_bytes = first.at[pl.ds(0, CHIPS - 1)]
    remote(chip_bytes, chip_bytes, sem1.at[0], sem1.at[1], sibling).wait_recv()
    own = jnp.sum(first[...], axis=0)
    mine[...] = own
    for hop in (1, 7, 2, 6, 3, 5, 4):
        device = (zs[hop] * NY + y, par)
        remote(mine, second.at[z], sem2.at[0], sem2.at[1], device).start()
    second[z] = own
    column_bytes = second.at[pl.ds(0, NZ - 1)]
    remote(column_bytes, column_bytes, sem2.at[0], sem2.at[1], sibling).wait_recv()
    block = pl.ds(pl.multiple_of(low_here + chip * 8, 8), 8)
    gram_ref[block, :] = jnp.sum(second[...], axis=0)
    for _, device in chips:
        remote(gram_ref.at[block], gram_ref.at[block], sem3.at[0], sem3.at[1], device).start()
    gram_bytes = gram_ref.at[pl.ds(low_here, (CHIPS - 1) * 8)]
    remote(gram_bytes, gram_bytes, sem3.at[0], sem3.at[1], sibling).wait_recv()
    half_here = gram_ref.at[pl.ds(low_here, 128)]
    core_back = remote(half_here, half_here, sem4.at[0], sem4.at[1], sibling)
    core_back.start()

    sent = send_ref.at[pl.ds(0, NSAMP - 1)]
    remote(sent, sent, send_sem, recv_sem.at[0], sibling).wait_send()
    energy_bytes = energies_ref.at[pl.ds(0, NSAMP - 1)]
    remote(energy_bytes, energy_bytes, esem.at[0], esem.at[1], sibling).wait()
    core_copy.wait_send()
    remote(chip_bytes, chip_bytes, sem1.at[0], sem1.at[1], sibling).wait_send()
    remote(column_bytes, column_bytes, sem2.at[0], sem2.at[1], sibling).wait_send()
    remote(gram_bytes, gram_bytes, sem3.at[0], sem3.at[1], sibling).wait_send()
    core_back.wait()
    cent_copy.wait()


def main_call(activations, cotangents, spin_bits, off_row):
    whole = pl.BlockSpec(memory_space=VMEM)
    anywhere = pl.BlockSpec(memory_space=pl.ANY)
    dma = pltpu.SemaphoreType.DMA
    return pl.pallas_call(
        main_kernel,
        in_specs=[anywhere, anywhere, whole, whole],
        out_specs=[whole, anywhere, whole],
        out_shape=[
            jax.ShapeDtypeStruct((NS, NS), jnp.float32),
            jax.ShapeDtypeStruct((NS, WIDTH), jnp.bfloat16),
            jax.ShapeDtypeStruct((NSAMP, 1, 128), jnp.float32),
        ],
        scratch_shapes=[
            VMEM((LOCAL, LAYERS, CH, SITES), jnp.bfloat16),
            VMEM((LOCAL, LAYERS, CH, SITES), jnp.bfloat16),
            VMEM((PER_WAVE, KK * CH, LAYERS * PADK), jnp.bfloat16),
            VMEM((PER_WAVE, LAYERS * CH, LAYERS * PADK), jnp.bfloat16),
            VMEM((NSAMP, CHUNK, 128), jnp.float32),
            VMEM((NSAMP, CHUNK, 128), jnp.bfloat16),
            VMEM((NSAMP, CHUNK, 128), jnp.bfloat16),
            VMEM((NSAMP * CHUNK, 128), jnp.float32),
            VMEM((NS, WIDTH), jnp.bfloat16),
            VMEM((1, 128), jnp.float32),
            VMEM((3, 128, NS), jnp.float32),
            VMEM((CHIPS, 8, NS), jnp.float32),
            VMEM((8, NS), jnp.float32),
            VMEM((NZ, 8, NS), jnp.float32),
            dma((LOCAL,)),
            dma((LOCAL,)),
            dma,
            dma,
            dma((NY,)),
            dma((2,)),
            dma((2,)),
            dma((2,)),
            dma((2,)),
            dma((2,)),
            dma((2,)),
        ],
        compiler_params=pltpu.CompilerParams(
            collective_id=0, has_side_effects=True, vmem_limit_bytes=VMEM_LIMIT
        ),
    )(activations, cotangents, spin_bits, off_row)


BLOCK = 64
PANEL = 8


def reciprocal(value):
    guess = pl.reciprocal(value, approx=True)
    guess = guess * (2.0 - value * guess)
    return guess * (2.0 - value * guess)


def invert_block(diag):
    eye = lax.broadcasted_iota(jnp.int32, (BLOCK, BLOCK), 0) == lax.broadcasted_iota(
        jnp.int32, (BLOCK, BLOCK), 1
    )
    wide = jnp.concatenate([diag, jnp.where(eye, 1.0, 0.0)], axis=1)
    tiles = [wide[8 * q : 8 * q + 8] for q in range(BLOCK // 8)]
    sub = lax.broadcasted_iota(jnp.int32, (8, 128), 0)

    def lanes(tile, col):
        return jnp.broadcast_to(tile[:, col : col + 1], (8, 128))

    for panel in range(BLOCK // PANEL):
        tile = tiles[panel]
        base = panel * PANEL
        columns = [lanes(tile, base + j) for j in range(PANEL)]
        low = {
            (i, j): jnp.broadcast_to(columns[j][i : i + 1], (8, 128))
            for i in range(PANEL)
            for j in range(i + 1)
        }
        rows = [jnp.broadcast_to(tile[i : i + 1], (8, 128)) for i in range(PANEL)]
        ups, downs, starts = {}, {}, {}
        for p in range(0, PANEL, 2):
            q = p + 1
            a, b, c = low[p, p], low[q, p], low[q, q]
            recip = reciprocal(a * c - b * b)
            starts[p] = (c * rows[p] - b * rows[q]) * recip
            starts[q] = (a * rows[q] - b * rows[p]) * recip
            for i in range(q + 1, PANEL):
                up = c * low[i, p] - b * low[i, q]
                down = a * low[i, q] - b * low[i, p]
                for m in range(q + 1, i + 1):
                    low[i, m] = low[i, m] - (up * low[m, p] + down * low[m, q]) * recip
                ups[i, p], downs[i, p] = up * recip, down * recip
                rows[i] = rows[i] - (ups[i, p] * rows[p] + downs[i, p] * rows[q])
        solved = [None] * PANEL
        for p in reversed(range(0, PANEL, 2)):
            for total, factor, at in ((starts[p], ups, p), (starts[p + 1], downs, p + 1)):
                for i in reversed(range(p + 2, PANEL)):
                    total = total - factor[i, p] * solved[i]
                solved[at] = total
        for q in range(BLOCK // 8):
            if q == panel:
                continue
            old = tiles[q]
            terms = [lanes(old, base + i) * solved[i] for i in range(PANEL)]
            while len(terms) > 1:
                terms = [terms[a] + terms[a + 1] for a in range(0, len(terms), 2)]
            tiles[q] = old - terms[0]
        joined = solved[0]
        for i in range(1, PANEL):
            joined = jnp.where(sub == i, solved[i], joined)
        tiles[panel] = joined
    return jnp.concatenate(tiles, axis=0)[:, BLOCK:]


def solve_kernel(gram_ref, energies_ref, cent_hbm, update_ref, coeff_ref, work, held, cent_ref, cent_sem):
    cent_copy = pltpu.make_async_copy(cent_hbm, cent_ref, cent_sem)
    cent_copy.start()
    rows_iota = lax.broadcasted_iota(jnp.int32, (NS, NS), 0)
    cols_iota = lax.broadcasted_iota(jnp.int32, (NS, NS), 1)
    gram = gram_ref[...]
    diagonal = rows_iota == cols_iota
    trace = jnp.sum(jnp.where(diagonal, gram, 0.0), keepdims=True)
    level = 1.0 / (trace / NS)
    pieces = jnp.broadcast_to(energies_ref[...], (NSAMP, LOCAL, 128)).reshape(NS, 128)
    lane = lax.broadcasted_iota(jnp.int32, (NS, 128), 1)
    row = lax.broadcasted_iota(jnp.int32, (NS, 128), 0)
    energy = jnp.sum(jnp.where(lane == row % LOCAL, pieces, 0.0), axis=1, keepdims=True)
    mean = jnp.sum(energy, axis=0, keepdims=True) / NS
    residual = -(energy - mean) / math.sqrt(NS)
    work[:, :NS] = gram * level + jnp.where(diagonal, 0.01, 0.0)
    work[:, NS:] = jnp.broadcast_to(residual, (NS, 128))

    def step(index, carry):
        own = pl.ds(pl.multiple_of(index * BLOCK, BLOCK), BLOCK)
        panel = work[own, :]
        inverse = invert_block(panel[:, :BLOCK])
        solved = jnp.dot(inverse, panel, precision=HIGHEST, preferred_element_type=jnp.float32)
        held[...] = work[...] - jnp.dot(
            work[:, :BLOCK], solved, precision=HIGHEST, preferred_element_type=jnp.float32
        )
        held[own, :] = solved
        work[:, : NS - BLOCK] = held[:, BLOCK:NS]
        work[:, NS - BLOCK : NS] = held[:, :BLOCK]
        work[:, NS:] = held[:, NS:]
        return carry

    lax.fori_loop(0, NS // BLOCK, step, 0)
    coeff = work[:, NS:] * level
    held[:, NS:] = coeff
    own = held[pl.ds(pl.multiple_of(lax.axis_index("samp") * LOCAL, LOCAL), LOCAL), NS:]
    here = lax.broadcasted_iota(jnp.int32, (LOCAL, 128), 0) == lax.broadcasted_iota(
        jnp.int32, (LOCAL, 128), 1
    )
    coeff_ref[...] = jnp.sum(jnp.where(here, own, 0.0), axis=0, keepdims=True)[:, :LOCAL]
    both = jnp.concatenate([coeff, coeff], axis=1)
    weighted = jnp.sum(gram * both, axis=0, keepdims=True)
    across = jnp.sum(jnp.where(diagonal, both, 0.0), axis=0, keepdims=True)
    square_total = jnp.sum(weighted * across, keepdims=True)
    scale = lax.rsqrt(square_total / ENTRIES + 1e-06)
    first = lax.broadcasted_iota(jnp.int32, (1, 128), 1) < CH
    cent_copy.wait()
    for pair in range(ROWS // 2):
        parts = []
        for half in range(2):
            column = 128 * (2 * pair + half)
            cent = cent_ref[:, column : column + 128].astype(jnp.float32)
            parts.append(jnp.sum(cent * coeff, axis=0, keepdims=True) * scale)
        turned = [jnp.concatenate([item[:, CH:], item[:, :CH]], axis=1) for item in parts]
        update_ref[0:1, 128 * pair : 128 * pair + 128] = jnp.where(first, parts[0], turned[1])
        update_ref[1:2, 128 * pair : 128 * pair + 128] = jnp.where(first, turned[0], parts[1])


def solve_call(gram, energies, cent):
    whole = pl.BlockSpec(memory_space=VMEM)
    return pl.pallas_call(
        solve_kernel,
        in_specs=[whole, whole, pl.BlockSpec(memory_space=pl.ANY)],
        out_specs=[whole, whole],
        out_shape=[
            jax.ShapeDtypeStruct((LAYERS, ROWS * CH), jnp.float32),
            jax.ShapeDtypeStruct((1, LOCAL), jnp.float32),
        ],
        scratch_shapes=[
            VMEM((NS, NS + 128), jnp.float32),
            VMEM((NS, NS + 128), jnp.float32),
            VMEM((NS, WIDTH), jnp.bfloat16),
            pltpu.SemaphoreType.DMA,
        ],
        compiler_params=pltpu.CompilerParams(vmem_limit_bytes=VMEM_LIMIT),
    )(gram, energies, cent)


def on_device(activations, cotangents, spin_bits, offdiag_energy):
    gram, cent, energies = main_call(
        activations, cotangents, spin_bits, offdiag_energy.reshape(1, LOCAL)
    )
    update, coeff = solve_call(gram, energies, cent)
    return update, coeff.reshape(LOCAL)


def solution(mesh):
    in_specs = (
        P("samp", "par", None, None),
        P("samp", "par", None, None),
        P("samp", None),
        P("samp"),
    )
    out_specs = (P("par", "samp"), P("samp"))
    return jax.shard_map(
        on_device, mesh=mesh, in_specs=in_specs, out_specs=out_specs, check_vma=False
    )
```

time: 85.5 us -> 79.7 us (0.932)
  Pallas kernels: 83.4 us -> 78.9 us
  local copies, waits for them, and re-layouts: 1.31 us -> 0 us
    pallas_call x1, Pallas kernels: 65.1 us -> 62.4 us  [main_call(): pl.pallas_call(main_kernel, in_specs=[anywhere, anywhere, whole, whole],...]
    pallas_call x1, Pallas kernels: 18.2 us -> 16.5 us  [solve_call(): pl.pallas_call(solve_kernel, in_specs=[whole, whole, pl.BlockSpec(memory_...]
    slice x1 -> x0, local copies, waits for them, and re-layouts: 1.31 us -> none  [on_device(): return (update, coeff[:, 0])]
where the time goes in v2:
time: 79.7 us; the launch traced here: 79.5 us
  Pallas kernels  78.9 us (99%)
    pallas_call x1, Pallas kernels, main_call(): pl.pallas_call(main_kernel, in_specs=[anywhere, anywhere, whole, whole],...  62.4 us
    pallas_call x1, Pallas kernels, solve_call(): pl.pallas_call(solve_kernel, in_specs=[whole, whole, pl.BlockSpec(memory_...  16.5 us

profile of v2, /device:TPU:1, one launch (start us, length us, event | category | flops | bytes accessed | tf_op | source)
XLA Modules:
  0.0 79.5 jit_solution(12055578998768251893)
XLA Ops:
  0.6 62.4 %shard_map.59 = (f32[256,256]{1,0:T(8,128)}, bf16[256,2304]{1,0:T(8,128)(2,1)}, f32[32,1,128]{2,1,0:T(1,128)}) custom-call(bf16[8,2,64,576]{3,2,1,0:T(8,128)(2,1)} %act_hbm.1, bf16[8,2,64,576]{3,2,1,0:T(8,128)(2,1)} %cot_hbm.1, s32[8,576]{1,0:T(8,128)} %spin_ref.1, f32[1,8]{1,0:T(1,128)} %bitcast.2), custom_call_target="tpu_custom_call" | custom-call | tf_op jit(solution)/shard_map/pallas_call | solution.py:283
  63.1 16.5 %shard_map.60 = (f32[2,1152]{1,0:T(2,128)}, f32[1,8]{1,0:T(1,128)}) custom-call(f32[256,256]{1,0:T(8,128)} %get-tuple-element.7.gram_ref, f32[32,1,128]{2,1,0:T(1,128)} %get-tuple-element.8.energies_ref, bf16[256,2304]{1,0:T(8,128)(2,1)} %get-tuple-element.9.cent_hbm), custom_call_target="tpu_custom_call" | custom-call | tf_op jit(solution)/shard_map/pallas_call | solution.py:451

commit v3 on v2

--- a/solution.py
+++ b/solution.py
@@ -65,36 +65,38 @@
     return jnp.sum(jnp.where(here, wide, 0.0), axis=0, keepdims=True)
 
 
-WAVES = 4
-PER_WAVE = LOCAL // WAVES
-CHIPS = 16
-TAIL = 48
+WAVES = ((0, 0, 16), (2, 16, 32), (4, 48, 32), (7, 80, 64))
+MEMBERS = 32
 
 
 def main_kernel(
     act_hbm, cot_hbm, spin_ref, off_ref,
     gram_ref, cent_hbm, energies_ref,
     act_ref, cot_ref, lhs, rhs, wide_rows, send_ref, recv_ref, wide_recv, cent_ref,
-    energy_ref, half_ref, first, mine, second,
-    act_sem, cot_sem, cent_sem, send_sem, recv_sem, esem, core_sem, sem1, sem2, sem3, sem4,
+    energy_ref, relay_ref, part_ref, first, mine, second,
+    act_sem, cot_sem, cent_sem, send_sem, recv_sem, esem, relay_sem, sem1, sem2, sem3,
 ):
     samp = lax.axis_index("samp")
     par = lax.axis_index("par")
     z, y = samp // NY, samp % NY
     x, core = par // 2, par % 2
-    chip = y * 4 + x
     slot_here = y * NZ + z
     sibling = (samp, x * 2 + 1 - core)
     zs = [wrap(z + hop, NZ) for hop in range(NZ)]
     ys = [wrap(y + down, NY) for down in range(NY)]
     xs = [wrap(x + across, 4) for across in range(4)]
     partners = [(down, zs[hop] * NY + ys[down]) for down, hop in STEPS]
-    chips = [
-        (ys[down] * 4 + xs[across], (z * NY + ys[down], xs[across] * 2 + core))
+    far = {(down, hop): other for (down, other), (_, hop) in zip(partners, STEPS) if hop == 4}
+    sorted_partners = [
+        item for item, (_, hop) in sorted(zip(partners, STEPS), key=lambda pair: pair[1][1] != 4)
+    ]
+    block_here = y * NPAR + par
+    members = [
+        (ys[down] * NPAR + xs[across] * 2 + side, (z * NY + ys[down], xs[across] * 2 + side))
         for down in range(NY)
         for across in range(4)
-        if (down, across) != (0, 0)
-    ]
+        for side in (core, 1 - core)
+    ][1:]
 
     def act_copy(n):
         return pltpu.make_async_copy(act_hbm.at[n], act_ref.at[n], act_sem.at[n])
@@ -121,72 +123,89 @@
     for _, other in partners:
         pl.semaphore_signal(barrier, inc=1, device_id=(other, par), device_id_type=MESH)
         greeted += 1
-    for down in range(NY):
-        for across in range(1, 4):
-            device = (z * NY + ys[down], xs[across] * 2 + core)
+    for number, (_, device) in enumerate(members, 1):
+        if number % 8:
             pl.semaphore_signal(barrier, inc=1, device_id=device, device_id_type=MESH)
             greeted += 1
-    pl.semaphore_signal(barrier, inc=1, device_id=sibling, device_id_type=MESH)
-    greeted += 1
 
     rhs[...] = jnp.zeros_like(rhs)
     for layer in range(LAYERS):
         edge = layer * PADK + SITES - CH
-        lhs[:, :, edge : edge + 128] = jnp.zeros((PER_WAVE, KK * CH, 128), jnp.bfloat16)
-
-    def compute(wave):
-        for slot in range(PER_WAVE):
-            sample = wave * PER_WAVE + slot
-            act_copy(sample).wait()
-            cot_copy(sample).wait()
-            for layer in range(LAYERS):
-                base = layer * PADK
-                act = act_ref[sample, layer]
-                rhs[slot, layer * CH : (layer + 1) * CH, base : base + SITES] = cot_ref[sample, layer]
-                for col_step in (-1, 0, 1):
-                    moved = column_shift(act, col_step)
-                    for row_step in (-1, 0, 1):
-                        tap = 3 * (row_step + 1) + col_step + 1
-                        lhs[slot, tap * CH : (tap + 1) * CH, base : base + SITES] = rolled(
-                            moved, LAT * row_step
-                        )
-            out = lax.dot_general(
-                lhs[slot], rhs[slot], (((1,), (1,)), ((), ())), preferred_element_type=jnp.float32
-            )
-            for dest in range(NSAMP):
-                wide_rows[dest, pl.ds(sample * ROWS, ROWS), :] = out[dest * ROWS : (dest + 1) * ROWS]
-
-    def send_wave(low, rows):
-        for down, other in partners:
+        lhs[:, :, edge : edge + 128] = jnp.zeros((2, KK * CH, 128), jnp.bfloat16)
+
+    def compute(sample):
+        slot = sample % 2
+        act_copy(sample).wait()
+        cot_copy(sample).wait()
+        for layer in range(LAYERS):
+            base = layer * PADK
+            act = act_ref[sample, layer]
+            rhs[slot, layer * CH : (layer + 1) * CH, base : base + SITES] = cot_ref[sample, layer]
+            for col_step in (-1, 0, 1):
+                moved = column_shift(act, col_step)
+                for row_step in (-1, 0, 1):
+                    tap = 3 * (row_step + 1) + col_step + 1
+                    lhs[slot, tap * CH : (tap + 1) * CH, base : base + SITES] = rolled(
+                        moved, LAT * row_step
+                    )
+        out = lax.dot_general(
+            lhs[slot], rhs[slot], (((1,), (1,)), ((), ())), preferred_element_type=jnp.float32
+        )
+        for dest in range(NSAMP):
+            wide_rows[dest, pl.ds(sample * ROWS, ROWS), :] = out[dest * ROWS : (dest + 1) * ROWS]
+
+    def send_wave(low, rows, wave):
+        for down, other in sorted_partners:
             send_ref[other, pl.ds(low, rows), :] = wide_rows[other, pl.ds(low, rows), :].astype(
                 jnp.bfloat16
             )
+            source = send_ref.at[other, pl.ds(low, rows)]
+            if (down, 4) in far and far[down, 4] is other:
+                via = zs[2] if down < 2 else zs[6]
+                remote(
+                    source,
+                    relay_ref.at[down, pl.ds(low, rows)],
+                    send_sem,
+                    relay_sem.at[wave],
+                    (via * NY + y, par),
+                ).start()
+            else:
+                remote(
+                    source,
+                    recv_ref.at[slot_here, pl.ds(low, rows)],
+                    send_sem,
+                    recv_sem.at[down],
+                    (other, par),
+                ).start()
+
+    def pass_on(low, rows, wave):
+        landed = relay_ref.at[:, pl.ds(low, rows)]
+        remote(landed, landed, send_sem, relay_sem.at[wave], sibling).wait_recv()
+        for down in range(NY):
+            origin, goal = (zs[6], zs[2]) if down < 2 else (zs[2], zs[6])
             remote(
-                send_ref.at[other, pl.ds(low, rows)],
-                recv_ref.at[slot_here, pl.ds(low, rows)],
+                relay_ref.at[down, pl.ds(low, rows)],
+                recv_ref.at[y * NZ + origin, pl.ds(low, rows)],
                 send_sem,
                 recv_sem.at[down],
-                (other, par),
+                (goal * NY + ys[down], par),
             ).start()
 
-    compute(0)
     pl.semaphore_wait(barrier, greeted)
-    send_wave(0, 32)
-
-    def later(wave, carry):
-        compute(wave)
-
-        @pl.when(wave < WAVES - 1)
-        def _():
-            send_wave(pl.multiple_of(wave * 32, 32), 32)
-
-        @pl.when(wave == WAVES - 1)
-        def _():
-            send_wave(96, TAIL)
+
+    def one_sample(sample, carry):
+        compute(sample)
+        for wave, (last, low, rows) in enumerate(WAVES):
+
+            @pl.when(sample == last)
+            def _(wave=wave, low=low, rows=rows):
+                if wave > 0:
+                    pass_on(*WAVES[wave - 1][1:], wave - 1)
+                send_wave(low, rows, wave)
 
         return carry
 
-    lax.fori_loop(1, WAVES, later, 0)
+    lax.fori_loop(0, LOCAL, one_sample, 0)
 
     flat = diagonal_energy(spin_ref[...])
     energy_ref[...] = jnp.zeros_like(energy_ref)
@@ -195,6 +214,7 @@
         remote(energy_ref, energies_ref.at[samp], esem.at[0], esem.at[1], (other, par)).start()
     energies_ref[samp] = energy_ref[...]
     recv_ref[slot_here] = wide_rows[samp].astype(jnp.bfloat16)
+    pass_on(*WAVES[-1][1:], len(WAVES) - 1)
 
     group = NZ * CHUNK
     for down in range(NY):
@@ -222,58 +242,43 @@
     cent_copy = pltpu.make_async_copy(cent_ref, cent_hbm, cent_sem)
     cent_copy.start()
 
-    def gram_rows(low):
-        return lax.dot_general(
-            cent_ref[pl.ds(low, 128), :], cent_ref[...], (((1,), (1,)), ((), ())),
-            preferred_element_type=jnp.float32,
-        )
-
-    low_here = pl.multiple_of(core * 128, 128)
-    core_copy = remote(half_ref.at[0], half_ref.at[1], core_sem.at[0], core_sem.at[1], sibling)
-    half_ref[0] = gram_rows(pl.multiple_of((1 - core) * 128, 128))
-    core_copy.start()
-    half_ref[2] = gram_rows(low_here)
-    core_copy.wait_recv()
-    half_ref[2] = half_ref[2] + half_ref[1]
+    part_ref[...] = lax.dot_general(
+        cent_ref[...], cent_ref[...], (((1,), (1,)), ((), ())), preferred_element_type=jnp.float32
+    )
 
     def rows_of(index):
         return pl.ds(pl.multiple_of(index * 8, 8), 8)
 
-    for other, device in chips:
+    for other, device in members:
         remote(
-            half_ref.at[2, rows_of(other)], first.at[chip], sem1.at[0], sem1.at[1], device
+            part_ref.at[rows_of(other)], first.at[block_here], sem1.at[0], sem1.at[1], device
         ).start()
-    first[chip] = half_ref[2, rows_of(chip), :]
-    chip_bytes = first.at[pl.ds(0, CHIPS - 1)]
-    remote(chip_bytes, chip_bytes, sem1.at[0], sem1.at[1], sibling).wait_recv()
+    first[block_here] = part_ref[rows_of(block_here), :]
+    member_bytes = first.at[pl.ds(0, MEMBERS - 1)]
+    remote(member_bytes, member_bytes, sem1.at[0], sem1.at[1], sibling).wait_recv()
     own = jnp.sum(first[...], axis=0)
     mine[...] = own
-    for hop in (1, 7, 2, 6, 3, 5, 4):
+    for hop in (4, 3, 5, 2, 6, 1, 7):
         device = (zs[hop] * NY + y, par)
         remote(mine, second.at[z], sem2.at[0], sem2.at[1], device).start()
     second[z] = own
     column_bytes = second.at[pl.ds(0, NZ - 1)]
     remote(column_bytes, column_bytes, sem2.at[0], sem2.at[1], sibling).wait_recv()
-    block = pl.ds(pl.multiple_of(low_here + chip * 8, 8), 8)
+    block = rows_of(block_here)
     gram_ref[block, :] = jnp.sum(second[...], axis=0)
-    for _, device in chips:
+    for _, device in members:
         remote(gram_ref.at[block], gram_ref.at[block], sem3.at[0], sem3.at[1], device).start()
-    gram_bytes = gram_ref.at[pl.ds(low_here, (CHIPS - 1) * 8)]
-    remote(gram_bytes, gram_bytes, sem3.at[0], sem3.at[1], sibling).wait_recv()
-    half_here = gram_ref.at[pl.ds(low_here, 128)]
-    core_back = remote(half_here, half_here, sem4.at[0], sem4.at[1], sibling)
-    core_back.start()
 
     sent = send_ref.at[pl.ds(0, NSAMP - 1)]
     remote(sent, sent, send_sem, recv_sem.at[0], sibling).wait_send()
+    remote(relay_ref, relay_ref, send_sem, recv_sem.at[0], sibling).wait_send()
     energy_bytes = energies_ref.at[pl.ds(0, NSAMP - 1)]
     remote(energy_bytes, energy_bytes, esem.at[0], esem.at[1], sibling).wait()
-    core_copy.wait_send()
-    remote(chip_bytes, chip_bytes, sem1.at[0], sem1.at[1], sibling).wait_send()
+    remote(member_bytes, member_bytes, sem1.at[0], sem1.at[1], sibling).wait_send()
     remote(column_bytes, column_bytes, sem2.at[0], sem2.at[1], sibling).wait_send()
-    remote(gram_bytes, gram_bytes, sem3.at[0], sem3.at[1], sibling).wait_send()
-    core_back.wait()
     cent_copy.wait()
+    gram_bytes = gram_ref.at[pl.ds(0, (MEMBERS - 1) * 8)]
+    remote(gram_bytes, gram_bytes, sem3.at[0], sem3.at[1], sibling).wait()
 
 
 def main_call(activations, cotangents, spin_bits, off_row):
@@ -292,16 +297,17 @@
         scratch_shapes=[
             VMEM((LOCAL, LAYERS, CH, SITES), jnp.bfloat16),
             VMEM((LOCAL, LAYERS, CH, SITES), jnp.bfloat16),
-            VMEM((PER_WAVE, KK * CH, LAYERS * PADK), jnp.bfloat16),
-            VMEM((PER_WAVE, LAYERS * CH, LAYERS * PADK), jnp.bfloat16),
+            VMEM((2, KK * CH, LAYERS * PADK), jnp.bfloat16),
+            VMEM((2, LAYERS * CH, LAYERS * PADK), jnp.bfloat16),
             VMEM((NSAMP, CHUNK, 128), jnp.float32),
             VMEM((NSAMP, CHUNK, 128), jnp.bfloat16),
             VMEM((NSAMP, CHUNK, 128), jnp.bfloat16),
             VMEM((NSAMP * CHUNK, 128), jnp.float32),
             VMEM((NS, WIDTH), jnp.bfloat16),
             VMEM((1, 128), jnp.float32),
-            VMEM((3, 128, NS), jnp.float32),
-            VMEM((CHIPS, 8, NS), jnp.float32),
+            VMEM((NY, CHUNK, 128), jnp.bfloat16),
+            VMEM((NS, NS), jnp.float32),
+            VMEM((MEMBERS, 8, NS), jnp.float32),
             VMEM((8, NS), jnp.float32),
             VMEM((NZ, 8, NS), jnp.float32),
             dma((LOCAL,)),
@@ -310,8 +316,7 @@
             dma,
             dma((NY,)),
             dma((2,)),
-            dma((2,)),
-            dma((2,)),
+            dma((len(WAVES),)),
             dma((2,)),
             dma((2,)),
             dma((2,)),
@@ -332,27 +337,37 @@
     return guess * (2.0 - value * guess)
 
 
-def invert_block(diag):
+def forward_block(diag, tile_ref, column_ref):
     eye = lax.broadcasted_iota(jnp.int32, (BLOCK, BLOCK), 0) == lax.broadcasted_iota(
         jnp.int32, (BLOCK, BLOCK), 1
     )
     wide = jnp.concatenate([diag, jnp.where(eye, 1.0, 0.0)], axis=1)
-    tiles = [wide[8 * q : 8 * q + 8] for q in range(BLOCK // 8)]
+    count = BLOCK // PANEL
+    tiles = [wide[8 * q : 8 * q + 8] for q in range(count)]
     sub = lax.broadcasted_iota(jnp.int32, (8, 128), 0)
 
     def lanes(tile, col):
         return jnp.broadcast_to(tile[:, col : col + 1], (8, 128))
 
-    for panel in range(BLOCK // PANEL):
+    def joined(parts):
+        total = parts[0]
+        for i in range(1, PANEL):
+            total = jnp.where(sub == i, parts[i], total)
+        return total
+
+    reduced, scaled = [], []
+    for panel in range(count):
         tile = tiles[panel]
         base = panel * PANEL
-        columns = [lanes(tile, base + j) for j in range(PANEL)]
+        tile_ref[panel] = tile
+        for j in range(PANEL):
+            column_ref[panel, j] = lanes(tile, base + j)
         low = {
-            (i, j): jnp.broadcast_to(columns[j][i : i + 1], (8, 128))
+            (i, j): column_ref[panel, j, pl.ds(i, 8, stride=0), :]
             for i in range(PANEL)
             for j in range(i + 1)
         }
-        rows = [jnp.broadcast_to(tile[i : i + 1], (8, 128)) for i in range(PANEL)]
+        rows = [tile_ref[panel, pl.ds(i, 8, stride=0), :] for i in range(PANEL)]
         ups, downs, starts = {}, {}, {}
         for p in range(0, PANEL, 2):
             q = p + 1
@@ -367,28 +382,30 @@
                     low[i, m] = low[i, m] - (up * low[m, p] + down * low[m, q]) * recip
                 ups[i, p], downs[i, p] = up * recip, down * recip
                 rows[i] = rows[i] - (ups[i, p] * rows[p] + downs[i, p] * rows[q])
+        reduced.append(joined(rows))
+        scaled.append(joined([starts[i] for i in range(PANEL)]))
+        if panel == count - 1:
+            break
         solved = [None] * PANEL
         for p in reversed(range(0, PANEL, 2)):
             for total, factor, at in ((starts[p], ups, p), (starts[p + 1], downs, p + 1)):
                 for i in reversed(range(p + 2, PANEL)):
                     total = total - factor[i, p] * solved[i]
                 solved[at] = total
-        for q in range(BLOCK // 8):
-            if q == panel:
-                continue
+        for q in range(panel + 1, count):
             old = tiles[q]
             terms = [lanes(old, base + i) * solved[i] for i in range(PANEL)]
             while len(terms) > 1:
                 terms = [terms[a] + terms[a + 1] for a in range(0, len(terms), 2)]
             tiles[q] = old - terms[0]
-        joined = solved[0]
-        for i in range(1, PANEL):
-            joined = jnp.where(sub == i, solved[i], joined)
-        tiles[panel] = joined
-    return jnp.concatenate(tiles, axis=0)[:, BLOCK:]
-
-
-def solve_kernel(gram_ref, energies_ref, cent_hbm, update_ref, coeff_ref, work, held, cent_ref, cent_sem):
+    lower = jnp.concatenate(reduced, axis=0)[:, BLOCK:]
+    return lower, jnp.concatenate(scaled, axis=0)[:, BLOCK:]
+
+
+def solve_kernel(
+    gram_ref, energies_ref, cent_hbm, update_ref, coeff_ref,
+    work, held, cent_ref, cent_sem, tile_ref, column_ref,
+):
     cent_copy = pltpu.make_async_copy(cent_hbm, cent_ref, cent_sem)
     cent_copy.start()
     rows_iota = lax.broadcasted_iota(jnp.int32, (NS, NS), 0)
@@ -409,7 +426,10 @@
     def step(index, carry):
         own = pl.ds(pl.multiple_of(index * BLOCK, BLOCK), BLOCK)
         panel = work[own, :]
-        inverse = invert_block(panel[:, :BLOCK])
+        lower, scaled = forward_block(panel[:, :BLOCK], tile_ref, column_ref)
+        inverse = lax.dot_general(
+            lower, scaled, (((0,), (0,)), ((), ())), precision=HIGHEST, preferred_element_type=jnp.float32
+        )
         solved = jnp.dot(inverse, panel, precision=HIGHEST, preferred_element_type=jnp.float32)
         held[...] = work[...] - jnp.dot(
             work[:, :BLOCK], solved, precision=HIGHEST, preferred_element_type=jnp.float32
@@ -461,6 +481,8 @@
             VMEM((NS, NS + 128), jnp.float32),
             VMEM((NS, WIDTH), jnp.bfloat16),
             pltpu.SemaphoreType.DMA,
+            VMEM((BLOCK // PANEL, 8, 128), jnp.float32),
+            VMEM((BLOCK // PANEL, PANEL, 8, 128), jnp.float32),
         ],
         compiler_params=pltpu.CompilerParams(vmem_limit_bytes=VMEM_LIMIT),
     )(gram, energies, cent)

time: 79.7 us -> 76.9 us (0.965)
  Pallas kernels: 78.9 us -> 76.1 us
    pallas_call x1, Pallas kernels: 16.5 us -> 14.5 us  [solve_call(): pl.pallas_call(solve_kernel, in_specs=[whole, whole, pl.BlockSpec(memory_...]
    pallas_call x1, Pallas kernels: 62.4 us -> 61.6 us  [main_call(): pl.pallas_call(main_kernel, in_specs=[anywhere, anywhere, whole, whole],...]
where the time goes in v3:
time: 76.9 us; the launch traced here: 76.7 us
  Pallas kernels  76.1 us (99%)
    pallas_call x1, Pallas kernels, main_call(): pl.pallas_call(main_kernel, in_specs=[anywhere, anywhere, whole, whole],...  61.6 us
    pallas_call x1, Pallas kernels, solve_call(): pl.pallas_call(solve_kernel, in_specs=[whole, whole, pl.BlockSpec(memory_...  14.5 us

profile of v3, /device:TPU:1, one launch (start us, length us, event | category | flops | bytes accessed | tf_op | source)
XLA Modules:
  0.0 76.7 jit_solution(12477751202880170143)
XLA Ops:
  0.6 61.6 %shard_map.59 = (f32[256,256]{1,0:T(8,128)}, bf16[256,2304]{1,0:T(8,128)(2,1)}, f32[32,1,128]{2,1,0:T(1,128)}) custom-call(bf16[8,2,64,576]{3,2,1,0:T(8,128)(2,1)} %act_hbm.1, bf16[8,2,64,576]{3,2,1,0:T(8,128)(2,1)} %cot_hbm.1, s32[8,576]{1,0:T(8,128)} %spin_ref.1, f32[1,8]{1,0:T(1,128)} %bitcast.2), custom_call_target="tpu_custom_call" | custom-call | tf_op jit(solution)/shard_map/pallas_call | solution.py:288
  62.2 14.5 %shard_map.60 = (f32[2,1152]{1,0:T(2,128)}, f32[1,8]{1,0:T(1,128)}) custom-call(f32[256,256]{1,0:T(8,128)} %get-tuple-element.7.gram_ref, f32[32,1,128]{2,1,0:T(1,128)} %get-tuple-element.8.energies_ref, bf16[256,2304]{1,0:T(8,128)(2,1)} %get-tuple-element.9.cent_hbm), custom_call_target="tpu_custom_call" | custom-call | tf_op jit(solution)/shard_map/pallas_call | solution.py:471

commit v4 on v3

--- a/solution.py
+++ b/solution.py
@@ -65,14 +65,14 @@
     return jnp.sum(jnp.where(here, wide, 0.0), axis=0, keepdims=True)
 
 
-WAVES = ((0, 0, 16), (2, 16, 32), (4, 48, 32), (7, 80, 64))
+RHS_ROWS = ((0, 1, 2), (1, 0, 3))
 MEMBERS = 32
 
 
 def main_kernel(
     act_hbm, cot_hbm, spin_ref, off_ref,
     gram_ref, cent_hbm, energies_ref,
-    act_ref, cot_ref, lhs, rhs, wide_rows, send_ref, recv_ref, wide_recv, cent_ref,
+    act_ref, cot_ref, lhs, rhs, wide_rows, send_ref, recv_ref, cent_ref,
     energy_ref, relay_ref, part_ref, first, mine, second,
     act_sem, cot_sem, cent_sem, send_sem, recv_sem, esem, relay_sem, sem1, sem2, sem3,
 ):
@@ -86,7 +86,7 @@
     ys = [wrap(y + down, NY) for down in range(NY)]
     xs = [wrap(x + across, 4) for across in range(4)]
     partners = [(down, zs[hop] * NY + ys[down]) for down, hop in STEPS]
-    far = {(down, hop): other for (down, other), (_, hop) in zip(partners, STEPS) if hop == 4}
+    far = {down: other for (down, other), (_, hop) in zip(partners, STEPS) if hop == 4}
     sorted_partners = [
         item for item, (_, hop) in sorted(zip(partners, STEPS), key=lambda pair: pair[1][1] != 4)
     ]
@@ -128,84 +128,58 @@
             pl.semaphore_signal(barrier, inc=1, device_id=device, device_id_type=MESH)
             greeted += 1
 
-    rhs[...] = jnp.zeros_like(rhs)
-    for layer in range(LAYERS):
-        edge = layer * PADK + SITES - CH
-        lhs[:, :, edge : edge + 128] = jnp.zeros((2, KK * CH, 128), jnp.bfloat16)
-
-    def compute(sample):
-        slot = sample % 2
+    first_half = lax.broadcasted_iota(jnp.int32, (3 * CH, 128), 1) < CH
+    lhs[:, :, :, PADK - 128 :] = jnp.zeros((2, LAYERS, 3 * CH, 128), jnp.bfloat16)
+    rhs[:, :, :, PADK - 128 :] = jnp.zeros((2, LAYERS, 4 * CH, 128), jnp.bfloat16)
+    rhs[:, 1, 2 * CH : 3 * CH, :] = jnp.zeros((2, CH, PADK), jnp.bfloat16)
+
+    def product(slot, layer, width):
+        return lax.dot_general(
+            lhs[slot, layer], rhs[slot, layer, :width], (((1,), (1,)), ((), ())),
+            preferred_element_type=jnp.float32,
+        )
+
+    def compute(sample, slot):
         act_copy(sample).wait()
         cot_copy(sample).wait()
         for layer in range(LAYERS):
-            base = layer * PADK
             act = act_ref[sample, layer]
-            rhs[slot, layer * CH : (layer + 1) * CH, base : base + SITES] = cot_ref[sample, layer]
-            for col_step in (-1, 0, 1):
-                moved = column_shift(act, col_step)
-                for row_step in (-1, 0, 1):
-                    tap = 3 * (row_step + 1) + col_step + 1
-                    lhs[slot, tap * CH : (tap + 1) * CH, base : base + SITES] = rolled(
-                        moved, LAT * row_step
-                    )
-        out = lax.dot_general(
-            lhs[slot], rhs[slot], (((1,), (1,)), ((), ())), preferred_element_type=jnp.float32
+            cot = cot_ref[sample, layer]
+            for step in (-1, 0, 1):
+                low = (step + 1) * CH
+                lhs[slot, layer, low : low + CH, :SITES] = column_shift(act, step)
+                low = RHS_ROWS[layer][step + 1] * CH
+                rhs[slot, layer, low : low + CH, :SITES] = rolled(cot, -LAT * step)
+        one = product(slot, 0, 3 * CH)
+        two = product(slot, 1, 4 * CH)
+        blocks = (
+            jnp.where(first_half, one[:, :128], two[:, :128]),
+            jnp.where(first_half, two[:, :128], one[:, :128]),
+            jnp.where(first_half, jnp.concatenate([one[:, 128:], one[:, 128:]], axis=1), two[:, 128:]),
         )
-        for dest in range(NSAMP):
-            wide_rows[dest, pl.ds(sample * ROWS, ROWS), :] = out[dest * ROWS : (dest + 1) * ROWS]
-
-    def send_wave(low, rows, wave):
-        for down, other in sorted_partners:
-            send_ref[other, pl.ds(low, rows), :] = wide_rows[other, pl.ds(low, rows), :].astype(
-                jnp.bfloat16
-            )
-            source = send_ref.at[other, pl.ds(low, rows)]
-            if (down, 4) in far and far[down, 4] is other:
-                via = zs[2] if down < 2 else zs[6]
-                remote(
-                    source,
-                    relay_ref.at[down, pl.ds(low, rows)],
-                    send_sem,
-                    relay_sem.at[wave],
-                    (via * NY + y, par),
-                ).start()
-            else:
-                remote(
-                    source,
-                    recv_ref.at[slot_here, pl.ds(low, rows)],
-                    send_sem,
-                    recv_sem.at[down],
-                    (other, par),
-                ).start()
-
-    def pass_on(low, rows, wave):
-        landed = relay_ref.at[:, pl.ds(low, rows)]
-        remote(landed, landed, send_sem, relay_sem.at[wave], sibling).wait_recv()
-        for down in range(NY):
-            origin, goal = (zs[6], zs[2]) if down < 2 else (zs[2], zs[6])
-            remote(
-                relay_ref.at[down, pl.ds(low, rows)],
-                recv_ref.at[y * NZ + origin, pl.ds(low, rows)],
-                send_sem,
-                recv_sem.at[down],
-                (goal * NY + ys[down], par),
-            ).start()
+        for down in range(3):
+            wide_rows[pl.ds(down * 3 * CH * LOCAL + sample, 3 * CH, stride=LOCAL), :] = blocks[down]
+
+    def two_samples(pair, carry):
+        for slot in range(2):
+            compute(pair * 2 + slot, slot)
+        return carry
+
+    lax.fori_loop(0, LOCAL // 2, two_samples, 0)
+
+    def rounded(other):
+        start = pl.multiple_of(other * CHUNK, CHUNK)
+        return wide_rows[pl.ds(start, CHUNK), :].astype(jnp.bfloat16)
 
     pl.semaphore_wait(barrier, greeted)
-
-    def one_sample(sample, carry):
-        compute(sample)
-        for wave, (last, low, rows) in enumerate(WAVES):
-
-            @pl.when(sample == last)
-            def _(wave=wave, low=low, rows=rows):
-                if wave > 0:
-                    pass_on(*WAVES[wave - 1][1:], wave - 1)
-                send_wave(low, rows, wave)
-
-        return carry
-
-    lax.fori_loop(0, LOCAL, one_sample, 0)
+    for down, other in sorted_partners:
+        send_ref[other] = rounded(other)
+        if far[down] is other:
+            via = zs[2] if down < 2 else zs[6]
+            target, arrived, device = relay_ref.at[down], relay_sem, (via * NY + y, par)
+        else:
+            target, arrived, device = recv_ref.at[slot_here], recv_sem.at[down], (other, par)
+        remote(send_ref.at[other], target, send_sem, arrived, device).start()
 
     flat = diagonal_energy(spin_ref[...])
     energy_ref[...] = jnp.zeros_like(energy_ref)
@@ -213,32 +187,36 @@
     for _, other in partners:
         remote(energy_ref, energies_ref.at[samp], esem.at[0], esem.at[1], (other, par)).start()
     energies_ref[samp] = energy_ref[...]
-    recv_ref[slot_here] = wide_rows[samp].astype(jnp.bfloat16)
-    pass_on(*WAVES[-1][1:], len(WAVES) - 1)
-
-    group = NZ * CHUNK
+    recv_ref[slot_here] = rounded(samp)
+    remote(relay_ref, relay_ref, send_sem, relay_sem, sibling).wait_recv()
+    for down in range(NY):
+        origin, goal = (zs[6], zs[2]) if down < 2 else (zs[2], zs[6])
+        remote(
+            relay_ref.at[down],
+            recv_ref.at[y * NZ + origin],
+            send_sem,
+            recv_sem.at[down],
+            (goal * NY + ys[down], par),
+        ).start()
+
     for down in range(NY):
         low = wrap(y + NY - down, NY) * NZ
         taken = recv_ref.at[pl.ds(0, NZ - 1)] if down == 0 else recv_ref.at[pl.ds(low, NZ)]
         remote(taken, taken, send_sem, recv_sem.at[down], sibling).wait_recv()
-        start = pl.multiple_of(low * CHUNK, group)
-        wide_recv[pl.ds(start, group), :] = (
-            recv_ref[pl.ds(low, NZ)].astype(jnp.float32).reshape(group, 128)
-        )
-
-    def centre(row, carry):
-        part = jnp.stack(
+
+    for pair in range(ROWS // 2):
+        tile = jnp.stack(
             [
-                wide_recv[pl.ds(((src % NY) * NZ + src // NY) * CHUNK + row, LOCAL, stride=ROWS), :]
+                recv_ref[(src % NY) * NZ + src // NY, 16 * pair : 16 * pair + 16, :].astype(jnp.float32)
                 for src in range(NSAMP)
             ]
-        )
-        mean = jnp.sum(jnp.sum(part, axis=0), axis=0, keepdims=True) / NS
-        cent = ((part - mean) / math.sqrt(NS)).reshape(NS, 128)
-        cent_ref[:, pl.ds(pl.multiple_of(row * 128, 128), 128)] = cent.astype(jnp.bfloat16)
-        return carry
-
-    lax.fori_loop(0, ROWS, centre, 0)
+        ).reshape(NSAMP, 2, LOCAL, 128)
+        for half in range(2):
+            part = tile[:, half]
+            mean = jnp.sum(jnp.sum(part, axis=0), axis=0, keepdims=True) / NS
+            cent = ((part - mean) / math.sqrt(NS)).reshape(NS, 128)
+            column = 128 * (2 * pair + half)
+            cent_ref[:, column : column + 128] = cent.astype(jnp.bfloat16)
     cent_copy = pltpu.make_async_copy(cent_ref, cent_hbm, cent_sem)
     cent_copy.start()
 
@@ -297,12 +275,11 @@
         scratch_shapes=[
             VMEM((LOCAL, LAYERS, CH, SITES), jnp.bfloat16),
             VMEM((LOCAL, LAYERS, CH, SITES), jnp.bfloat16),
-            VMEM((2, KK * CH, LAYERS * PADK), jnp.bfloat16),
-            VMEM((2, LAYERS * CH, LAYERS * PADK), jnp.bfloat16),
-            VMEM((NSAMP, CHUNK, 128), jnp.float32),
+            VMEM((2, LAYERS, 3 * CH, PADK), jnp.bfloat16),
+            VMEM((2, LAYERS, 4 * CH, PADK), jnp.bfloat16),
+            VMEM((NSAMP * CHUNK, 128), jnp.float32),
             VMEM((NSAMP, CHUNK, 128), jnp.bfloat16),
             VMEM((NSAMP, CHUNK, 128), jnp.bfloat16),
-            VMEM((NSAMP * CHUNK, 128), jnp.float32),
             VMEM((NS, WIDTH), jnp.bfloat16),
             VMEM((1, 128), jnp.float32),
             VMEM((NY, CHUNK, 128), jnp.bfloat16),
@@ -316,7 +293,7 @@
             dma,
             dma((NY,)),
             dma((2,)),
-            dma((len(WAVES),)),
+            dma,
             dma((2,)),
             dma((2,)),
             dma((2,)),
@@ -329,12 +306,6 @@
 
 BLOCK = 64
 PANEL = 8
-
-
-def reciprocal(value):
-    guess = pl.reciprocal(value, approx=True)
-    guess = guess * (2.0 - value * guess)
-    return guess * (2.0 - value * guess)
 
 
 def forward_block(diag, tile_ref, column_ref):
@@ -372,7 +343,7 @@
         for p in range(0, PANEL, 2):
             q = p + 1
             a, b, c = low[p, p], low[q, p], low[q, q]
-            recip = reciprocal(a * c - b * b)
+            recip = pl.reciprocal(a * c - b * b, approx=True)
             starts[p] = (c * rows[p] - b * rows[q]) * recip
             starts[q] = (a * rows[q] - b * rows[p]) * recip
             for i in range(q + 1, PANEL):
@@ -462,6 +433,13 @@
             cent = cent_ref[:, column : column + 128].astype(jnp.float32)
             parts.append(jnp.sum(cent * coeff, axis=0, keepdims=True) * scale)
         turned = [jnp.concatenate([item[:, CH:], item[:, :CH]], axis=1) for item in parts]
+        for half in range(2):
+            at = lax.axis_index("samp") * ROWS + 2 * pair + half
+            swapped = jnp.logical_and(at >= 3 * CH, at < 6 * CH)
+            parts[half], turned[half] = (
+                jnp.where(swapped, turned[half], parts[half]),
+                jnp.where(swapped, parts[half], turned[half]),
+            )
         update_ref[0:1, 128 * pair : 128 * pair + 128] = jnp.where(first, parts[0], turned[1])
         update_ref[1:2, 128 * pair : 128 * pair + 128] = jnp.where(first, turned[0], parts[1])
 

time: 76.9 us -> 73.5 us (0.956)
  Pallas kernels: 76.1 us -> 72.6 us
    pallas_call x1, Pallas kernels: 61.6 us -> 59.6 us  [main_call(): pl.pallas_call(main_kernel, in_specs=[anywhere, anywhere, whole, whole],...]
    pallas_call x1, Pallas kernels: 14.5 us -> 13 us  [solve_call(): pl.pallas_call(solve_kernel, in_specs=[whole, whole, pl.BlockSpec(memory_...]
where the time goes in v4:
time: 73.5 us; the launch traced here: 73.3 us
  Pallas kernels  72.6 us (99%)
    pallas_call x1, Pallas kernels, main_call(): pl.pallas_call(main_kernel, in_specs=[anywhere, anywhere, whole, whole],...  59.6 us
    pallas_call x1, Pallas kernels, solve_call(): pl.pallas_call(solve_kernel, in_specs=[whole, whole, pl.BlockSpec(memory_...  13 us

profile of v4, /device:TPU:1, one launch (start us, length us, event | category | flops | bytes accessed | tf_op | source)
XLA Modules:
  0.0 73.3 jit_solution(10244714343168462398)
XLA Ops:
  0.6 59.6 %shard_map.59 = (f32[256,256]{1,0:T(8,128)}, bf16[256,2304]{1,0:T(8,128)(2,1)}, f32[32,1,128]{2,1,0:T(1,128)}) custom-call(bf16[8,2,64,576]{3,2,1,0:T(8,128)(2,1)} %act_hbm.1, bf16[8,2,64,576]{3,2,1,0:T(8,128)(2,1)} %cot_hbm.1, s32[8,576]{1,0:T(8,128)} %spin_ref.1, f32[1,8]{1,0:T(1,128)} %bitcast.2), custom_call_target="tpu_custom_call" | custom-call | tf_op jit(solution)/shard_map/pallas_call | solution.py:266
  60.3 13.0 %shard_map.60 = (f32[2,1152]{1,0:T(2,128)}, f32[1,8]{1,0:T(1,128)}) custom-call(f32[256,256]{1,0:T(8,128)} %get-tuple-element.7.gram_ref, f32[32,1,128]{2,1,0:T(1,128)} %get-tuple-element.8.energies_ref, bf16[256,2304]{1,0:T(8,128)(2,1)} %get-tuple-element.9.cent_hbm), custom_call_target="tpu_custom_call" | custom-call | tf_op jit(solution)/shard_map/pallas_call | solution.py:449

commit v5 on v4

--- a/solution.py
+++ b/solution.py
@@ -66,7 +66,7 @@
 
 
 RHS_ROWS = ((0, 1, 2), (1, 0, 3))
-MEMBERS = 32
+CHIPS = 16
 
 
 def main_kernel(
@@ -88,15 +88,24 @@
     partners = [(down, zs[hop] * NY + ys[down]) for down, hop in STEPS]
     far = {down: other for (down, other), (_, hop) in zip(partners, STEPS) if hop == 4}
     sorted_partners = [
-        item for item, (_, hop) in sorted(zip(partners, STEPS), key=lambda pair: pair[1][1] != 4)
+        item for item, (_, hop) in sorted(zip(partners, STEPS), key=lambda pair: -min(pair[1][1], NZ - pair[1][1]))
     ]
-    block_here = y * NPAR + par
-    members = [
-        (ys[down] * NPAR + xs[across] * 2 + side, (z * NY + ys[down], xs[across] * 2 + side))
+    chip = y * 4 + x
+    others = [
+        (ys[down] * 4 + xs[across], z * NY + ys[down], xs[across] * 2)
         for down in range(NY)
         for across in range(4)
-        for side in (core, 1 - core)
     ][1:]
+    around = [(other, (row, pair + side), side) for other, row, pair in others for side in range(2)]
+
+    def by_core(body):
+        @pl.when(core == 0)
+        def _():
+            body(0, 128)
+
+        @pl.when(core == 1)
+        def _():
+            body(1, NS)
 
     def act_copy(n):
         return pltpu.make_async_copy(act_hbm.at[n], act_ref.at[n], act_sem.at[n])
@@ -123,10 +132,13 @@
     for _, other in partners:
         pl.semaphore_signal(barrier, inc=1, device_id=(other, par), device_id_type=MESH)
         greeted += 1
-    for number, (_, device) in enumerate(members, 1):
-        if number % 8:
-            pl.semaphore_signal(barrier, inc=1, device_id=device, device_id_type=MESH)
-            greeted += 1
+    for down in range(NY):
+        for across in range(4):
+            for side in (core, 1 - core):
+                if across > 0 or side is not core:
+                    device = (z * NY + ys[down], xs[across] * 2 + side)
+                    pl.semaphore_signal(barrier, inc=1, device_id=device, device_id_type=MESH)
+                    greeted += 1
 
     first_half = lax.broadcasted_iota(jnp.int32, (3 * CH, 128), 1) < CH
     lhs[:, :, :, PADK - 128 :] = jnp.zeros((2, LAYERS, 3 * CH, 128), jnp.bfloat16)
@@ -224,39 +236,69 @@
         cent_ref[...], cent_ref[...], (((1,), (1,)), ((), ())), preferred_element_type=jnp.float32
     )
 
-    def rows_of(index):
-        return pl.ds(pl.multiple_of(index * 8, 8), 8)
-
-    for other, device in members:
+    def rows_of(side, index):
+        return pl.ds(pl.multiple_of(side * 128 + index * 8, 8), 8)
+
+    slot = core * CHIPS + chip
+    widths = (128, NS)
+
+    def send_first(other, device, side):
+        wide = pl.ds(0, widths[side])
         remote(
-            part_ref.at[rows_of(other)], first.at[block_here], sem1.at[0], sem1.at[1], device
+            part_ref.at[rows_of(side, other), wide],
+            first.at[slot, :, wide],
+            sem1.at[side],
+            sem1.at[2],
+            device,
         ).start()
-    first[block_here] = part_ref[rows_of(block_here), :]
-    member_bytes = first.at[pl.ds(0, MEMBERS - 1)]
-    remote(member_bytes, member_bytes, sem1.at[0], sem1.at[1], sibling).wait_recv()
-    own = jnp.sum(first[...], axis=0)
-    mine[...] = own
-    for hop in (4, 3, 5, 2, 6, 1, 7):
-        device = (zs[hop] * NY + y, par)
-        remote(mine, second.at[z], sem2.at[0], sem2.at[1], device).start()
-    second[z] = own
-    column_bytes = second.at[pl.ds(0, NZ - 1)]
-    remote(column_bytes, column_bytes, sem2.at[0], sem2.at[1], sibling).wait_recv()
-    block = rows_of(block_here)
-    gram_ref[block, :] = jnp.sum(second[...], axis=0)
-    for _, device in members:
-        remote(gram_ref.at[block], gram_ref.at[block], sem3.at[0], sem3.at[1], device).start()
+
+    for other, device, side in around:
+        send_first(other, device, side)
+    by_core(lambda side, width: send_first(chip, sibling, 1 - side))
+
+    def middle(side, width):
+        wide = pl.ds(0, width)
+        first[slot, :, wide] = part_ref[rows_of(side, chip), wide]
+        landed = first.at[pl.ds(0, 2 * CHIPS - 1), :, wide]
+        remote(landed, landed, sem1.at[0], sem1.at[2], sibling).wait_recv()
+        own = jnp.sum(first[:, :, wide], axis=0)
+        mine[:, wide] = own
+        for hop in (4, 3, 5, 2, 6, 1, 7):
+            device = (zs[hop] * NY + y, par)
+            remote(
+                mine.at[:, wide], second.at[z, :, wide], sem2.at[0], sem2.at[1], device
+            ).start()
+        second[z, :, wide] = own
+        landed = second.at[pl.ds(0, NZ - 1), :, wide]
+        remote(landed, landed, sem2.at[0], sem2.at[1], sibling).wait_recv()
+        block = rows_of(side, chip)
+        gram_ref[block, wide] = jnp.sum(second[:, :, wide], axis=0)
+        done = gram_ref.at[block, wide]
+        for _, device, _ in around:
+            remote(done, done, sem3.at[0], sem3.at[1 + side], device).start()
+        remote(done, done, sem3.at[0], sem3.at[1 + side], sibling).start()
+
+    by_core(middle)
 
     sent = send_ref.at[pl.ds(0, NSAMP - 1)]
     remote(sent, sent, send_sem, recv_sem.at[0], sibling).wait_send()
     remote(relay_ref, relay_ref, send_sem, recv_sem.at[0], sibling).wait_send()
     energy_bytes = energies_ref.at[pl.ds(0, NSAMP - 1)]
     remote(energy_bytes, energy_bytes, esem.at[0], esem.at[1], sibling).wait()
-    remote(member_bytes, member_bytes, sem1.at[0], sem1.at[1], sibling).wait_send()
-    remote(column_bytes, column_bytes, sem2.at[0], sem2.at[1], sibling).wait_send()
     cent_copy.wait()
-    gram_bytes = gram_ref.at[pl.ds(0, (MEMBERS - 1) * 8)]
-    remote(gram_bytes, gram_bytes, sem3.at[0], sem3.at[1], sibling).wait()
+
+    def finish(side, width):
+        wide = pl.ds(0, width)
+        for kind in range(2):
+            count = CHIPS - 1 if kind == side else CHIPS
+            bytes_ref = gram_ref.at[pl.ds(0, count * 8), pl.ds(0, widths[kind])]
+            remote(bytes_ref, bytes_ref, sem1.at[kind], sem3.at[1 + kind], sibling).wait()
+        landed = second.at[pl.ds(0, NZ - 1), :, wide]
+        remote(landed, landed, sem2.at[0], sem2.at[1], sibling).wait_send()
+        landed = first.at[pl.ds(0, 2 * CHIPS - 1), :, wide]
+        remote(landed, landed, sem3.at[0], sem1.at[2], sibling).wait_send()
+
+    by_core(finish)
 
 
 def main_call(activations, cotangents, spin_bits, off_row):
@@ -284,7 +326,7 @@
             VMEM((1, 128), jnp.float32),
             VMEM((NY, CHUNK, 128), jnp.bfloat16),
             VMEM((NS, NS), jnp.float32),
-            VMEM((MEMBERS, 8, NS), jnp.float32),
+            VMEM((2 * CHIPS, 8, NS), jnp.float32),
             VMEM((8, NS), jnp.float32),
             VMEM((NZ, 8, NS), jnp.float32),
             dma((LOCAL,)),
@@ -294,9 +336,9 @@
             dma((NY,)),
             dma((2,)),
             dma,
+            dma((3,)),
             dma((2,)),
-            dma((2,)),
-            dma((2,)),
+            dma((3,)),
         ],
         compiler_params=pltpu.CompilerParams(
             collective_id=0, has_side_effects=True, vmem_limit_bytes=VMEM_LIMIT
@@ -308,7 +350,7 @@
 PANEL = 8
 
 
-def forward_block(diag, tile_ref, column_ref):
+def forward_block(diag, tile_ref, column_ref, cross_ref):
     eye = lax.broadcasted_iota(jnp.int32, (BLOCK, BLOCK), 0) == lax.broadcasted_iota(
         jnp.int32, (BLOCK, BLOCK), 1
     )
@@ -326,36 +368,62 @@
             total = jnp.where(sub == i, parts[i], total)
         return total
 
+    def broadcast_row(ref, panel, j, i):
+        return ref[panel, j, pl.ds(i, 8, stride=0), :]
+
     reduced, scaled = [], []
+    columns = [lanes(tiles[0], j) for j in range(PANEL)]
     for panel in range(count):
-        tile = tiles[panel]
         base = panel * PANEL
-        tile_ref[panel] = tile
+        last = panel == count - 1
+        tile_ref[panel, 0] = tiles[panel]
         for j in range(PANEL):
-            column_ref[panel, j] = lanes(tile, base + j)
+            column_ref[panel, j] = columns[j]
         low = {
-            (i, j): column_ref[panel, j, pl.ds(i, 8, stride=0), :]
+            (i, j): broadcast_row(column_ref, panel, j, i)
             for i in range(PANEL)
             for j in range(i + 1)
         }
-        rows = [tile_ref[panel, pl.ds(i, 8, stride=0), :] for i in range(PANEL)]
-        ups, downs, starts = {}, {}, {}
+        rows = [broadcast_row(tile_ref, panel, 0, i) for i in range(PANEL)]
+        old_columns = {
+            q: [lanes(tiles[q], base + i) for i in range(PANEL)] for q in range(panel + 1, count)
+        }
+        if not last:
+            cross = list(old_columns[panel + 1])
+            columns = [lanes(tiles[panel + 1], base + PANEL + j) for j in range(PANEL)]
+        ups, downs, starts, cross_scaled = {}, {}, {}, {}
         for p in range(0, PANEL, 2):
             q = p + 1
             a, b, c = low[p, p], low[q, p], low[q, q]
             recip = pl.reciprocal(a * c - b * b, approx=True)
-            starts[p] = (c * rows[p] - b * rows[q]) * recip
-            starts[q] = (a * rows[q] - b * rows[p]) * recip
             for i in range(q + 1, PANEL):
                 up = c * low[i, p] - b * low[i, q]
                 down = a * low[i, q] - b * low[i, p]
                 for m in range(q + 1, i + 1):
                     low[i, m] = low[i, m] - (up * low[m, p] + down * low[m, q]) * recip
                 ups[i, p], downs[i, p] = up * recip, down * recip
+            if not last:
+                cross_scaled[p] = (c * cross[p] - b * cross[q]) * recip
+                cross_scaled[q] = (a * cross[q] - b * cross[p]) * recip
+                for i in range(q + 1, PANEL):
+                    cross[i] = cross[i] - (ups[i, p] * cross[p] + downs[i, p] * cross[q])
+            starts[p] = (c * rows[p] - b * rows[q]) * recip
+            starts[q] = (a * rows[q] - b * rows[p]) * recip
+            for i in range(q + 1, PANEL):
                 rows[i] = rows[i] - (ups[i, p] * rows[p] + downs[i, p] * rows[q])
+        if not last:
+            for i in range(PANEL):
+                cross_ref[panel, i] = cross[i]
+            for j in range(PANEL):
+                terms = [
+                    cross_scaled[i] * broadcast_row(cross_ref, panel, i, j) for i in range(PANEL)
+                ]
+                while len(terms) > 1:
+                    terms = [terms[a] + terms[a + 1] for a in range(0, len(terms), 2)]
+                columns[j] = columns[j] - terms[0]
         reduced.append(joined(rows))
         scaled.append(joined([starts[i] for i in range(PANEL)]))
-        if panel == count - 1:
+        if last:
             break
         solved = [None] * PANEL
         for p in reversed(range(0, PANEL, 2)):
@@ -364,24 +432,33 @@
                     total = total - factor[i, p] * solved[i]
                 solved[at] = total
         for q in range(panel + 1, count):
-            old = tiles[q]
-            terms = [lanes(old, base + i) * solved[i] for i in range(PANEL)]
+            terms = [old_columns[q][i] * solved[i] for i in range(PANEL)]
             while len(terms) > 1:
                 terms = [terms[a] + terms[a + 1] for a in range(0, len(terms), 2)]
-            tiles[q] = old - terms[0]
+            tiles[q] = tiles[q] - terms[0]
     lower = jnp.concatenate(reduced, axis=0)[:, BLOCK:]
     return lower, jnp.concatenate(scaled, axis=0)[:, BLOCK:]
 
 
+def product(one, two, first_dim, second_dim):
+    return lax.dot_general(
+        one, two, (((first_dim,), (second_dim,)), ((), ())),
+        precision=HIGHEST, preferred_element_type=jnp.float32,
+    )
+
+
 def solve_kernel(
     gram_ref, energies_ref, cent_hbm, update_ref, coeff_ref,
-    work, held, cent_ref, cent_sem, tile_ref, column_ref,
+    work, held, cent_ref, cent_sem, tile_ref, column_ref, cross_ref,
 ):
     cent_copy = pltpu.make_async_copy(cent_hbm, cent_ref, cent_sem)
     cent_copy.start()
     rows_iota = lax.broadcasted_iota(jnp.int32, (NS, NS), 0)
     cols_iota = lax.broadcasted_iota(jnp.int32, (NS, NS), 1)
-    gram = gram_ref[...]
+    below = gram_ref[128:, :128]
+    gram = jnp.concatenate(
+        [jnp.concatenate([gram_ref[:128, :128], below.T], axis=1), gram_ref[128:, :]], axis=0
+    )
     diagonal = rows_iota == cols_iota
     trace = jnp.sum(jnp.where(diagonal, gram, 0.0), keepdims=True)
     level = 1.0 / (trace / NS)
@@ -397,15 +474,11 @@
     def step(index, carry):
         own = pl.ds(pl.multiple_of(index * BLOCK, BLOCK), BLOCK)
         panel = work[own, :]
-        lower, scaled = forward_block(panel[:, :BLOCK], tile_ref, column_ref)
-        inverse = lax.dot_general(
-            lower, scaled, (((0,), (0,)), ((), ())), precision=HIGHEST, preferred_element_type=jnp.float32
-        )
-        solved = jnp.dot(inverse, panel, precision=HIGHEST, preferred_element_type=jnp.float32)
-        held[...] = work[...] - jnp.dot(
-            work[:, :BLOCK], solved, precision=HIGHEST, preferred_element_type=jnp.float32
-        )
-        held[own, :] = solved
+        lower, scaled = forward_block(panel[:, :BLOCK], tile_ref, column_ref, cross_ref)
+        middle = product(scaled, panel, 1, 0)
+        outer = product(work[:, :BLOCK], lower, 1, 1)
+        held[...] = work[...] - product(outer, middle, 1, 0)
+        held[own, :] = product(lower, middle, 0, 0)
         work[:, : NS - BLOCK] = held[:, BLOCK:NS]
         work[:, NS - BLOCK : NS] = held[:, :BLOCK]
         work[:, NS:] = held[:, NS:]
@@ -459,7 +532,8 @@
             VMEM((NS, NS + 128), jnp.float32),
             VMEM((NS, WIDTH), jnp.bfloat16),
             pltpu.SemaphoreType.DMA,
-            VMEM((BLOCK // PANEL, 8, 128), jnp.float32),
+            VMEM((BLOCK // PANEL, 1, 8, 128), jnp.float32),
+            VMEM((BLOCK // PANEL, PANEL, 8, 128), jnp.float32),
             VMEM((BLOCK // PANEL, PANEL, 8, 128), jnp.float32),
         ],
         compiler_params=pltpu.CompilerParams(vmem_limit_bytes=VMEM_LIMIT),

time: 73.5 us -> 71.1 us (0.967)
  Pallas kernels: 72.6 us -> 70.2 us
    pallas_call x1, Pallas kernels: 13 us -> 11.2 us  [solve_call(): pl.pallas_call(solve_kernel, in_specs=[whole, whole, pl.BlockSpec(memory_...]
where the time goes in v5:
time: 71.1 us; the launch traced here: 70.9 us
  Pallas kernels  70.2 us (99%)
    pallas_call x1, Pallas kernels, main_call(): pl.pallas_call(main_kernel, in_specs=[anywhere, anywhere, whole, whole],...  59 us
    pallas_call x1, Pallas kernels, solve_call(): pl.pallas_call(solve_kernel, in_specs=[whole, whole, pl.BlockSpec(memory_...  11.2 us

profile of v5, /device:TPU:1, one launch (start us, length us, event | category | flops | bytes accessed | tf_op | source)
XLA Modules:
  0.0 70.9 jit_solution(1777098120246534340)
XLA Ops:
  0.6 59.0 %shard_map.59 = (f32[256,256]{1,0:T(8,128)}, bf16[256,2304]{1,0:T(8,128)(2,1)}, f32[32,1,128]{2,1,0:T(1,128)}) custom-call(bf16[8,2,64,576]{3,2,1,0:T(8,128)(2,1)} %act_hbm.1, bf16[8,2,64,576]{3,2,1,0:T(8,128)(2,1)} %cot_hbm.1, s32[8,576]{1,0:T(8,128)} %spin_ref.1, f32[1,8]{1,0:T(1,128)} %bitcast.2), custom_call_target="tpu_custom_call" | custom-call | tf_op jit(solution)/shard_map/pallas_call | solution.py:308
  59.6 11.2 %shard_map.60 = (f32[2,1152]{1,0:T(2,128)}, f32[1,8]{1,0:T(1,128)}) custom-call(f32[256,256]{1,0:T(8,128)} %get-tuple-element.7.gram_ref, f32[32,1,128]{2,1,0:T(1,128)} %get-tuple-element.8.energies_ref, bf16[256,2304]{1,0:T(8,128)(2,1)} %get-tuple-element.9.cent_hbm), custom_call_target="tpu_custom_call" | custom-call | tf_op jit(solution)/shard_map/pallas_call | solution.py:522

commit v6 on v5

--- a/solution.py
+++ b/solution.py
@@ -36,12 +36,15 @@
     return jnp.concatenate([value[:, amount:], value[:, :amount]], axis=1)
 
 
-def column_shift(value, col_step):
+def edge_mask(shape, col_step):
+    column = lax.broadcasted_iota(jnp.int32, shape, 1) % LAT
+    return column == (LAT - 1 if col_step > 0 else 0)
+
+
+def column_shift(value, col_step, edge):
     if col_step == 0:
         return value
-    column = lax.broadcasted_iota(jnp.int32, value.shape, 1) % LAT
-    edge = LAT - 1 if col_step > 0 else 0
-    return jnp.where(column == edge, rolled(value, col_step - LAT * col_step), rolled(value, col_step))
+    return jnp.where(edge, rolled(value, col_step - LAT * col_step), rolled(value, col_step))
 
 
 def wrap(value, size):
@@ -53,8 +56,8 @@
 
 def diagonal_energy(spin_bits):
     spin = (2 * spin_bits - 1).astype(jnp.float32)
-    right = column_shift(spin, 1)
-    left = column_shift(spin, -1)
+    right = column_shift(spin, 1, edge_mask(spin.shape, 1))
+    left = column_shift(spin, -1, edge_mask(spin.shape, -1))
     pairs = spin * rolled(spin, LAT) + spin * right
     corners = spin * rolled(right, LAT) + spin * rolled(left, LAT)
     diag = 0.25 * jnp.sum(pairs + 0.5 * corners, axis=1, keepdims=True)
@@ -72,7 +75,7 @@
 def main_kernel(
     act_hbm, cot_hbm, spin_ref, off_ref,
     gram_ref, cent_hbm, energies_ref,
-    act_ref, cot_ref, lhs, rhs, wide_rows, send_ref, recv_ref, cent_ref,
+    act_ref, cot_ref, edges, lhs, rhs, wide_rows, send_ref, recv_ref, cent_ref,
     energy_ref, relay_ref, part_ref, first, mine, second,
     act_sem, cot_sem, cent_sem, send_sem, recv_sem, esem, relay_sem, sem1, sem2, sem3,
 ):
@@ -144,6 +147,9 @@
     lhs[:, :, :, PADK - 128 :] = jnp.zeros((2, LAYERS, 3 * CH, 128), jnp.bfloat16)
     rhs[:, :, :, PADK - 128 :] = jnp.zeros((2, LAYERS, 4 * CH, 128), jnp.bfloat16)
     rhs[:, 1, 2 * CH : 3 * CH, :] = jnp.zeros((2, CH, PADK), jnp.bfloat16)
+    for at, step in enumerate((-1, 1)):
+        strip = jnp.where(edge_mask((8, SITES), step), 1.0, 0.0)
+        edges[at] = jnp.concatenate([strip] * (CH // 8), axis=0).astype(jnp.bfloat16)
 
     def product(slot, layer, width):
         return lax.dot_general(
@@ -159,7 +165,8 @@
             cot = cot_ref[sample, layer]
             for step in (-1, 0, 1):
                 low = (step + 1) * CH
-                lhs[slot, layer, low : low + CH, :SITES] = column_shift(act, step)
+                edge = edges[max(step, 0)] > 0
+                lhs[slot, layer, low : low + CH, :SITES] = column_shift(act, step, edge)
                 low = RHS_ROWS[layer][step + 1] * CH
                 rhs[slot, layer, low : low + CH, :SITES] = rolled(cot, -LAT * step)
         one = product(slot, 0, 3 * CH)
@@ -223,18 +230,28 @@
                 for src in range(NSAMP)
             ]
         ).reshape(NSAMP, 2, LOCAL, 128)
+        halves = []
         for half in range(2):
             part = tile[:, half]
             mean = jnp.sum(jnp.sum(part, axis=0), axis=0, keepdims=True) / NS
             cent = ((part - mean) / math.sqrt(NS)).reshape(NS, 128)
-            column = 128 * (2 * pair + half)
-            cent_ref[:, column : column + 128] = cent.astype(jnp.bfloat16)
+            halves.append(cent.astype(jnp.bfloat16))
+        cent = jnp.concatenate(halves, axis=1)
+        cent_ref[:, 256 * pair : 256 * pair + 256] = cent
+        light = lax.dot_general(
+            cent[:128], cent[:128], (((1,), (1,)), ((), ())), preferred_element_type=jnp.float32
+        )
+        heavy = lax.dot_general(
+            cent[128:], cent, (((1,), (1,)), ((), ())), preferred_element_type=jnp.float32
+        )
+        if pair == 0:
+            part_ref[:128, :128] = light
+            part_ref[128:, :] = heavy
+        else:
+            part_ref[:128, :128] += light
+            part_ref[128:, :] += heavy
     cent_copy = pltpu.make_async_copy(cent_ref, cent_hbm, cent_sem)
     cent_copy.start()
-
-    part_ref[...] = lax.dot_general(
-        cent_ref[...], cent_ref[...], (((1,), (1,)), ((), ())), preferred_element_type=jnp.float32
-    )
 
     def rows_of(side, index):
         return pl.ds(pl.multiple_of(side * 128 + index * 8, 8), 8)
@@ -317,6 +334,7 @@
         scratch_shapes=[
             VMEM((LOCAL, LAYERS, CH, SITES), jnp.bfloat16),
             VMEM((LOCAL, LAYERS, CH, SITES), jnp.bfloat16),
+            VMEM((2, CH, SITES), jnp.bfloat16),
             VMEM((2, LAYERS, 3 * CH, PADK), jnp.bfloat16),
             VMEM((2, LAYERS, 4 * CH, PADK), jnp.bfloat16),
             VMEM((NSAMP * CHUNK, 128), jnp.float32),
@@ -465,29 +483,25 @@
     pieces = jnp.broadcast_to(energies_ref[...], (NSAMP, LOCAL, 128)).reshape(NS, 128)
     lane = lax.broadcasted_iota(jnp.int32, (NS, 128), 1)
     row = lax.broadcasted_iota(jnp.int32, (NS, 128), 0)
-    energy = jnp.sum(jnp.where(lane == row % LOCAL, pieces, 0.0), axis=1, keepdims=True)
+    energy = jnp.sum(jnp.where(lane == jnp.bitwise_and(row, LOCAL - 1), pieces, 0.0), axis=1, keepdims=True)
     mean = jnp.sum(energy, axis=0, keepdims=True) / NS
     residual = -(energy - mean) / math.sqrt(NS)
     work[:, :NS] = gram * level + jnp.where(diagonal, 0.01, 0.0)
     work[:, NS:] = jnp.broadcast_to(residual, (NS, 128))
 
-    def step(index, carry):
-        own = pl.ds(pl.multiple_of(index * BLOCK, BLOCK), BLOCK)
-        panel = work[own, :]
-        lower, scaled = forward_block(panel[:, :BLOCK], tile_ref, column_ref, cross_ref)
-        middle = product(scaled, panel, 1, 0)
-        outer = product(work[:, :BLOCK], lower, 1, 1)
-        held[...] = work[...] - product(outer, middle, 1, 0)
-        held[own, :] = product(lower, middle, 0, 0)
-        work[:, : NS - BLOCK] = held[:, BLOCK:NS]
-        work[:, NS - BLOCK : NS] = held[:, :BLOCK]
-        work[:, NS:] = held[:, NS:]
-        return carry
-
-    lax.fori_loop(0, NS // BLOCK, step, 0)
+    for index in range(NS // BLOCK):
+        low = index * BLOCK
+        own = slice(low, low + BLOCK)
+        rest = slice(128 * ((index + 1) // 2), NS + 128)
+        lower, scaled = forward_block(work[own, own], tile_ref, column_ref, cross_ref)
+        middle = product(scaled, work[own, rest], 1, 0)
+        outer = product(work[:, own], lower, 1, 1)
+        work[:, rest] = work[:, rest] - product(outer, middle, 1, 0)
+        work[own, rest] = product(lower, middle, 0, 0)
+
     coeff = work[:, NS:] * level
-    held[:, NS:] = coeff
-    own = held[pl.ds(pl.multiple_of(lax.axis_index("samp") * LOCAL, LOCAL), LOCAL), NS:]
+    held[...] = coeff
+    own = held[pl.ds(pl.multiple_of(lax.axis_index("samp") * LOCAL, LOCAL), LOCAL), :]
     here = lax.broadcasted_iota(jnp.int32, (LOCAL, 128), 0) == lax.broadcasted_iota(
         jnp.int32, (LOCAL, 128), 1
     )
@@ -529,7 +543,7 @@
         ],
         scratch_shapes=[
             VMEM((NS, NS + 128), jnp.float32),
-            VMEM((NS, NS + 128), jnp.float32),
+            VMEM((NS, 128), jnp.float32),
             VMEM((NS, WIDTH), jnp.bfloat16),
             pltpu.SemaphoreType.DMA,
             VMEM((BLOCK // PANEL, 1, 8, 128), jnp.float32),

time: 71.1 us -> 69.5 us (0.977)
  Pallas kernels: 70.2 us -> 68.7 us
    pallas_call x1, Pallas kernels: 11.2 us -> 9.61 us  [solve_call(): pl.pallas_call(solve_kernel, in_specs=[whole, whole, pl.BlockSpec(memory_...]
where the time goes in v6:
time: 69.5 us; the launch traced here: 69.3 us
  Pallas kernels  68.7 us (99%)
    pallas_call x1, Pallas kernels, main_call(): pl.pallas_call(main_kernel, in_specs=[anywhere, anywhere, whole, whole],...  59.1 us
    pallas_call x1, Pallas kernels, solve_call(): pl.pallas_call(solve_kernel, in_specs=[whole, whole, pl.BlockSpec(memory_...  9.61 us

profile of v6, /device:TPU:1, one launch (start us, length us, event | category | flops | bytes accessed | tf_op | source)
XLA Modules:
  0.0 69.3 jit_solution(658472793189440028)
XLA Ops:
  0.6 59.1 %shard_map.59 = (f32[256,256]{1,0:T(8,128)}, bf16[256,2304]{1,0:T(8,128)(2,1)}, f32[32,1,128]{2,1,0:T(1,128)}) custom-call(bf16[8,2,64,576]{3,2,1,0:T(8,128)(2,1)} %act_hbm.1, bf16[8,2,64,576]{3,2,1,0:T(8,128)(2,1)} %cot_hbm.1, s32[8,576]{1,0:T(8,128)} %spin_ref.1, f32[1,8]{1,0:T(1,128)} %bitcast.2), custom_call_target="tpu_custom_call" | custom-call | tf_op jit(solution)/shard_map/pallas_call | solution.py:325
  59.7 9.6 %shard_map.60 = (f32[2,1152]{1,0:T(2,128)}, f32[1,8]{1,0:T(1,128)}) custom-call(f32[256,256]{1,0:T(8,128)} %get-tuple-element.7.gram_ref, f32[32,1,128]{2,1,0:T(1,128)} %get-tuple-element.8.energies_ref, bf16[256,2304]{1,0:T(8,128)(2,1)} %get-tuple-element.9.cent_hbm), custom_call_target="tpu_custom_call" | custom-call | tf_op jit(solution)/shard_map/pallas_call | solution.py:536

commit v7 on v6

--- a/solution.py
+++ b/solution.py
@@ -68,6 +68,10 @@
     return jnp.sum(jnp.where(here, wide, 0.0), axis=0, keepdims=True)
 
 
+PLANE = sorted(
+    ((down, across) for down in range(NY) for across in range(4) if (down, across) != (0, 0)),
+    key=lambda step: -(min(step[0], NY - step[0]) + min(step[1], 4 - step[1])),
+)
 RHS_ROWS = ((0, 1, 2), (1, 0, 3))
 CHIPS = 16
 
@@ -76,8 +80,8 @@
     act_hbm, cot_hbm, spin_ref, off_ref,
     gram_ref, cent_hbm, energies_ref,
     act_ref, cot_ref, edges, lhs, rhs, wide_rows, send_ref, recv_ref, cent_ref,
-    energy_ref, relay_ref, part_ref, first, mine, second,
-    act_sem, cot_sem, cent_sem, send_sem, recv_sem, esem, relay_sem, sem1, sem2, sem3,
+    energy_ref, part_ref, first, mine, second,
+    act_sem, cot_sem, cent_sem, send_sem, recv_sem, esem, sem1, sem2, sem3,
 ):
     samp = lax.axis_index("samp")
     par = lax.axis_index("par")
@@ -89,16 +93,14 @@
     ys = [wrap(y + down, NY) for down in range(NY)]
     xs = [wrap(x + across, 4) for across in range(4)]
     partners = [(down, zs[hop] * NY + ys[down]) for down, hop in STEPS]
-    far = {down: other for (down, other), (_, hop) in zip(partners, STEPS) if hop == 4}
     sorted_partners = [
         item for item, (_, hop) in sorted(zip(partners, STEPS), key=lambda pair: -min(pair[1][1], NZ - pair[1][1]))
     ]
     chip = y * 4 + x
     others = [
         (ys[down] * 4 + xs[across], z * NY + ys[down], xs[across] * 2)
-        for down in range(NY)
-        for across in range(4)
-    ][1:]
+        for down, across in PLANE
+    ]
     around = [(other, (row, pair + side), side) for other, row, pair in others for side in range(2)]
 
     def by_core(body):
@@ -193,12 +195,9 @@
     pl.semaphore_wait(barrier, greeted)
     for down, other in sorted_partners:
         send_ref[other] = rounded(other)
-        if far[down] is other:
-            via = zs[2] if down < 2 else zs[6]
-            target, arrived, device = relay_ref.at[down], relay_sem, (via * NY + y, par)
-        else:
-            target, arrived, device = recv_ref.at[slot_here], recv_sem.at[down], (other, par)
-        remote(send_ref.at[other], target, send_sem, arrived, device).start()
+        remote(
+            send_ref.at[other], recv_ref.at[slot_here], send_sem, recv_sem.at[down], (other, par)
+        ).start()
 
     flat = diagonal_energy(spin_ref[...])
     energy_ref[...] = jnp.zeros_like(energy_ref)
@@ -207,17 +206,6 @@
         remote(energy_ref, energies_ref.at[samp], esem.at[0], esem.at[1], (other, par)).start()
     energies_ref[samp] = energy_ref[...]
     recv_ref[slot_here] = rounded(samp)
-    remote(relay_ref, relay_ref, send_sem, relay_sem, sibling).wait_recv()
-    for down in range(NY):
-        origin, goal = (zs[6], zs[2]) if down < 2 else (zs[2], zs[6])
-        remote(
-            relay_ref.at[down],
-            recv_ref.at[y * NZ + origin],
-            send_sem,
-            recv_sem.at[down],
-            (goal * NY + ys[down], par),
-        ).start()
-
     for down in range(NY):
         low = wrap(y + NY - down, NY) * NZ
         taken = recv_ref.at[pl.ds(0, NZ - 1)] if down == 0 else recv_ref.at[pl.ds(low, NZ)]
@@ -299,7 +287,6 @@
 
     sent = send_ref.at[pl.ds(0, NSAMP - 1)]
     remote(sent, sent, send_sem, recv_sem.at[0], sibling).wait_send()
-    remote(relay_ref, relay_ref, send_sem, recv_sem.at[0], sibling).wait_send()
     energy_bytes = energies_ref.at[pl.ds(0, NSAMP - 1)]
     remote(energy_bytes, energy_bytes, esem.at[0], esem.at[1], sibling).wait()
     cent_copy.wait()
@@ -342,7 +329,6 @@
             VMEM((NSAMP, CHUNK, 128), jnp.bfloat16),
             VMEM((NS, WIDTH), jnp.bfloat16),
             VMEM((1, 128), jnp.float32),
-            VMEM((NY, CHUNK, 128), jnp.bfloat16),
             VMEM((NS, NS), jnp.float32),
             VMEM((2 * CHIPS, 8, NS), jnp.float32),
             VMEM((8, NS), jnp.float32),
@@ -353,7 +339,6 @@
             dma,
             dma((NY,)),
             dma((2,)),
-            dma,
             dma((3,)),
             dma((2,)),
             dma((3,)),

time: 69.5 us -> 68.8 us (0.990)
  Pallas kernels: 68.7 us -> 68 us
    pallas_call x1, Pallas kernels: 59.1 us -> 58.4 us  [main_call(): pl.pallas_call(main_kernel, in_specs=[anywhere, anywhere, whole, whole],...]
where the time goes in v7:
time: 68.8 us; the launch traced here: 68.6 us
  Pallas kernels  68 us (99%)
    pallas_call x1, Pallas kernels, main_call(): pl.pallas_call(main_kernel, in_specs=[anywhere, anywhere, whole, whole],...  58.4 us
    pallas_call x1, Pallas kernels, solve_call(): pl.pallas_call(solve_kernel, in_specs=[whole, whole, pl.BlockSpec(memory_...  9.61 us

profile of v7, /device:TPU:1, one launch (start us, length us, event | category | flops | bytes accessed | tf_op | source)
XLA Modules:
  0.0 68.6 jit_solution(6415235528753193398)
XLA Ops:
  0.6 58.4 %shard_map.59 = (f32[256,256]{1,0:T(8,128)}, bf16[256,2304]{1,0:T(8,128)(2,1)}, f32[32,1,128]{2,1,0:T(1,128)}) custom-call(bf16[8,2,64,576]{3,2,1,0:T(8,128)(2,1)} %act_hbm.1, bf16[8,2,64,576]{3,2,1,0:T(8,128)(2,1)} %cot_hbm.1, s32[8,576]{1,0:T(8,128)} %spin_ref.1, f32[1,8]{1,0:T(1,128)} %bitcast.2), custom_call_target="tpu_custom_call" | custom-call | tf_op jit(solution)/shard_map/pallas_call | solution.py:312
  59.0 9.6 %shard_map.60 = (f32[2,1152]{1,0:T(2,128)}, f32[1,8]{1,0:T(1,128)}) custom-call(f32[256,256]{1,0:T(8,128)} %get-tuple-element.7.gram_ref, f32[32,1,128]{2,1,0:T(1,128)} %get-tuple-element.8.energies_ref, bf16[256,2304]{1,0:T(8,128)(2,1)} %get-tuple-element.9.cent_hbm), custom_call_target="tpu_custom_call" | custom-call | tf_op jit(solution)/shard_map/pallas_call | solution.py:521

commit v8 on v4

v8 whole, which is shorter than its diff:
```python
import math

import jax
import jax.numpy as jnp
from jax import lax
from jax.experimental import pallas as pl
from jax.experimental.pallas import tpu as pltpu
from jax.sharding import PartitionSpec as P

CH = 64
KK = 9
LAT = 24
SITES = LAT * LAT
NSAMP = 32
NPAR = 8
NZ = 8
NY = 4
LOCAL = 8
NS = NSAMP * LOCAL
ROWS = KK * CH // NSAMP
CHUNK = ROWS * LOCAL
WIDTH = ROWS * 128
PADK = 640
LAYERS = 2
ENTRIES = 16 * KK * CH * CH
MESH = pl.DeviceIdType.MESH
VMEM_LIMIT = 56 * 1024 * 1024
HIGHEST = lax.Precision.HIGHEST
VMEM = pltpu.VMEM


def rolled(value, amount):
    amount = amount % SITES
    if amount == 0:
        return value
    return jnp.concatenate([value[:, amount:], value[:, :amount]], axis=1)


def edge_mask(shape, col_step):
    column = lax.broadcasted_iota(jnp.int32, shape, 1) % LAT
    return column == (LAT - 1 if col_step > 0 else 0)


def column_shift(value, col_step, edge):
    if col_step == 0:
        return value
    return jnp.where(edge, rolled(value, col_step - LAT * col_step), rolled(value, col_step))


def wrap(value, size):
    return lax.select(value >= size, value - size, value)


STEPS = [(down, hop) for down in range(NY) for hop in (1, 7, 2, 6, 3, 5, 4, 0) if (down, hop) != (0, 0)]


def diagonal_energy(spin_bits):
    spin = (2 * spin_bits - 1).astype(jnp.float32)
    right = column_shift(spin, 1, edge_mask(spin.shape, 1))
    left = column_shift(spin, -1, edge_mask(spin.shape, -1))
    pairs = spin * rolled(spin, LAT) + spin * right
    corners = spin * rolled(right, LAT) + spin * rolled(left, LAT)
    diag = 0.25 * jnp.sum(pairs + 0.5 * corners, axis=1, keepdims=True)
    wide = jnp.broadcast_to(diag, (LOCAL, 128))
    here = lax.broadcasted_iota(jnp.int32, (LOCAL, 128), 0) == lax.broadcasted_iota(
        jnp.int32, (LOCAL, 128), 1
    )
    return jnp.sum(jnp.where(here, wide, 0.0), axis=0, keepdims=True)


PLANE = sorted(
    ((down, across) for down in range(NY) for across in range(4) if (down, across) != (0, 0)),
    key=lambda step: -(min(step[0], NY - step[0]) + min(step[1], 4 - step[1])),
)
RHS_ROWS = ((0, 1, 2), (1, 0, 3))
CHIPS = 16


BLOCK = 64
PANEL = 8


def forward_block(diag, tile_ref, column_ref, cross_ref):
    eye = lax.broadcasted_iota(jnp.int32, (BLOCK, BLOCK), 0) == lax.broadcasted_iota(
        jnp.int32, (BLOCK, BLOCK), 1
    )
    wide = jnp.concatenate([diag, jnp.where(eye, 1.0, 0.0)], axis=1)
    count = BLOCK // PANEL
    tiles = [wide[8 * q : 8 * q + 8] for q in range(count)]
    sub = lax.broadcasted_iota(jnp.int32, (8, 128), 0)

    def lanes(tile, col):
        return jnp.broadcast_to(tile[:, col : col + 1], (8, 128))

    def joined(parts):
        total = parts[0]
        for i in range(1, PANEL):
            total = jnp.where(sub == i, parts[i], total)
        return total

    def broadcast_row(ref, panel, j, i):
        return ref[panel, j, pl.ds(i, 8, stride=0), :]

    reduced, scaled = [], []
    columns = [lanes(tiles[0], j) for j in range(PANEL)]
    for panel in range(count):
        base = panel * PANEL
        last = panel == count - 1
        tile_ref[panel, 0] = tiles[panel]
        for j in range(PANEL):
            column_ref[panel, j] = columns[j]
        low = {
            (i, j): broadcast_row(column_ref, panel, j, i)
            for i in range(PANEL)
            for j in range(i + 1)
        }
        rows = [broadcast_row(tile_ref, panel, 0, i) for i in range(PANEL)]
        old_columns = {
            q: [lanes(tiles[q], base + i) for i in range(PANEL)] for q in range(panel + 1, count)
        }
        if not last:
            cross = list(old_columns[panel + 1])
            columns = [lanes(tiles[panel + 1], base + PANEL + j) for j in range(PANEL)]
        ups, downs, starts, cross_scaled = {}, {}, {}, {}
        for p in range(0, PANEL, 2):
            q = p + 1
            a, b, c = low[p, p], low[q, p], low[q, q]
            recip = pl.reciprocal(a * c - b * b, approx=True)
            for i in range(q + 1, PANEL):
                up = c * low[i, p] - b * low[i, q]
                down = a * low[i, q] - b * low[i, p]
                for m in range(q + 1, i + 1):
                    low[i, m] = low[i, m] - (up * low[m, p] + down * low[m, q]) * recip
                ups[i, p], downs[i, p] = up * recip, down * recip
            if not last:
                cross_scaled[p] = (c * cross[p] - b * cross[q]) * recip
                cross_scaled[q] = (a * cross[q] - b * cross[p]) * recip
                for i in range(q + 1, PANEL):
                    cross[i] = cross[i] - (ups[i, p] * cross[p] + downs[i, p] * cross[q])
            starts[p] = (c * rows[p] - b * rows[q]) * recip
            starts[q] = (a * rows[q] - b * rows[p]) * recip
            for i in range(q + 1, PANEL):
                rows[i] = rows[i] - (ups[i, p] * rows[p] + downs[i, p] * rows[q])
        if not last:
            for i in range(PANEL):
                cross_ref[panel, i] = cross[i]
            for j in range(PANEL):
                terms = [
                    cross_scaled[i] * broadcast_row(cross_ref, panel, i, j) for i in range(PANEL)
                ]
                while len(terms) > 1:
                    terms = [terms[a] + terms[a + 1] for a in range(0, len(terms), 2)]
                columns[j] = columns[j] - terms[0]
        reduced.append(joined(rows))
        scaled.append(joined([starts[i] for i in range(PANEL)]))
        if last:
            break
        solved = [None] * PANEL
        for p in reversed(range(0, PANEL, 2)):
            for total, factor, at in ((starts[p], ups, p), (starts[p + 1], downs, p + 1)):
                for i in reversed(range(p + 2, PANEL)):
                    total = total - factor[i, p] * solved[i]
                solved[at] = total
        for q in range(panel + 1, count):
            terms = [old_columns[q][i] * solved[i] for i in range(PANEL)]
            while len(terms) > 1:
                terms = [terms[a] + terms[a + 1] for a in range(0, len(terms), 2)]
            tiles[q] = tiles[q] - terms[0]
    lower = jnp.concatenate(reduced, axis=0)[:, BLOCK:]
    return lower, jnp.concatenate(scaled, axis=0)[:, BLOCK:]


def product(one, two, first_dim, second_dim):
    return lax.dot_general(
        one, two, (((first_dim,), (second_dim,)), ((), ())),
        precision=HIGHEST, preferred_element_type=jnp.float32,
    )


def main_kernel(
    act_hbm, cot_hbm, spin_ref, off_ref,
    update_ref, coeff_ref, scale_ref,
    act_ref, cot_ref, edges, lhs, rhs, wide_rows, send_ref, recv_ref, cent_ref,
    energy_ref, energies_ref, part_ref, first, mine, second, gram_ref,
    work, held, tile_ref, column_ref, cross_ref,
    act_sem, cot_sem, send_sem, recv_sem, esem, sem1, sem2, sem3,
):
    samp = lax.axis_index("samp")
    par = lax.axis_index("par")
    z, y = samp // NY, samp % NY
    x, core = par // 2, par % 2
    slot_here = y * NZ + z
    sibling = (samp, x * 2 + 1 - core)
    zs = [wrap(z + hop, NZ) for hop in range(NZ)]
    ys = [wrap(y + down, NY) for down in range(NY)]
    xs = [wrap(x + across, 4) for across in range(4)]
    partners = [(down, zs[hop] * NY + ys[down]) for down, hop in STEPS]
    sorted_partners = [
        item for item, (_, hop) in sorted(zip(partners, STEPS), key=lambda pair: -min(pair[1][1], NZ - pair[1][1]))
    ]
    chip = y * 4 + x
    others = [
        (ys[down] * 4 + xs[across], z * NY + ys[down], xs[across] * 2)
        for down, across in PLANE
    ]
    around = [(other, (row, pair + side), side) for other, row, pair in others for side in range(2)]

    def by_core(body):
        @pl.when(core == 0)
        def _():
            body(0, 128)

        @pl.when(core == 1)
        def _():
            body(1, NS)

    def act_copy(n):
        return pltpu.make_async_copy(act_hbm.at[n], act_ref.at[n], act_sem.at[n])

    def cot_copy(n):
        return pltpu.make_async_copy(cot_hbm.at[n], cot_ref.at[n], cot_sem.at[n])

    for n in range(LOCAL):
        act_copy(n).start()
        cot_copy(n).start()

    def remote(source, target, send, recv, device):
        return pltpu.make_async_remote_copy(
            src_ref=source,
            dst_ref=target,
            send_sem=send,
            recv_sem=recv,
            device_id=device,
            device_id_type=MESH,
        )

    barrier = pltpu.get_barrier_semaphore()
    greeted = 0
    for _, other in partners:
        pl.semaphore_signal(barrier, inc=1, device_id=(other, par), device_id_type=MESH)
        greeted += 1
    for down in range(NY):
        for across in range(4):
            for side in (core, 1 - core):
                if across > 0 or side is not core:
                    device = (z * NY + ys[down], xs[across] * 2 + side)
                    pl.semaphore_signal(barrier, inc=1, device_id=device, device_id_type=MESH)
                    greeted += 1

    first_half = lax.broadcasted_iota(jnp.int32, (3 * CH, 128), 1) < CH
    lhs[:, :, :, PADK - 128 :] = jnp.zeros((2, LAYERS, 3 * CH, 128), jnp.bfloat16)
    rhs[:, :, :, PADK - 128 :] = jnp.zeros((2, LAYERS, 4 * CH, 128), jnp.bfloat16)
    rhs[:, 1, 2 * CH : 3 * CH, :] = jnp.zeros((2, CH, PADK), jnp.bfloat16)
    for at, step in enumerate((-1, 1)):
        strip = jnp.where(edge_mask((8, SITES), step), 1.0, 0.0)
        edges[at] = jnp.concatenate([strip] * (CH // 8), axis=0).astype(jnp.bfloat16)

    def taps(slot, layer, width):
        return lax.dot_general(
            lhs[slot, layer], rhs[slot, layer, :width], (((1,), (1,)), ((), ())),
            preferred_element_type=jnp.float32,
        )

    def compute(sample, slot):
        act_copy(sample).wait()
        cot_copy(sample).wait()
        for layer in range(LAYERS):
            act = act_ref[sample, layer]
            cot = cot_ref[sample, layer]
            for step in (-1, 0, 1):
                low = (step + 1) * CH
                edge = edges[max(step, 0)] > 0
                lhs[slot, layer, low : low + CH, :SITES] = column_shift(act, step, edge)
                low = RHS_ROWS[layer][step + 1] * CH
                rhs[slot, layer, low : low + CH, :SITES] = rolled(cot, -LAT * step)
        one = taps(slot, 0, 3 * CH)
        two = taps(slot, 1, 4 * CH)
        blocks = (
            jnp.where(first_half, one[:, :128], two[:, :128]),
            jnp.where(first_half, two[:, :128], one[:, :128]),
            jnp.where(first_half, jnp.concatenate([one[:, 128:], one[:, 128:]], axis=1), two[:, 128:]),
        )
        for down in range(3):
            wide_rows[pl.ds(down * 3 * CH * LOCAL + sample, 3 * CH, stride=LOCAL), :] = blocks[down]

    def two_samples(pair, carry):
        for slot in range(2):
            compute(pair * 2 + slot, slot)
        return carry

    lax.fori_loop(0, LOCAL // 2, two_samples, 0)

    def rounded(other):
        start = pl.multiple_of(other * CHUNK, CHUNK)
        return wide_rows[pl.ds(start, CHUNK), :].astype(jnp.bfloat16)

    pl.semaphore_wait(barrier, greeted)
    for down, other in sorted_partners:
        send_ref[other] = rounded(other)
        remote(
            send_ref.at[other], recv_ref.at[slot_here], send_sem, recv_sem.at[down], (other, par)
        ).start()

    flat = diagonal_energy(spin_ref[...])
    energy_ref[...] = jnp.zeros_like(energy_ref)
    energy_ref[:, :LOCAL] = flat[:, :LOCAL] + off_ref[...]
    for _, other in partners:
        remote(energy_ref, energies_ref.at[samp], esem.at[0], esem.at[1], (other, par)).start()
    energies_ref[samp] = energy_ref[...]
    recv_ref[slot_here] = rounded(samp)
    for down in range(NY):
        low = wrap(y + NY - down, NY) * NZ
        taken = recv_ref.at[pl.ds(0, NZ - 1)] if down == 0 else recv_ref.at[pl.ds(low, NZ)]
        remote(taken, taken, send_sem, recv_sem.at[down], sibling).wait_recv()

    for pair in range(ROWS // 2):
        tile = jnp.stack(
            [
                recv_ref[(src % NY) * NZ + src // NY, 16 * pair : 16 * pair + 16, :].astype(jnp.float32)
                for src in range(NSAMP)
            ]
        ).reshape(NSAMP, 2, LOCAL, 128)
        halves = []
        for half in range(2):
            part = tile[:, half]
            mean = jnp.sum(jnp.sum(part, axis=0), axis=0, keepdims=True) / NS
            cent = ((part - mean) / math.sqrt(NS)).reshape(NS, 128)
            halves.append(cent.astype(jnp.bfloat16))
        cent = jnp.concatenate(halves, axis=1)
        cent_ref[:, 256 * pair : 256 * pair + 256] = cent
        light = lax.dot_general(
            cent[:128], cent[:128], (((1,), (1,)), ((), ())), preferred_element_type=jnp.float32
        )
        heavy = lax.dot_general(
            cent[128:], cent, (((1,), (1,)), ((), ())), preferred_element_type=jnp.float32
        )
        if pair == 0:
            part_ref[:128, :128] = light
            part_ref[128:, :] = heavy
        else:
            part_ref[:128, :128] += light
            part_ref[128:, :] += heavy
    eye = lax.broadcasted_iota(jnp.int32, (128, 128), 0) == lax.broadcasted_iota(
        jnp.int32, (128, 128), 1
    )
    trace = jnp.sum(
        jnp.where(eye, part_ref[:128, :128] + part_ref[128:, 128:], 0.0), keepdims=True
    )
    corner = jnp.logical_and(
        lax.broadcasted_iota(jnp.int32, (8, 128), 0) == 0,
        lax.broadcasted_iota(jnp.int32, (8, 128), 1) == 127,
    )
    part_ref[:8, :128] = jnp.where(corner, trace, part_ref[:8, :128])

    def rows_of(side, index):
        return pl.ds(pl.multiple_of(side * 128 + index * 8, 8), 8)

    slot = core * CHIPS + chip
    widths = (128, NS)

    def send_first(other, device, side):
        wide = pl.ds(0, widths[side])
        remote(
            part_ref.at[rows_of(side, other), wide],
            first.at[slot, :, wide],
            sem1.at[side],
            sem1.at[2],
            device,
        ).start()

    for other, device, side in around:
        send_first(other, device, side)
    by_core(lambda side, width: send_first(chip, sibling, 1 - side))

    def middle(side, width):
        wide = pl.ds(0, width)
        first[slot, :, wide] = part_ref[rows_of(side, chip), wide]
        landed = first.at[pl.ds(0, 2 * CHIPS - 1), :, wide]
        remote(landed, landed, sem1.at[0], sem1.at[2], sibling).wait_recv()
        own = jnp.sum(first[:, :, wide], axis=0)
        mine[:, wide] = own
        for hop in (4, 3, 5, 2, 6, 1, 7):
            device = (zs[hop] * NY + y, par)
            remote(
                mine.at[:, wide], second.at[z, :, wide], sem2.at[0], sem2.at[1], device
            ).start()
        second[z, :, wide] = own
        landed = second.at[pl.ds(0, NZ - 1), :, wide]
        remote(landed, landed, sem2.at[0], sem2.at[1], sibling).wait_recv()
        block = rows_of(side, chip)
        gram_ref[block, wide] = jnp.sum(second[:, :, wide], axis=0)
        done = gram_ref.at[block, wide]
        kind = 1 + y // 2 if side == 0 else 3
        for _, device, _ in around:
            remote(done, done, sem3.at[0], sem3.at[kind], device).start()
        remote(done, done, sem3.at[0], sem3.at[kind], sibling).start()

    by_core(middle)

    def await_rows(kind, count, width, own_kind):
        for less in range(2):

            @pl.when(own_kind if less else jnp.logical_not(own_kind))
            def _(less=less):
                landed = gram_ref.at[pl.ds(0, (count - less) * 8), pl.ds(0, width)]
                remote(landed, landed, sem3.at[0], sem3.at[kind], sibling).wait_recv()

    await_rows(1, 8, 128, jnp.logical_and(core == 0, y < 2))
    level = 1.0 / (gram_ref[0:1, 127:128] / NS)
    block_eye = lax.broadcasted_iota(jnp.int32, (BLOCK, BLOCK), 0) == lax.broadcasted_iota(
        jnp.int32, (BLOCK, BLOCK), 1
    )
    leading = gram_ref[:BLOCK, :BLOCK] * level + jnp.where(block_eye, 0.01, 0.0)
    factors = forward_block(leading, tile_ref, column_ref, cross_ref)
    energy_bytes = energies_ref.at[pl.ds(0, NSAMP - 1)]
    remote(energy_bytes, energy_bytes, esem.at[0], esem.at[1], sibling).wait()
    await_rows(2, 8, 128, jnp.logical_and(core == 0, y >= 2))
    await_rows(3, CHIPS, NS, core == 1)

    below = gram_ref[128:, :128]
    above = gram_ref[:128, :128]
    wide_corner = jnp.logical_and(
        lax.broadcasted_iota(jnp.int32, (128, 128), 0) == 0,
        lax.broadcasted_iota(jnp.int32, (128, 128), 1) == 127,
    )
    above = jnp.where(wide_corner, gram_ref[127:128, 0:1], above)
    gram = jnp.concatenate(
        [jnp.concatenate([above, below.T], axis=1), gram_ref[128:, :]], axis=0
    )
    diagonal = lax.broadcasted_iota(jnp.int32, (NS, NS), 0) == lax.broadcasted_iota(
        jnp.int32, (NS, NS), 1
    )
    pieces = jnp.broadcast_to(energies_ref[...], (NSAMP, LOCAL, 128)).reshape(NS, 128)
    lane = lax.broadcasted_iota(jnp.int32, (NS, 128), 1)
    row = lax.broadcasted_iota(jnp.int32, (NSAMP, LOCAL, 128), 1).reshape(NS, 128)
    energy = jnp.sum(jnp.where(lane == row, pieces, 0.0), axis=1, keepdims=True)
    mean = jnp.sum(energy, axis=0, keepdims=True) / NS
    residual = -(energy - mean) / math.sqrt(NS)
    work[:, :NS] = gram * level + jnp.where(diagonal, 0.01, 0.0)
    work[:, NS:] = jnp.broadcast_to(residual, (NS, 128))

    for index in range(NS // BLOCK):
        low = index * BLOCK
        own = slice(low, low + BLOCK)
        rest = slice(128 * ((index + 1) // 2), NS + 128)
        if index > 0:
            factors = forward_block(work[own, own], tile_ref, column_ref, cross_ref)
        lower, scaled = factors
        middle_rows = product(scaled, work[own, rest], 1, 0)
        outer = product(work[:, own], lower, 1, 1)
        work[:, rest] = work[:, rest] - product(outer, middle_rows, 1, 0)
        work[own, rest] = product(lower, middle_rows, 0, 0)

    coeff = work[:, NS:] * level
    held[...] = coeff
    own = held[pl.ds(pl.multiple_of(samp * LOCAL, LOCAL), LOCAL), :]
    here = lax.broadcasted_iota(jnp.int32, (LOCAL, 128), 0) == lax.broadcasted_iota(
        jnp.int32, (LOCAL, 128), 1
    )
    coeff_ref[...] = jnp.sum(jnp.where(here, own, 0.0), axis=0, keepdims=True)
    both = jnp.concatenate([coeff, coeff], axis=1)
    weighted = jnp.sum(gram * both, axis=0, keepdims=True)
    across = jnp.sum(jnp.where(diagonal, both, 0.0), axis=0, keepdims=True)
    square_total = jnp.sum(weighted * across, keepdims=True)
    scale_ref[...] = jnp.broadcast_to(lax.rsqrt(square_total / ENTRIES + 1e-06), (1, 128))
    left = lax.broadcasted_iota(jnp.int32, (1, 128), 1) < CH
    for pair in range(ROWS // 2):
        parts = []
        for half in range(2):
            column = 128 * (2 * pair + half)
            cent = cent_ref[:, column : column + 128].astype(jnp.float32)
            parts.append(jnp.sum(cent * coeff, axis=0, keepdims=True))
        turned = [jnp.concatenate([item[:, CH:], item[:, :CH]], axis=1) for item in parts]
        for half in range(2):
            at = samp * ROWS + 2 * pair + half
            swapped = jnp.logical_and(at >= 3 * CH, at < 6 * CH)
            parts[half], turned[half] = (
                jnp.where(swapped, turned[half], parts[half]),
                jnp.where(swapped, parts[half], turned[half]),
            )
        update_ref[0:1, 128 * pair : 128 * pair + 128] = jnp.where(left, parts[0], turned[1])
        update_ref[1:2, 128 * pair : 128 * pair + 128] = jnp.where(left, turned[0], parts[1])

    sent = send_ref.at[pl.ds(0, NSAMP - 1)]
    remote(sent, sent, send_sem, recv_sem.at[0], sibling).wait_send()

    def finish(side, width):
        wide = pl.ds(0, width)
        for kind in range(2):
            count = CHIPS - 1 if kind == side else CHIPS
            bytes_ref = gram_ref.at[pl.ds(0, count * 8), pl.ds(0, widths[kind])]
            remote(bytes_ref, bytes_ref, sem1.at[kind], sem1.at[2], sibling).wait_send()
        landed = second.at[pl.ds(0, NZ - 1), :, wide]
        remote(landed, landed, sem2.at[0], sem2.at[1], sibling).wait_send()
        landed = first.at[pl.ds(0, 2 * CHIPS - 1), :, wide]
        remote(landed, landed, sem3.at[0], sem1.at[2], sibling).wait_send()

    by_core(finish)


def main_call(activations, cotangents, spin_bits, off_row):
    whole = pl.BlockSpec(memory_space=VMEM)
    anywhere = pl.BlockSpec(memory_space=pl.ANY)
    dma = pltpu.SemaphoreType.DMA
    return pl.pallas_call(
        main_kernel,
        in_specs=[anywhere, anywhere, whole, whole],
        out_specs=[whole, whole, whole],
        out_shape=[
            jax.ShapeDtypeStruct((LAYERS, ROWS * CH), jnp.float32),
            jax.ShapeDtypeStruct((1, 128), jnp.float32),
            jax.ShapeDtypeStruct((1, 128), jnp.float32),
        ],
        scratch_shapes=[
            VMEM((LOCAL, LAYERS, CH, SITES), jnp.bfloat16),
            VMEM((LOCAL, LAYERS, CH, SITES), jnp.bfloat16),
            VMEM((2, CH, SITES), jnp.bfloat16),
            VMEM((2, LAYERS, 3 * CH, PADK), jnp.bfloat16),
            VMEM((2, LAYERS, 4 * CH, PADK), jnp.bfloat16),
            VMEM((NSAMP * CHUNK, 128), jnp.float32),
            VMEM((NSAMP, CHUNK, 128), jnp.bfloat16),
            VMEM((NSAMP, CHUNK, 128), jnp.bfloat16),
            VMEM((NS, WIDTH), jnp.bfloat16),
            VMEM((1, 128), jnp.float32),
            VMEM((NSAMP, 1, 128), jnp.float32),
            VMEM((NS, NS), jnp.float32),
            VMEM((2 * CHIPS, 8, NS), jnp.float32),
            VMEM((8, NS), jnp.float32),
            VMEM((NZ, 8, NS), jnp.float32),
            VMEM((NS, NS), jnp.float32),
            VMEM((NS, NS + 128), jnp.float32),
            VMEM((NS, 128), jnp.float32),
            VMEM((BLOCK // PANEL, 1, 8, 128), jnp.float32),
            VMEM((BLOCK // PANEL, PANEL, 8, 128), jnp.float32),
            VMEM((BLOCK // PANEL, PANEL, 8, 128), jnp.float32),
            dma((LOCAL,)),
            dma((LOCAL,)),
            dma,
            dma((NY,)),
            dma((2,)),
            dma((3,)),
            dma((2,)),
            dma((4,)),
        ],
        compiler_params=pltpu.CompilerParams(
            collective_id=0, has_side_effects=True, vmem_limit_bytes=VMEM_LIMIT
        ),
    )(activations, cotangents, spin_bits, off_row)


def scale_kernel(raw_ref, coeff_in, scale_ref, update_ref, coeff_ref):
    update_ref[...] = raw_ref[...] * scale_ref[:, :1]
    coeff_ref[...] = coeff_in[:, :LOCAL]


def scale_call(raw, coeff, scale):
    return pl.pallas_call(
        scale_kernel,
        out_shape=[
            jax.ShapeDtypeStruct((LAYERS, ROWS * CH), jnp.float32),
            jax.ShapeDtypeStruct((1, LOCAL), jnp.float32),
        ],
    )(raw, coeff, scale)


def on_device(activations, cotangents, spin_bits, offdiag_energy):
    raw, coeff_row, scale = main_call(
        activations, cotangents, spin_bits, offdiag_energy.reshape(1, LOCAL)
    )
    update, coeff = scale_call(raw, coeff_row, scale)
    return update, coeff.reshape(LOCAL)


def solution(mesh):
    in_specs = (
        P("samp", "par", None, None),
        P("samp", "par", None, None),
        P("samp", None),
        P("samp"),
    )
    out_specs = (P("par", "samp"), P("samp"))
    return jax.shard_map(
        on_device, mesh=mesh, in_specs=in_specs, out_specs=out_specs, check_vma=False
    )
```

time: 73.5 us -> 67.9 us (0.924)
  Pallas kernels: 72.6 us -> 67.1 us
    pallas_call x1, Pallas kernels: 13 us -> 1.38 us  [scale_call(): pl.pallas_call(scale_kernel, out_shape=[jax.ShapeDtypeStruct((LAYERS, ROW...]
    pallas_call x1, Pallas kernels: 59.6 us -> 65.7 us  [main_call(): pl.pallas_call(main_kernel, in_specs=[anywhere, anywhere, whole, whole],...]
where the time goes in v8:
time: 67.9 us; the launch traced here: 67.7 us
  Pallas kernels  67.1 us (99%)
    pallas_call x1, Pallas kernels, main_call(): pl.pallas_call(main_kernel, in_specs=[anywhere, anywhere, whole, whole],...  65.7 us
    pallas_call x1, Pallas kernels, scale_call(): pl.pallas_call(scale_kernel, out_shape=[jax.ShapeDtypeStruct((LAYERS, ROW...  1.38 us

profile of v8, /device:TPU:1, one launch (start us, length us, event | category | flops | bytes accessed | tf_op | source)
XLA Modules:
  0.0 67.7 jit_solution(5627451373824053985)
XLA Ops:
  0.6 65.7 %shard_map.59 = (f32[2,1152]{1,0:T(2,128)}, f32[1,128]{1,0:T(1,128)}, f32[1,128]{1,0:T(1,128)}) custom-call(bf16[8,2,64,576]{3,2,1,0:T(8,128)(2,1)} %act_hbm.1, bf16[8,2,64,576]{3,2,1,0:T(8,128)(2,1)} %cot_hbm.1, s32[8,576]{1,0:T(8,128)} %spin_ref.1, f32[1,8]{1,0:T(1,128)} %bitcast.2), custom_call_target="tpu_custom_call" | custom-call | tf_op jit(solution)/shard_map/pallas_call | solution.py:505
  66.4 1.4 %shard_map.60 = (f32[2,1152]{1,0:T(2,128)}, f32[1,8]{1,0:T(1,128)}) custom-call(f32[2,1152]{1,0:T(2,128)} %get-tuple-element.7.raw_ref, f32[1,128]{1,0:T(1,128)} %get-tuple-element.8.coeff_in, f32[1,128]{1,0:T(1,128)} %get-tuple-element.9.scale_ref), custom_call_target="tpu_custom_call" | custom-call | tf_op jit(solution)/shard_map/pallas_call | solution.py:557

commit v9 on v8

--- a/solution.py
+++ b/solution.py
@@ -179,7 +179,7 @@
 
 def main_kernel(
     act_hbm, cot_hbm, spin_ref, off_ref,
-    update_ref, coeff_ref, scale_ref,
+    update_ref, coeff_ref,
     act_ref, cot_ref, edges, lhs, rhs, wide_rows, send_ref, recv_ref, cent_ref,
     energy_ref, energies_ref, part_ref, first, mine, second, gram_ref,
     work, held, tile_ref, column_ref, cross_ref,
@@ -368,9 +368,12 @@
             device,
         ).start()
 
-    for other, device, side in around:
-        send_first(other, device, side)
-    by_core(lambda side, width: send_first(chip, sibling, 1 - side))
+    by_core(lambda side, width: send_first(chip, sibling, 0) if side == 1 else None)
+    for kind in range(2):
+        for other, device, side in around:
+            if side == kind:
+                send_first(other, device, side)
+    by_core(lambda side, width: send_first(chip, sibling, 1) if side == 0 else None)
 
     def middle(side, width):
         wide = pl.ds(0, width)
@@ -457,19 +460,19 @@
     here = lax.broadcasted_iota(jnp.int32, (LOCAL, 128), 0) == lax.broadcasted_iota(
         jnp.int32, (LOCAL, 128), 1
     )
-    coeff_ref[...] = jnp.sum(jnp.where(here, own, 0.0), axis=0, keepdims=True)
+    coeff_ref[...] = jnp.sum(jnp.where(here, own, 0.0), axis=0, keepdims=True)[:, :LOCAL]
     both = jnp.concatenate([coeff, coeff], axis=1)
     weighted = jnp.sum(gram * both, axis=0, keepdims=True)
     across = jnp.sum(jnp.where(diagonal, both, 0.0), axis=0, keepdims=True)
     square_total = jnp.sum(weighted * across, keepdims=True)
-    scale_ref[...] = jnp.broadcast_to(lax.rsqrt(square_total / ENTRIES + 1e-06), (1, 128))
+    scale = lax.rsqrt(square_total / ENTRIES + 1e-06)
     left = lax.broadcasted_iota(jnp.int32, (1, 128), 1) < CH
     for pair in range(ROWS // 2):
         parts = []
         for half in range(2):
             column = 128 * (2 * pair + half)
             cent = cent_ref[:, column : column + 128].astype(jnp.float32)
-            parts.append(jnp.sum(cent * coeff, axis=0, keepdims=True))
+            parts.append(jnp.sum(cent * coeff, axis=0, keepdims=True) * scale)
         turned = [jnp.concatenate([item[:, CH:], item[:, :CH]], axis=1) for item in parts]
         for half in range(2):
             at = samp * ROWS + 2 * pair + half
@@ -505,11 +508,10 @@
     return pl.pallas_call(
         main_kernel,
         in_specs=[anywhere, anywhere, whole, whole],
-        out_specs=[whole, whole, whole],
+        out_specs=[whole, whole],
         out_shape=[
             jax.ShapeDtypeStruct((LAYERS, ROWS * CH), jnp.float32),
-            jax.ShapeDtypeStruct((1, 128), jnp.float32),
-            jax.ShapeDtypeStruct((1, 128), jnp.float32),
+            jax.ShapeDtypeStruct((1, LOCAL), jnp.float32),
         ],
         scratch_shapes=[
             VMEM((LOCAL, LAYERS, CH, SITES), jnp.bfloat16),
@@ -548,26 +550,36 @@
     )(activations, cotangents, spin_bits, off_row)
 
 
-def scale_kernel(raw_ref, coeff_in, scale_ref, update_ref, coeff_ref):
-    update_ref[...] = raw_ref[...] * scale_ref[:, :1]
-    coeff_ref[...] = coeff_in[:, :LOCAL]
-
-
-def scale_call(raw, coeff, scale):
+def hand_on_kernel(update_in, coeff_in, update_ref, coeff_ref, sems):
+    copies = [
+        pltpu.make_async_copy(update_in, update_ref, sems.at[0]),
+        pltpu.make_async_copy(coeff_in, coeff_ref, sems.at[1]),
+    ]
+    for copy in copies:
+        copy.start()
+    for copy in copies:
+        copy.wait()
+
+
+def hand_on(update, coeff):
+    anywhere = pl.BlockSpec(memory_space=pl.ANY)
     return pl.pallas_call(
-        scale_kernel,
+        hand_on_kernel,
+        in_specs=[anywhere, anywhere],
+        out_specs=[anywhere, anywhere],
         out_shape=[
             jax.ShapeDtypeStruct((LAYERS, ROWS * CH), jnp.float32),
             jax.ShapeDtypeStruct((1, LOCAL), jnp.float32),
         ],
-    )(raw, coeff, scale)
+        scratch_shapes=[pltpu.SemaphoreType.DMA((2,))],
+        compiler_params=pltpu.CompilerParams(vmem_limit_bytes=VMEM_LIMIT),
+    )(update, coeff)
 
 
 def on_device(activations, cotangents, spin_bits, offdiag_energy):
-    raw, coeff_row, scale = main_call(
-        activations, cotangents, spin_bits, offdiag_energy.reshape(1, LOCAL)
-    )
-    update, coeff = scale_call(raw, coeff_row, scale)
+    update, coeff = hand_on(
+        *main_call(activations, cotangents, spin_bits, offdiag_energy.reshape(1, LOCAL))
+    )
     return update, coeff.reshape(LOCAL)
 
 

time: 67.9 us -> 67.9 us (level)
  no operation moved by 1% of the time
where the time goes in v9:
time: 67.9 us; the launch traced here: 67.8 us
  Pallas kernels  67.1 us (99%)
    pallas_call x1, Pallas kernels, main_call(): pl.pallas_call(main_kernel, in_specs=[anywhere, anywhere, whole, whole],...  65.7 us
    pallas_call x1, Pallas kernels, hand_on(): pl.pallas_call(hand_on_kernel, in_specs=[anywhere, anywhere], out_specs=[...  1.42 us

profile of v9, /device:TPU:1, one launch (start us, length us, event | category | flops | bytes accessed | tf_op | source)
XLA Modules:
  0.0 67.8 jit_solution(18097603316541789984)
XLA Ops:
  0.6 65.7 %shard_map.59 = (f32[2,1152]{1,0:T(2,128)}, f32[1,8]{1,0:T(1,128)}) custom-call(bf16[8,2,64,576]{3,2,1,0:T(8,128)(2,1)} %act_hbm.1, bf16[8,2,64,576]{3,2,1,0:T(8,128)(2,1)} %cot_hbm.1, s32[8,576]{1,0:T(8,128)} %spin_ref.1, f32[1,8]{1,0:T(1,128)} %bitcast.2), custom_call_target="tpu_custom_call" | custom-call | tf_op jit(solution)/shard_map/pallas_call | solution.py:508
  66.4 1.4 %shard_map.60 = (f32[2,1152]{1,0:T(2,128)}, f32[1,8]{1,0:T(1,128)}) custom-call(f32[2,1152]{1,0:T(2,128)} %get-tuple-element.6.update_in, f32[1,8]{1,0:T(1,128)} %get-tuple-element.7.coeff_in), custom_call_target="tpu_custom_call" | custom-call | tf_op jit(solution)/shard_map/pallas_call | solution.py:566

commit v10 on v9

--- a/solution.py
+++ b/solution.py
@@ -181,9 +181,9 @@
     act_hbm, cot_hbm, spin_ref, off_ref,
     update_ref, coeff_ref,
     act_ref, cot_ref, edges, lhs, rhs, wide_rows, send_ref, recv_ref, cent_ref,
-    energy_ref, energies_ref, part_ref, first, mine, second, gram_ref,
+    energy_ref, relay_ref, energies_ref, part_ref, first, mine, second, gram_ref,
     work, held, tile_ref, column_ref, cross_ref,
-    act_sem, cot_sem, send_sem, recv_sem, esem, sem1, sem2, sem3,
+    act_sem, cot_sem, send_sem, recv_sem, esem, relay_sem, sem1, sem2, sem3,
 ):
     samp = lax.axis_index("samp")
     par = lax.axis_index("par")
@@ -295,7 +295,24 @@
         return wide_rows[pl.ds(start, CHUNK), :].astype(jnp.bfloat16)
 
     pl.semaphore_wait(barrier, greeted)
-    for down, other in sorted_partners:
+    for down, other in sorted_partners[:NY]:
+        via = zs[2] if down < 2 else zs[6]
+        send_ref[other] = rounded(other)
+        remote(
+            send_ref.at[other], relay_ref.at[down], send_sem, relay_sem, (via * NY + y, par)
+        ).start()
+    for number, (down, other) in enumerate(sorted_partners[NY:]):
+        if number == 13:
+            remote(relay_ref, relay_ref, send_sem, relay_sem, sibling).wait_recv()
+            for turn in range(NY):
+                origin, goal = (zs[6], zs[2]) if turn < 2 else (zs[2], zs[6])
+                remote(
+                    relay_ref.at[turn],
+                    recv_ref.at[y * NZ + origin],
+                    send_sem,
+                    recv_sem.at[turn],
+                    (goal * NY + ys[turn], par),
+                ).start()
         send_ref[other] = rounded(other)
         remote(
             send_ref.at[other], recv_ref.at[slot_here], send_sem, recv_sem.at[down], (other, par)
@@ -486,6 +503,7 @@
 
     sent = send_ref.at[pl.ds(0, NSAMP - 1)]
     remote(sent, sent, send_sem, recv_sem.at[0], sibling).wait_send()
+    remote(relay_ref, relay_ref, send_sem, relay_sem, sibling).wait_send()
 
     def finish(side, width):
         wide = pl.ds(0, width)
@@ -524,6 +542,7 @@
             VMEM((NSAMP, CHUNK, 128), jnp.bfloat16),
             VMEM((NS, WIDTH), jnp.bfloat16),
             VMEM((1, 128), jnp.float32),
+            VMEM((NY, CHUNK, 128), jnp.bfloat16),
             VMEM((NSAMP, 1, 128), jnp.float32),
             VMEM((NS, NS), jnp.float32),
             VMEM((2 * CHIPS, 8, NS), jnp.float32),
@@ -540,6 +559,7 @@
             dma,
             dma((NY,)),
             dma((2,)),
+            dma,
             dma((3,)),
             dma((2,)),
             dma((4,)),

time: 67.9 us -> 68 us (level)
  no operation moved by 1% of the time
where the time goes in v10:
time: 68 us; the launch traced here: 67.9 us
  Pallas kernels  67.2 us (99%)
    pallas_call x1, Pallas kernels, main_call(): pl.pallas_call(main_kernel, in_specs=[anywhere, anywhere, whole, whole],...  65.8 us
    pallas_call x1, Pallas kernels, hand_on(): pl.pallas_call(hand_on_kernel, in_specs=[anywhere, anywhere], out_specs=[...  1.42 us

profile of v10, /device:TPU:1, one launch (start us, length us, event | category | flops | bytes accessed | tf_op | source)
XLA Modules:
  0.0 67.9 jit_solution(370830212304318872)
XLA Ops:
  0.6 65.8 %shard_map.59 = (f32[2,1152]{1,0:T(2,128)}, f32[1,8]{1,0:T(1,128)}) custom-call(bf16[8,2,64,576]{3,2,1,0:T(8,128)(2,1)} %act_hbm.1, bf16[8,2,64,576]{3,2,1,0:T(8,128)(2,1)} %cot_hbm.1, s32[8,576]{1,0:T(8,128)} %spin_ref.1, f32[1,8]{1,0:T(1,128)} %bitcast.2), custom_call_target="tpu_custom_call" | custom-call | tf_op jit(solution)/shard_map/pallas_call | solution.py:526
  66.4 1.4 %shard_map.60 = (f32[2,1152]{1,0:T(2,128)}, f32[1,8]{1,0:T(1,128)}) custom-call(f32[2,1152]{1,0:T(2,128)} %get-tuple-element.6.update_in, f32[1,8]{1,0:T(1,128)} %get-tuple-element.7.coeff_in), custom_call_target="tpu_custom_call" | custom-call | tf_op jit(solution)/shard_map/pallas_call | solution.py:586

commit v11 on v9

--- a/solution.py
+++ b/solution.py
@@ -72,7 +72,9 @@
     ((down, across) for down in range(NY) for across in range(4) if (down, across) != (0, 0)),
     key=lambda step: -(min(step[0], NY - step[0]) + min(step[1], 4 - step[1])),
 )
-RHS_ROWS = ((0, 1, 2), (1, 0, 3))
+PAIRS = 3 * CH // 2
+HALF = CHUNK // 2
+HEAD = 64
 CHIPS = 16
 
 
@@ -180,7 +182,7 @@
 def main_kernel(
     act_hbm, cot_hbm, spin_ref, off_ref,
     update_ref, coeff_ref,
-    act_ref, cot_ref, edges, lhs, rhs, wide_rows, send_ref, recv_ref, cent_ref,
+    act_ref, cot_ref, edges, lhs, rhs, stage, wide_rows, send_ref, recv_ref, cent_ref,
     energy_ref, energies_ref, part_ref, first, mine, second, gram_ref,
     work, held, tile_ref, column_ref, cross_ref,
     act_sem, cot_sem, send_sem, recv_sem, esem, sem1, sem2, sem3,
@@ -247,59 +249,79 @@
                     pl.semaphore_signal(barrier, inc=1, device_id=device, device_id_type=MESH)
                     greeted += 1
 
-    first_half = lax.broadcasted_iota(jnp.int32, (3 * CH, 128), 1) < CH
-    lhs[:, :, :, PADK - 128 :] = jnp.zeros((2, LAYERS, 3 * CH, 128), jnp.bfloat16)
-    rhs[:, :, :, PADK - 128 :] = jnp.zeros((2, LAYERS, 4 * CH, 128), jnp.bfloat16)
-    rhs[:, 1, 2 * CH : 3 * CH, :] = jnp.zeros((2, CH, PADK), jnp.bfloat16)
+    left = lax.broadcasted_iota(jnp.int32, (PAIRS, 128), 1) < CH
+    lhs[:, :, PADK - 128 :] = jnp.zeros((2, 3 * CH, 128), jnp.bfloat16)
+    rhs[:, :, PADK - 128 :] = jnp.zeros((2, 3 * CH, 128), jnp.bfloat16)
+    stage[:, 1] = jnp.zeros((2, 3 * CH, 128), jnp.float32)
     for at, step in enumerate((-1, 1)):
         strip = jnp.where(edge_mask((8, SITES), step), 1.0, 0.0)
         edges[at] = jnp.concatenate([strip] * (CH // 8), axis=0).astype(jnp.bfloat16)
 
-    def taps(slot, layer, width):
-        return lax.dot_general(
-            lhs[slot, layer], rhs[slot, layer, :width], (((1,), (1,)), ((), ())),
-            preferred_element_type=jnp.float32,
+    def compute(sample, layer, slot):
+        act = act_ref[sample, layer]
+        cot = cot_ref[sample, layer]
+        for step in (-1, 0, 1):
+            low = (step + 1) * CH
+            edge = edges[max(step, 0)] > 0
+            lhs[slot, low : low + CH, :SITES] = column_shift(act, step, edge)
+            rhs[slot, low : low + CH, :SITES] = rolled(cot, -LAT * step)
+        out = lax.dot_general(
+            lhs[slot], rhs[slot], (((1,), (1,)), ((), ())), preferred_element_type=jnp.float32
         )
-
-    def compute(sample, slot):
-        act_copy(sample).wait()
-        cot_copy(sample).wait()
-        for layer in range(LAYERS):
-            act = act_ref[sample, layer]
-            cot = cot_ref[sample, layer]
-            for step in (-1, 0, 1):
-                low = (step + 1) * CH
-                edge = edges[max(step, 0)] > 0
-                lhs[slot, layer, low : low + CH, :SITES] = column_shift(act, step, edge)
-                low = RHS_ROWS[layer][step + 1] * CH
-                rhs[slot, layer, low : low + CH, :SITES] = rolled(cot, -LAT * step)
-        one = taps(slot, 0, 3 * CH)
-        two = taps(slot, 1, 4 * CH)
+        stage[slot, 0] = out[:, :128]
+        stage[slot, 1, :, :CH] = out[:, 128:]
+        even, odd, even_last, odd_last = [
+            stage[slot, part, pl.ds(parity, PAIRS, stride=2), :]
+            for part in (0, 1)
+            for parity in (0, 1)
+        ]
         blocks = (
-            jnp.where(first_half, one[:, :128], two[:, :128]),
-            jnp.where(first_half, two[:, :128], one[:, :128]),
-            jnp.where(first_half, jnp.concatenate([one[:, 128:], one[:, 128:]], axis=1), two[:, 128:]),
+            jnp.where(left, even, pltpu.roll(odd, CH, 1)),
+            jnp.where(left, pltpu.roll(even, CH, 1), odd),
+            jnp.where(left, even_last, pltpu.roll(odd_last, CH, 1)),
         )
         for down in range(3):
-            wide_rows[pl.ds(down * 3 * CH * LOCAL + sample, 3 * CH, stride=LOCAL), :] = blocks[down]
-
-    def two_samples(pair, carry):
+            wide_rows[layer, pl.ds(down * PAIRS * LOCAL + sample, PAIRS, stride=LOCAL), :] = blocks[down]
+
+    def first_layer(pair, carry):
         for slot in range(2):
-            compute(pair * 2 + slot, slot)
+            sample = pair * 2 + slot
+            act_copy(sample).wait()
+            cot_copy(sample).wait()
+            compute(sample, 0, slot)
         return carry
 
-    lax.fori_loop(0, LOCAL // 2, two_samples, 0)
-
-    def rounded(other):
-        start = pl.multiple_of(other * CHUNK, CHUNK)
-        return wide_rows[pl.ds(start, CHUNK), :].astype(jnp.bfloat16)
-
+    def second_layer(pair, carry):
+        for slot in range(2):
+            compute(pair * 2 + slot, 1, slot)
+        return carry
+
+    def rounded(other, layer, low, rows):
+        start = pl.multiple_of(other * HALF + low, 8)
+        return wide_rows[layer, pl.ds(start, rows), :]
+
+    def send_wave(low, rows):
+        for down, other in sorted_partners:
+            if low == 0:
+                block = rounded(other, 0, 0, HEAD)
+            else:
+                block = jnp.concatenate(
+                    [rounded(other, 0, HEAD, HALF - HEAD), rounded(other, 1, 0, HALF)], axis=0
+                )
+            send_ref[other, low : low + rows] = block.astype(jnp.bfloat16)
+            remote(
+                send_ref.at[other, pl.ds(low, rows)],
+                recv_ref.at[slot_here, pl.ds(low, rows)],
+                send_sem,
+                recv_sem.at[down],
+                (other, par),
+            ).start()
+
+    lax.fori_loop(0, LOCAL // 2, first_layer, 0)
     pl.semaphore_wait(barrier, greeted)
-    for down, other in sorted_partners:
-        send_ref[other] = rounded(other)
-        remote(
-            send_ref.at[other], recv_ref.at[slot_here], send_sem, recv_sem.at[down], (other, par)
-        ).start()
+    send_wave(0, HEAD)
+    lax.fori_loop(0, LOCAL // 2, second_layer, 0)
+    send_wave(HEAD, CHUNK - HEAD)
 
     flat = diagonal_energy(spin_ref[...])
     energy_ref[...] = jnp.zeros_like(energy_ref)
@@ -307,7 +329,9 @@
     for _, other in partners:
         remote(energy_ref, energies_ref.at[samp], esem.at[0], esem.at[1], (other, par)).start()
     energies_ref[samp] = energy_ref[...]
-    recv_ref[slot_here] = rounded(samp)
+    recv_ref[slot_here] = jnp.concatenate(
+        [rounded(samp, layer, 0, HALF) for layer in range(LAYERS)], axis=0
+    ).astype(jnp.bfloat16)
     for down in range(NY):
         low = wrap(y + NY - down, NY) * NZ
         taken = recv_ref.at[pl.ds(0, NZ - 1)] if down == 0 else recv_ref.at[pl.ds(low, NZ)]
@@ -466,23 +490,12 @@
     across = jnp.sum(jnp.where(diagonal, both, 0.0), axis=0, keepdims=True)
     square_total = jnp.sum(weighted * across, keepdims=True)
     scale = lax.rsqrt(square_total / ENTRIES + 1e-06)
-    left = lax.broadcasted_iota(jnp.int32, (1, 128), 1) < CH
-    for pair in range(ROWS // 2):
-        parts = []
-        for half in range(2):
-            column = 128 * (2 * pair + half)
-            cent = cent_ref[:, column : column + 128].astype(jnp.float32)
-            parts.append(jnp.sum(cent * coeff, axis=0, keepdims=True) * scale)
-        turned = [jnp.concatenate([item[:, CH:], item[:, :CH]], axis=1) for item in parts]
-        for half in range(2):
-            at = samp * ROWS + 2 * pair + half
-            swapped = jnp.logical_and(at >= 3 * CH, at < 6 * CH)
-            parts[half], turned[half] = (
-                jnp.where(swapped, turned[half], parts[half]),
-                jnp.where(swapped, parts[half], turned[half]),
-            )
-        update_ref[0:1, 128 * pair : 128 * pair + 128] = jnp.where(left, parts[0], turned[1])
-        update_ref[1:2, 128 * pair : 128 * pair + 128] = jnp.where(left, turned[0], parts[1])
+    for index in range(ROWS):
+        cent = cent_ref[:, 128 * index : 128 * index + 128].astype(jnp.float32)
+        layer, column = index // (ROWS // 2), 128 * (index % (ROWS // 2))
+        update_ref[layer : layer + 1, column : column + 128] = (
+            jnp.sum(cent * coeff, axis=0, keepdims=True) * scale
+        )
 
     sent = send_ref.at[pl.ds(0, NSAMP - 1)]
     remote(sent, sent, send_sem, recv_sem.at[0], sibling).wait_send()
@@ -517,9 +530,10 @@
             VMEM((LOCAL, LAYERS, CH, SITES), jnp.bfloat16),
             VMEM((LOCAL, LAYERS, CH, SITES), jnp.bfloat16),
             VMEM((2, CH, SITES), jnp.bfloat16),
-            VMEM((2, LAYERS, 3 * CH, PADK), jnp.bfloat16),
-            VMEM((2, LAYERS, 4 * CH, PADK), jnp.bfloat16),
-            VMEM((NSAMP * CHUNK, 128), jnp.float32),
+            VMEM((2, 3 * CH, PADK), jnp.bfloat16),
+            VMEM((2, 3 * CH, PADK), jnp.bfloat16),
+            VMEM((2, 2, 3 * CH, 128), jnp.float32),
+            VMEM((LAYERS, NSAMP * HALF, 128), jnp.float32),
             VMEM((NSAMP, CHUNK, 128), jnp.bfloat16),
             VMEM((NSAMP, CHUNK, 128), jnp.bfloat16),
             VMEM((NS, WIDTH), jnp.bfloat16),

time: 67.9 us -> 66.9 us (0.985)
  Pallas kernels: 67.1 us -> 66.2 us
    pallas_call x1, Pallas kernels: 65.7 us -> 64.7 us  [main_call(): pl.pallas_call(main_kernel, in_specs=[anywhere, anywhere, whole, whole],...]
where the time goes in v11:
time: 66.9 us; the launch traced here: 66.8 us
  Pallas kernels  66.2 us (99%)
    pallas_call x1, Pallas kernels, main_call(): pl.pallas_call(main_kernel, in_specs=[anywhere, anywhere, whole, whole],...  64.7 us
    pallas_call x1, Pallas kernels, hand_on(): pl.pallas_call(hand_on_kernel, in_specs=[anywhere, anywhere], out_specs=[...  1.42 us

profile of v11, /device:TPU:1, one launch (start us, length us, event | category | flops | bytes accessed | tf_op | source)
XLA Modules:
  0.0 66.8 jit_solution(3020782116614477707)
XLA Ops:
  0.6 64.7 %shard_map.59 = (f32[2,1152]{1,0:T(2,128)}, f32[1,8]{1,0:T(1,128)}) custom-call(bf16[8,2,64,576]{3,2,1,0:T(8,128)(2,1)} %act_hbm.1, bf16[8,2,64,576]{3,2,1,0:T(8,128)(2,1)} %cot_hbm.1, s32[8,576]{1,0:T(8,128)} %spin_ref.1, f32[1,8]{1,0:T(1,128)} %bitcast.2), custom_call_target="tpu_custom_call" | custom-call | tf_op jit(solution)/shard_map/pallas_call | solution.py:521
  65.4 1.4 %shard_map.60 = (f32[2,1152]{1,0:T(2,128)}, f32[1,8]{1,0:T(1,128)}) custom-call(f32[2,1152]{1,0:T(2,128)} %get-tuple-element.6.update_in, f32[1,8]{1,0:T(1,128)} %get-tuple-element.7.coeff_in), custom_call_target="tpu_custom_call" | custom-call | tf_op jit(solution)/shard_map/pallas_call | solution.py:580

commit v12 on v11

--- a/solution.py
+++ b/solution.py
@@ -75,6 +75,7 @@
 PAIRS = 3 * CH // 2
 HALF = CHUNK // 2
 HEAD = 64
+SLOTS = 4
 CHIPS = 16
 
 
@@ -216,15 +217,20 @@
         def _():
             body(1, NS)
 
-    def act_copy(n):
-        return pltpu.make_async_copy(act_hbm.at[n], act_ref.at[n], act_sem.at[n])
-
-    def cot_copy(n):
-        return pltpu.make_async_copy(cot_hbm.at[n], cot_ref.at[n], cot_sem.at[n])
-
-    for n in range(LOCAL):
-        act_copy(n).start()
-        cot_copy(n).start()
+    def act_copy(n, layer):
+        return pltpu.make_async_copy(
+            act_hbm.at[n, layer], act_ref.at[n, layer], act_sem.at[layer, n]
+        )
+
+    def cot_copy(n, layer):
+        return pltpu.make_async_copy(
+            cot_hbm.at[n, layer], cot_ref.at[n, layer], cot_sem.at[layer, n]
+        )
+
+    for layer in range(LAYERS):
+        for n in range(LOCAL):
+            act_copy(n, layer).start()
+            cot_copy(n, layer).start()
 
     def remote(source, target, send, recv, device):
         return pltpu.make_async_remote_copy(
@@ -250,9 +256,9 @@
                     greeted += 1
 
     left = lax.broadcasted_iota(jnp.int32, (PAIRS, 128), 1) < CH
-    lhs[:, :, PADK - 128 :] = jnp.zeros((2, 3 * CH, 128), jnp.bfloat16)
-    rhs[:, :, PADK - 128 :] = jnp.zeros((2, 3 * CH, 128), jnp.bfloat16)
-    stage[:, 1] = jnp.zeros((2, 3 * CH, 128), jnp.float32)
+    lhs[:, :, PADK - 128 :] = jnp.zeros((SLOTS, 3 * CH, 128), jnp.bfloat16)
+    rhs[:, :, PADK - 128 :] = jnp.zeros((SLOTS, 3 * CH, 128), jnp.bfloat16)
+    stage[:, 1] = jnp.zeros((SLOTS, 3 * CH, 128), jnp.float32)
     for at, step in enumerate((-1, 1)):
         strip = jnp.where(edge_mask((8, SITES), step), 1.0, 0.0)
         edges[at] = jnp.concatenate([strip] * (CH // 8), axis=0).astype(jnp.bfloat16)
@@ -283,24 +289,23 @@
         for down in range(3):
             wide_rows[layer, pl.ds(down * PAIRS * LOCAL + sample, PAIRS, stride=LOCAL), :] = blocks[down]
 
-    def first_layer(pair, carry):
-        for slot in range(2):
-            sample = pair * 2 + slot
-            act_copy(sample).wait()
-            cot_copy(sample).wait()
-            compute(sample, 0, slot)
-        return carry
-
-    def second_layer(pair, carry):
-        for slot in range(2):
-            compute(pair * 2 + slot, 1, slot)
-        return carry
+    def products(layer):
+        def body(group, carry):
+            for slot in range(SLOTS):
+                sample = group * SLOTS + slot
+                act_copy(sample, layer).wait()
+                cot_copy(sample, layer).wait()
+            for slot in range(SLOTS):
+                compute(group * SLOTS + slot, layer, slot)
+            return carry
+
+        lax.fori_loop(0, LOCAL // SLOTS, body, 0)
 
     def rounded(other, layer, low, rows):
         start = pl.multiple_of(other * HALF + low, 8)
         return wide_rows[layer, pl.ds(start, rows), :]
 
-    def send_wave(low, rows):
+    def send_wave(wave, low, rows):
         for down, other in sorted_partners:
             if low == 0:
                 block = rounded(other, 0, 0, HEAD)
@@ -313,15 +318,15 @@
                 send_ref.at[other, pl.ds(low, rows)],
                 recv_ref.at[slot_here, pl.ds(low, rows)],
                 send_sem,
-                recv_sem.at[down],
+                recv_sem.at[wave, down],
                 (other, par),
             ).start()
 
-    lax.fori_loop(0, LOCAL // 2, first_layer, 0)
+    products(0)
     pl.semaphore_wait(barrier, greeted)
-    send_wave(0, HEAD)
-    lax.fori_loop(0, LOCAL // 2, second_layer, 0)
-    send_wave(HEAD, CHUNK - HEAD)
+    send_wave(0, 0, HEAD)
+    products(1)
+    send_wave(1, HEAD, CHUNK - HEAD)
 
     flat = diagonal_energy(spin_ref[...])
     energy_ref[...] = jnp.zeros_like(energy_ref)
@@ -332,12 +337,17 @@
     recv_ref[slot_here] = jnp.concatenate(
         [rounded(samp, layer, 0, HALF) for layer in range(LAYERS)], axis=0
     ).astype(jnp.bfloat16)
-    for down in range(NY):
-        low = wrap(y + NY - down, NY) * NZ
-        taken = recv_ref.at[pl.ds(0, NZ - 1)] if down == 0 else recv_ref.at[pl.ds(low, NZ)]
-        remote(taken, taken, send_sem, recv_sem.at[down], sibling).wait_recv()
-
+    def await_wave(wave, low, rows):
+        for down in range(NY):
+            at = wrap(y + NY - down, NY) * NZ
+            slots = pl.ds(0, NZ - 1) if down == 0 else pl.ds(at, NZ)
+            landed = recv_ref.at[slots, pl.ds(low, rows)]
+            remote(landed, landed, send_sem, recv_sem.at[wave, down], sibling).wait_recv()
+
+    await_wave(0, 0, HEAD)
     for pair in range(ROWS // 2):
+        if pair == HEAD // 16:
+            await_wave(1, HEAD, CHUNK - HEAD)
         tile = jnp.stack(
             [
                 recv_ref[(src % NY) * NZ + src // NY, 16 * pair : 16 * pair + 16, :].astype(jnp.float32)
@@ -432,39 +442,40 @@
                 landed = gram_ref.at[pl.ds(0, (count - less) * 8), pl.ds(0, width)]
                 remote(landed, landed, sem3.at[0], sem3.at[kind], sibling).wait_recv()
 
-    await_rows(1, 8, 128, jnp.logical_and(core == 0, y < 2))
-    level = 1.0 / (gram_ref[0:1, 127:128] / NS)
-    block_eye = lax.broadcasted_iota(jnp.int32, (BLOCK, BLOCK), 0) == lax.broadcasted_iota(
-        jnp.int32, (BLOCK, BLOCK), 1
-    )
-    leading = gram_ref[:BLOCK, :BLOCK] * level + jnp.where(block_eye, 0.01, 0.0)
-    factors = forward_block(leading, tile_ref, column_ref, cross_ref)
     energy_bytes = energies_ref.at[pl.ds(0, NSAMP - 1)]
     remote(energy_bytes, energy_bytes, esem.at[0], esem.at[1], sibling).wait()
-    await_rows(2, 8, 128, jnp.logical_and(core == 0, y >= 2))
-    await_rows(3, CHIPS, NS, core == 1)
-
-    below = gram_ref[128:, :128]
-    above = gram_ref[:128, :128]
-    wide_corner = jnp.logical_and(
-        lax.broadcasted_iota(jnp.int32, (128, 128), 0) == 0,
-        lax.broadcasted_iota(jnp.int32, (128, 128), 1) == 127,
-    )
-    above = jnp.where(wide_corner, gram_ref[127:128, 0:1], above)
-    gram = jnp.concatenate(
-        [jnp.concatenate([above, below.T], axis=1), gram_ref[128:, :]], axis=0
-    )
-    diagonal = lax.broadcasted_iota(jnp.int32, (NS, NS), 0) == lax.broadcasted_iota(
-        jnp.int32, (NS, NS), 1
-    )
     pieces = jnp.broadcast_to(energies_ref[...], (NSAMP, LOCAL, 128)).reshape(NS, 128)
     lane = lax.broadcasted_iota(jnp.int32, (NS, 128), 1)
     row = lax.broadcasted_iota(jnp.int32, (NSAMP, LOCAL, 128), 1).reshape(NS, 128)
     energy = jnp.sum(jnp.where(lane == row, pieces, 0.0), axis=1, keepdims=True)
     mean = jnp.sum(energy, axis=0, keepdims=True) / NS
     residual = -(energy - mean) / math.sqrt(NS)
+    work[:, NS:] = jnp.broadcast_to(residual, (NS, 128))
+
+    await_rows(1, 8, 128, jnp.logical_and(core == 0, y < 2))
+    level = 1.0 / (gram_ref[0:1, 127:128] / NS)
+    block_eye = lax.broadcasted_iota(jnp.int32, (BLOCK, BLOCK), 0) == lax.broadcasted_iota(
+        jnp.int32, (BLOCK, BLOCK), 1
+    )
+    leading = gram_ref[:BLOCK, :BLOCK] * level + jnp.where(block_eye, 0.01, 0.0)
+    factors = forward_block(leading, tile_ref, column_ref, cross_ref)
+    await_rows(2, 8, 128, jnp.logical_and(core == 0, y >= 2))
+    await_rows(3, CHIPS, NS, core == 1)
+
+    below = gram_ref[128:, :128]
+    above = gram_ref[:128, :128]
+    wide_corner = jnp.logical_and(
+        lax.broadcasted_iota(jnp.int32, (128, 128), 0) == 0,
+        lax.broadcasted_iota(jnp.int32, (128, 128), 1) == 127,
+    )
+    above = jnp.where(wide_corner, gram_ref[127:128, 0:1], above)
+    gram = jnp.concatenate(
+        [jnp.concatenate([above, below.T], axis=1), gram_ref[128:, :]], axis=0
+    )
+    diagonal = lax.broadcasted_iota(jnp.int32, (NS, NS), 0) == lax.broadcasted_iota(
+        jnp.int32, (NS, NS), 1
+    )
     work[:, :NS] = gram * level + jnp.where(diagonal, 0.01, 0.0)
-    work[:, NS:] = jnp.broadcast_to(residual, (NS, 128))
 
     for index in range(NS // BLOCK):
         low = index * BLOCK
@@ -498,7 +509,7 @@
         )
 
     sent = send_ref.at[pl.ds(0, NSAMP - 1)]
-    remote(sent, sent, send_sem, recv_sem.at[0], sibling).wait_send()
+    remote(sent, sent, send_sem, recv_sem.at[0, 0], sibling).wait_send()
 
     def finish(side, width):
         wide = pl.ds(0, width)
@@ -530,9 +541,9 @@
             VMEM((LOCAL, LAYERS, CH, SITES), jnp.bfloat16),
             VMEM((LOCAL, LAYERS, CH, SITES), jnp.bfloat16),
             VMEM((2, CH, SITES), jnp.bfloat16),
-            VMEM((2, 3 * CH, PADK), jnp.bfloat16),
-            VMEM((2, 3 * CH, PADK), jnp.bfloat16),
-            VMEM((2, 2, 3 * CH, 128), jnp.float32),
+            VMEM((SLOTS, 3 * CH, PADK), jnp.bfloat16),
+            VMEM((SLOTS, 3 * CH, PADK), jnp.bfloat16),
+            VMEM((SLOTS, 2, 3 * CH, 128), jnp.float32),
             VMEM((LAYERS, NSAMP * HALF, 128), jnp.float32),
             VMEM((NSAMP, CHUNK, 128), jnp.bfloat16),
             VMEM((NSAMP, CHUNK, 128), jnp.bfloat16),
@@ -549,10 +560,10 @@
             VMEM((BLOCK // PANEL, 1, 8, 128), jnp.float32),
             VMEM((BLOCK // PANEL, PANEL, 8, 128), jnp.float32),
             VMEM((BLOCK // PANEL, PANEL, 8, 128), jnp.float32),
-            dma((LOCAL,)),
-            dma((LOCAL,)),
+            dma((LAYERS, LOCAL)),
+            dma((LAYERS, LOCAL)),
             dma,
-            dma((NY,)),
+            dma((2, NY)),
             dma((2,)),
             dma((3,)),
             dma((2,)),

time: 66.9 us -> 66.7 us (level)
  no operation moved by 1% of the time
where the time goes in v12:
time: 66.7 us; the launch traced here: 66.5 us
  Pallas kernels  65.8 us (99%)
    pallas_call x1, Pallas kernels, main_call(): pl.pallas_call(main_kernel, in_specs=[anywhere, anywhere, whole, whole],...  64.4 us
    pallas_call x1, Pallas kernels, hand_on(): pl.pallas_call(hand_on_kernel, in_specs=[anywhere, anywhere], out_specs=[...  1.42 us

profile of v12, /device:TPU:1, one launch (start us, length us, event | category | flops | bytes accessed | tf_op | source)
XLA Modules:
  0.0 66.5 jit_solution(6556661824113673449)
XLA Ops:
  0.6 64.4 %shard_map.59 = (f32[2,1152]{1,0:T(2,128)}, f32[1,8]{1,0:T(1,128)}) custom-call(bf16[8,2,64,576]{3,2,1,0:T(8,128)(2,1)} %act_hbm.1, bf16[8,2,64,576]{3,2,1,0:T(8,128)(2,1)} %cot_hbm.1, s32[8,576]{1,0:T(8,128)} %spin_ref.1, f32[1,8]{1,0:T(1,128)} %bitcast.2), custom_call_target="tpu_custom_call" | custom-call | tf_op jit(solution)/shard_map/pallas_call | solution.py:532
  65.1 1.4 %shard_map.60 = (f32[2,1152]{1,0:T(2,128)}, f32[1,8]{1,0:T(1,128)}) custom-call(f32[2,1152]{1,0:T(2,128)} %get-tuple-element.6.update_in, f32[1,8]{1,0:T(1,128)} %get-tuple-element.7.coeff_in), custom_call_target="tpu_custom_call" | custom-call | tf_op jit(solution)/shard_map/pallas_call | solution.py:591

commit v13 on v12

--- a/solution.py
+++ b/solution.py
@@ -427,20 +427,19 @@
         block = rows_of(side, chip)
         gram_ref[block, wide] = jnp.sum(second[:, :, wide], axis=0)
         done = gram_ref.at[block, wide]
-        kind = 1 + y // 2 if side == 0 else 3
         for _, device, _ in around:
-            remote(done, done, sem3.at[0], sem3.at[kind], device).start()
-        remote(done, done, sem3.at[0], sem3.at[kind], sibling).start()
+            remote(done, done, sem3.at[0], sem3.at[1 + side], device).start()
+        remote(done, done, sem3.at[0], sem3.at[1 + side], sibling).start()
 
     by_core(middle)
 
-    def await_rows(kind, count, width, own_kind):
-        for less in range(2):
-
-            @pl.when(own_kind if less else jnp.logical_not(own_kind))
-            def _(less=less):
-                landed = gram_ref.at[pl.ds(0, (count - less) * 8), pl.ds(0, width)]
-                remote(landed, landed, sem3.at[0], sem3.at[kind], sibling).wait_recv()
+    def await_rows(kind):
+        def body(side, width):
+            count = CHIPS - 1 if side == kind else CHIPS
+            landed = gram_ref.at[pl.ds(0, count * 8), pl.ds(0, widths[kind])]
+            remote(landed, landed, sem3.at[0], sem3.at[1 + kind], sibling).wait_recv()
+
+        by_core(body)
 
     energy_bytes = energies_ref.at[pl.ds(0, NSAMP - 1)]
     remote(energy_bytes, energy_bytes, esem.at[0], esem.at[1], sibling).wait()
@@ -452,38 +451,53 @@
     residual = -(energy - mean) / math.sqrt(NS)
     work[:, NS:] = jnp.broadcast_to(residual, (NS, 128))
 
-    await_rows(1, 8, 128, jnp.logical_and(core == 0, y < 2))
+    await_rows(0)
     level = 1.0 / (gram_ref[0:1, 127:128] / NS)
-    block_eye = lax.broadcasted_iota(jnp.int32, (BLOCK, BLOCK), 0) == lax.broadcasted_iota(
-        jnp.int32, (BLOCK, BLOCK), 1
-    )
-    leading = gram_ref[:BLOCK, :BLOCK] * level + jnp.where(block_eye, 0.01, 0.0)
-    factors = forward_block(leading, tile_ref, column_ref, cross_ref)
-    await_rows(2, 8, 128, jnp.logical_and(core == 0, y >= 2))
-    await_rows(3, CHIPS, NS, core == 1)
-
-    below = gram_ref[128:, :128]
-    above = gram_ref[:128, :128]
     wide_corner = jnp.logical_and(
         lax.broadcasted_iota(jnp.int32, (128, 128), 0) == 0,
         lax.broadcasted_iota(jnp.int32, (128, 128), 1) == 127,
     )
-    above = jnp.where(wide_corner, gram_ref[127:128, 0:1], above)
-    gram = jnp.concatenate(
-        [jnp.concatenate([above, below.T], axis=1), gram_ref[128:, :]], axis=0
-    )
-    diagonal = lax.broadcasted_iota(jnp.int32, (NS, NS), 0) == lax.broadcasted_iota(
-        jnp.int32, (NS, NS), 1
-    )
-    work[:, :NS] = gram * level + jnp.where(diagonal, 0.01, 0.0)
-
-    for index in range(NS // BLOCK):
+    light = jnp.where(wide_corner, gram_ref[127:128, 0:1], gram_ref[:128, :128])
+    ridge = jnp.where(eye, 0.01, 0.0)
+    work[:128, :128] = light * level + ridge
+    one, two = slice(0, BLOCK), slice(BLOCK, 2 * BLOCK)
+    lower_one, scaled_one = forward_block(work[one, one], tile_ref, column_ref, cross_ref)
+    left = product(work[two, one], lower_one, 1, 1)
+    right = product(scaled_one, work[one, two], 1, 0)
+    lower_two, scaled_two = forward_block(
+        work[two, two] - product(left, right, 1, 0), tile_ref, column_ref, cross_ref
+    )
+    cross_part = product(left, scaled_one, 1, 0)
+    blank = jnp.zeros((BLOCK, BLOCK), jnp.float32)
+
+    def joined_factor(first_part, second_part):
+        return jnp.concatenate(
+            [
+                jnp.concatenate([first_part, blank], axis=1),
+                jnp.concatenate([-product(second_part, cross_part, 1, 0), second_part], axis=1),
+            ],
+            axis=0,
+        )
+
+    lower = joined_factor(lower_one, lower_two)
+    scaled = joined_factor(scaled_one, scaled_two)
+
+    await_rows(1)
+    below = gram_ref[128:, :128]
+    corner_block = gram_ref[128:, 128:]
+    scaled_below = below * level
+    work[:128, 128:NS] = scaled_below.T
+    work[128:, 128:NS] = corner_block * level + ridge
+    middle_rows = product(scaled, work[:128, 128:], 1, 0)
+    outer = product(scaled_below, lower, 1, 1)
+    work[128:, 128:] = work[128:, 128:] - product(outer, middle_rows, 1, 0)
+    work[:128, 128:] = product(lower, middle_rows, 0, 0)
+
+    for index in range(2, NS // BLOCK):
         low = index * BLOCK
         own = slice(low, low + BLOCK)
         rest = slice(128 * ((index + 1) // 2), NS + 128)
-        if index > 0:
-            factors = forward_block(work[own, own], tile_ref, column_ref, cross_ref)
-        lower, scaled = factors
+        lower, scaled = forward_block(work[own, own], tile_ref, column_ref, cross_ref)
         middle_rows = product(scaled, work[own, rest], 1, 0)
         outer = product(work[:, own], lower, 1, 1)
         work[:, rest] = work[:, rest] - product(outer, middle_rows, 1, 0)
@@ -496,10 +510,13 @@
         jnp.int32, (LOCAL, 128), 1
     )
     coeff_ref[...] = jnp.sum(jnp.where(here, own, 0.0), axis=0, keepdims=True)[:, :LOCAL]
-    both = jnp.concatenate([coeff, coeff], axis=1)
-    weighted = jnp.sum(gram * both, axis=0, keepdims=True)
-    across = jnp.sum(jnp.where(diagonal, both, 0.0), axis=0, keepdims=True)
-    square_total = jnp.sum(weighted * across, keepdims=True)
+    upper, under = coeff[:128], coeff[128:]
+    weighted = jnp.sum(light * upper + 2.0 * (below * under), axis=0, keepdims=True) * jnp.sum(
+        jnp.where(eye, upper, 0.0), axis=0, keepdims=True
+    ) + jnp.sum(corner_block * under, axis=0, keepdims=True) * jnp.sum(
+        jnp.where(eye, under, 0.0), axis=0, keepdims=True
+    )
+    square_total = jnp.sum(weighted, keepdims=True)
     scale = lax.rsqrt(square_total / ENTRIES + 1e-06)
     for index in range(ROWS):
         cent = cent_ref[:, 128 * index : 128 * index + 128].astype(jnp.float32)
@@ -567,7 +584,7 @@
             dma((2,)),
             dma((3,)),
             dma((2,)),
-            dma((4,)),
+            dma((3,)),
         ],
         compiler_params=pltpu.CompilerParams(
             collective_id=0, has_side_effects=True, vmem_limit_bytes=VMEM_LIMIT

time: 66.7 us -> 66.4 us (level)
  no operation moved by 1% of the time
where the time goes in v13:
time: 66.4 us; the launch traced here: 66.2 us
  Pallas kernels  65.6 us (99%)
    pallas_call x1, Pallas kernels, main_call(): pl.pallas_call(main_kernel, in_specs=[anywhere, anywhere, whole, whole],...  64.1 us
    pallas_call x1, Pallas kernels, hand_on(): pl.pallas_call(hand_on_kernel, in_specs=[anywhere, anywhere], out_specs=[...  1.42 us

profile of v13, /device:TPU:1, one launch (start us, length us, event | category | flops | bytes accessed | tf_op | source)
XLA Modules:
  0.0 66.2 jit_solution(16539920378238925616)
XLA Ops:
  0.6 64.1 %shard_map.59 = (f32[2,1152]{1,0:T(2,128)}, f32[1,8]{1,0:T(1,128)}) custom-call(bf16[8,2,64,576]{3,2,1,0:T(8,128)(2,1)} %act_hbm.1, bf16[8,2,64,576]{3,2,1,0:T(8,128)(2,1)} %cot_hbm.1, s32[8,576]{1,0:T(8,128)} %spin_ref.1, f32[1,8]{1,0:T(1,128)} %bitcast.2), custom_call_target="tpu_custom_call" | custom-call | tf_op jit(solution)/shard_map/pallas_call | solution.py:549
  64.8 1.4 %shard_map.60 = (f32[2,1152]{1,0:T(2,128)}, f32[1,8]{1,0:T(1,128)}) custom-call(f32[2,1152]{1,0:T(2,128)} %get-tuple-element.6.update_in, f32[1,8]{1,0:T(1,128)} %get-tuple-element.7.coeff_in), custom_call_target="tpu_custom_call" | custom-call | tf_op jit(solution)/shard_map/pallas_call | solution.py:608

commit v14 on v13

--- a/solution.py
+++ b/solution.py
@@ -75,6 +75,7 @@
 PAIRS = 3 * CH // 2
 HALF = CHUNK // 2
 HEAD = 64
+TAIL = 112
 SLOTS = 4
 CHIPS = 16
 
@@ -132,9 +133,13 @@
             for i in range(q + 1, PANEL):
                 up = c * low[i, p] - b * low[i, q]
                 down = a * low[i, q] - b * low[i, p]
+                ups[i, p], downs[i, p] = up * recip, down * recip
                 for m in range(q + 1, i + 1):
-                    low[i, m] = low[i, m] - (up * low[m, p] + down * low[m, q]) * recip
-                ups[i, p], downs[i, p] = up * recip, down * recip
+                    if i <= q + 2:
+                        step = (up * low[m, p] + down * low[m, q]) * recip
+                    else:
+                        step = ups[i, p] * low[m, p] + downs[i, p] * low[m, q]
+                    low[i, m] = low[i, m] - step
             if not last:
                 cross_scaled[p] = (c * cross[p] - b * cross[q]) * recip
                 cross_scaled[q] = (a * cross[q] - b * cross[p]) * recip
@@ -307,12 +312,14 @@
 
     def send_wave(wave, low, rows):
         for down, other in sorted_partners:
-            if low == 0:
+            if wave == 0:
                 block = rounded(other, 0, 0, HEAD)
+            elif wave == 1:
+                block = jnp.concatenate(
+                    [rounded(other, 0, HEAD, HALF - HEAD), rounded(other, 1, 0, TAIL - HALF)], axis=0
+                )
             else:
-                block = jnp.concatenate(
-                    [rounded(other, 0, HEAD, HALF - HEAD), rounded(other, 1, 0, HALF)], axis=0
-                )
+                block = rounded(other, 1, TAIL - HALF, CHUNK - TAIL)
             send_ref[other, low : low + rows] = block.astype(jnp.bfloat16)
             remote(
                 send_ref.at[other, pl.ds(low, rows)],
@@ -326,7 +333,8 @@
     pl.semaphore_wait(barrier, greeted)
     send_wave(0, 0, HEAD)
     products(1)
-    send_wave(1, HEAD, CHUNK - HEAD)
+    send_wave(1, HEAD, TAIL - HEAD)
+    send_wave(2, TAIL, CHUNK - TAIL)
 
     flat = diagonal_energy(spin_ref[...])
     energy_ref[...] = jnp.zeros_like(energy_ref)
@@ -344,10 +352,21 @@
             landed = recv_ref.at[slots, pl.ds(low, rows)]
             remote(landed, landed, send_sem, recv_sem.at[wave, down], sibling).wait_recv()
 
+    def heavy_part(pair):
+        columns = pl.ds(256 * pair, 256)
+        heavy = lax.dot_general(
+            cent_ref[128:, columns], cent_ref[:, columns], (((1,), (1,)), ((), ())),
+            preferred_element_type=jnp.float32,
+        )
+        part_ref[128:, :] = heavy if pair == 0 else part_ref[128:, :] + heavy
+
+    squares = jnp.zeros((8, 256), jnp.float32)
     await_wave(0, 0, HEAD)
     for pair in range(ROWS // 2):
         if pair == HEAD // 16:
-            await_wave(1, HEAD, CHUNK - HEAD)
+            await_wave(1, HEAD, TAIL - HEAD)
+        if pair == TAIL // 16:
+            await_wave(2, TAIL, CHUNK - TAIL)
         tile = jnp.stack(
             [
                 recv_ref[(src % NY) * NZ + src // NY, 16 * pair : 16 * pair + 16, :].astype(jnp.float32)
@@ -365,20 +384,17 @@
         light = lax.dot_general(
             cent[:128], cent[:128], (((1,), (1,)), ((), ())), preferred_element_type=jnp.float32
         )
-        heavy = lax.dot_general(
-            cent[128:], cent, (((1,), (1,)), ((), ())), preferred_element_type=jnp.float32
-        )
-        if pair == 0:
-            part_ref[:128, :128] = light
-            part_ref[128:, :] = heavy
-        else:
-            part_ref[:128, :128] += light
-            part_ref[128:, :] += heavy
+        part_ref[:128, :128] = light if pair == 0 else part_ref[:128, :128] + light
+        wide = cent[128:].astype(jnp.float32)
+        squares = squares + jnp.sum((wide * wide).reshape(16, 8, 256), axis=0)
+        if pair < TAIL // 16:
+            heavy_part(pair)
+
     eye = lax.broadcasted_iota(jnp.int32, (128, 128), 0) == lax.broadcasted_iota(
         jnp.int32, (128, 128), 1
     )
-    trace = jnp.sum(
-        jnp.where(eye, part_ref[:128, :128] + part_ref[128:, 128:], 0.0), keepdims=True
+    trace = jnp.sum(jnp.where(eye, part_ref[:128, :128], 0.0), keepdims=True) + jnp.sum(
+        squares, keepdims=True
     )
     corner = jnp.logical_and(
         lax.broadcasted_iota(jnp.int32, (8, 128), 0) == 0,
@@ -404,6 +420,9 @@
 
     by_core(lambda side, width: send_first(chip, sibling, 0) if side == 1 else None)
     for kind in range(2):
+        if kind == 1:
+            for pair in range(TAIL // 16, ROWS // 2):
+                heavy_part(pair)
         for other, device, side in around:
             if side == kind:
                 send_first(other, device, side)
@@ -580,7 +599,7 @@
             dma((LAYERS, LOCAL)),
             dma((LAYERS, LOCAL)),
             dma,
-            dma((2, NY)),
+            dma((3, NY)),
             dma((2,)),
             dma((3,)),
             dma((2,)),

time: 66.4 us -> 65.9 us (level)
  no operation moved by 1% of the time
where the time goes in v14:
time: 65.9 us; the launch traced here: 65.8 us
  Pallas kernels  65.1 us (99%)
    pallas_call x1, Pallas kernels, main_call(): pl.pallas_call(main_kernel, in_specs=[anywhere, anywhere, whole, whole],...  63.7 us
    pallas_call x1, Pallas kernels, hand_on(): pl.pallas_call(hand_on_kernel, in_specs=[anywhere, anywhere], out_specs=[...  1.42 us

profile of v14, /device:TPU:1, one launch (start us, length us, event | category | flops | bytes accessed | tf_op | source)
XLA Modules:
  0.0 65.8 jit_solution(8003522183639325327)
XLA Ops:
  0.6 63.7 %shard_map.59 = (f32[2,1152]{1,0:T(2,128)}, f32[1,8]{1,0:T(1,128)}) custom-call(bf16[8,2,64,576]{3,2,1,0:T(8,128)(2,1)} %act_hbm.1, bf16[8,2,64,576]{3,2,1,0:T(8,128)(2,1)} %cot_hbm.1, s32[8,576]{1,0:T(8,128)} %spin_ref.1, f32[1,8]{1,0:T(1,128)} %bitcast.2), custom_call_target="tpu_custom_call" | custom-call | tf_op jit(solution)/shard_map/pallas_call | solution.py:568
  64.3 1.4 %shard_map.60 = (f32[2,1152]{1,0:T(2,128)}, f32[1,8]{1,0:T(1,128)}) custom-call(f32[2,1152]{1,0:T(2,128)} %get-tuple-element.6.update_in, f32[1,8]{1,0:T(1,128)} %get-tuple-element.7.coeff_in), custom_call_target="tpu_custom_call" | custom-call | tf_op jit(solution)/shard_map/pallas_call | solution.py:627

commit v15 on v14

--- a/solution.py
+++ b/solution.py
@@ -76,7 +76,7 @@
 HALF = CHUNK // 2
 HEAD = 64
 TAIL = 112
-SLOTS = 4
+SLOTS = 8
 CHIPS = 16
 
 
@@ -505,22 +505,35 @@
     below = gram_ref[128:, :128]
     corner_block = gram_ref[128:, 128:]
     scaled_below = below * level
-    work[:128, 128:NS] = scaled_below.T
-    work[128:, 128:NS] = corner_block * level + ridge
+    above = scaled_below.T
+    last = corner_block * level + ridge
+    near_middle = product(scaled, above[:, :BLOCK], 1, 0)
+    near_outer = product(scaled_below[:BLOCK], lower, 1, 1)
+    lower_three, scaled_three = forward_block(
+        last[:BLOCK, :BLOCK] - product(near_outer, near_middle, 1, 0), tile_ref, column_ref, cross_ref
+    )
+    work[:128, 128:NS] = above
+    work[128:, 128:NS] = last
     middle_rows = product(scaled, work[:128, 128:], 1, 0)
     outer = product(scaled_below, lower, 1, 1)
     work[128:, 128:] = work[128:, 128:] - product(outer, middle_rows, 1, 0)
     work[:128, 128:] = product(lower, middle_rows, 0, 0)
 
-    for index in range(2, NS // BLOCK):
-        low = index * BLOCK
-        own = slice(low, low + BLOCK)
-        rest = slice(128 * ((index + 1) // 2), NS + 128)
-        lower, scaled = forward_block(work[own, own], tile_ref, column_ref, cross_ref)
-        middle_rows = product(scaled, work[own, rest], 1, 0)
-        outer = product(work[:, own], lower, 1, 1)
-        work[:, rest] = work[:, rest] - product(outer, middle_rows, 1, 0)
-        work[own, rest] = product(lower, middle_rows, 0, 0)
+    three, four = slice(128, 128 + BLOCK), slice(128 + BLOCK, NS)
+    near_middle = product(scaled_three, work[three, four], 1, 0)
+    near_outer = product(work[four, three], lower_three, 1, 1)
+    lower_four, scaled_four = forward_block(
+        work[four, four] - product(near_outer, near_middle, 1, 0), tile_ref, column_ref, cross_ref
+    )
+    middle_rows = product(scaled_three, work[three, 128:], 1, 0)
+    outer = product(work[:, three], lower_three, 1, 1)
+    work[:, 128:] = work[:, 128:] - product(outer, middle_rows, 1, 0)
+    work[three, 128:] = product(lower_three, middle_rows, 0, 0)
+
+    middle_rows = product(scaled_four, work[four, NS:], 1, 0)
+    outer = product(work[:, four], lower_four, 1, 1)
+    work[:, NS:] = work[:, NS:] - product(outer, middle_rows, 1, 0)
+    work[four, NS:] = product(lower_four, middle_rows, 0, 0)
 
     coeff = work[:, NS:] * level
     held[...] = coeff

time: 65.9 us -> 66.3 us (level)
  no operation moved by 1% of the time
where the time goes in v15:
time: 66.3 us; the launch traced here: 66.1 us
  Pallas kernels  65.3 us (98%)
  between operations  0.8 us (1%)
    pallas_call x1, Pallas kernels, main_call(): pl.pallas_call(main_kernel, in_specs=[anywhere, anywhere, whole, whole],...  63.8 us
    pallas_call x1, Pallas kernels, hand_on(): pl.pallas_call(hand_on_kernel, in_specs=[anywhere, anywhere], out_specs=[...  1.42 us

profile of v15, /device:TPU:1, one launch (start us, length us, event | category | flops | bytes accessed | tf_op | source)
XLA Modules:
  0.0 66.1 jit_solution(11175864727545038412)
XLA Ops:
  0.6 63.8 %shard_map.59 = (f32[2,1152]{1,0:T(2,128)}, f32[1,8]{1,0:T(1,128)}) custom-call(bf16[8,2,64,576]{3,2,1,0:T(8,128)(2,1)} %act_hbm.1, bf16[8,2,64,576]{3,2,1,0:T(8,128)(2,1)} %cot_hbm.1, s32[8,576]{1,0:T(8,128)} %spin_ref.1, f32[1,8]{1,0:T(1,128)} %bitcast.2), custom_call_target="tpu_custom_call" | custom-call | tf_op jit(solution)/shard_map/pallas_call | solution.py:581
  64.5 1.4 %shard_map.60 = (f32[2,1152]{1,0:T(2,128)}, f32[1,8]{1,0:T(1,128)}) custom-call(f32[2,1152]{1,0:T(2,128)} %get-tuple-element.6.update_in, f32[1,8]{1,0:T(1,128)} %get-tuple-element.7.coeff_in), custom_call_target="tpu_custom_call" | custom-call | tf_op jit(solution)/shard_map/pallas_call | solution.py:640

commit v16 on v15

--- a/solution.py
+++ b/solution.py
@@ -76,7 +76,7 @@
 HALF = CHUNK // 2
 HEAD = 64
 TAIL = 112
-SLOTS = 8
+SLOTS = 2
 CHIPS = 16
 
 

time: 66.3 us -> 65.5 us (0.988)
  no operation moved by 1% of the time
where the time goes in v16:
time: 65.5 us; the launch traced here: 65.3 us
  Pallas kernels  64.7 us (99%)
    pallas_call x1, Pallas kernels, main_call(): pl.pallas_call(main_kernel, in_specs=[anywhere, anywhere, whole, whole],...  63.3 us
    pallas_call x1, Pallas kernels, hand_on(): pl.pallas_call(hand_on_kernel, in_specs=[anywhere, anywhere], out_specs=[...  1.42 us

profile of v16, /device:TPU:1, one launch (start us, length us, event | category | flops | bytes accessed | tf_op | source)
XLA Modules:
  0.0 65.3 jit_solution(13595523104289872746)
XLA Ops:
  0.6 63.3 %shard_map.59 = (f32[2,1152]{1,0:T(2,128)}, f32[1,8]{1,0:T(1,128)}) custom-call(bf16[8,2,64,576]{3,2,1,0:T(8,128)(2,1)} %act_hbm.1, bf16[8,2,64,576]{3,2,1,0:T(8,128)(2,1)} %cot_hbm.1, s32[8,576]{1,0:T(8,128)} %spin_ref.1, f32[1,8]{1,0:T(1,128)} %bitcast.2), custom_call_target="tpu_custom_call" | custom-call | tf_op jit(solution)/shard_map/pallas_call | solution.py:581
  63.9 1.4 %shard_map.60 = (f32[2,1152]{1,0:T(2,128)}, f32[1,8]{1,0:T(1,128)}) custom-call(f32[2,1152]{1,0:T(2,128)} %get-tuple-element.6.update_in, f32[1,8]{1,0:T(1,128)} %get-tuple-element.7.coeff_in), custom_call_target="tpu_custom_call" | custom-call | tf_op jit(solution)/shard_map/pallas_call | solution.py:640

commit v17 on v16

--- a/solution.py
+++ b/solution.py
@@ -222,20 +222,19 @@
         def _():
             body(1, NS)
 
-    def act_copy(n, layer):
-        return pltpu.make_async_copy(
-            act_hbm.at[n, layer], act_ref.at[n, layer], act_sem.at[layer, n]
-        )
-
-    def cot_copy(n, layer):
-        return pltpu.make_async_copy(
-            cot_hbm.at[n, layer], cot_ref.at[n, layer], cot_sem.at[layer, n]
-        )
-
-    for layer in range(LAYERS):
-        for n in range(LOCAL):
-            act_copy(n, layer).start()
-            cot_copy(n, layer).start()
+    def fetches(group, layer):
+        samples = pl.ds(group * SLOTS, SLOTS) if layer == 0 else pl.ds(0, LOCAL)
+        return [
+            pltpu.make_async_copy(
+                hbm.at[samples, layer], local.at[samples, layer], sems.at[group]
+            )
+            for hbm, local, sems in ((act_hbm, act_ref, act_sem), (cot_hbm, cot_ref, cot_sem))
+        ]
+
+    groups = LOCAL // SLOTS
+    for group in range(groups):
+        for fetch in fetches(group, 0):
+            fetch.start()
 
     def remote(source, target, send, recv, device):
         return pltpu.make_async_remote_copy(
@@ -296,15 +295,14 @@
 
     def products(layer):
         def body(group, carry):
-            for slot in range(SLOTS):
-                sample = group * SLOTS + slot
-                act_copy(sample, layer).wait()
-                cot_copy(sample, layer).wait()
+            if layer == 0:
+                for fetch in fetches(group, 0):
+                    fetch.wait()
             for slot in range(SLOTS):
                 compute(group * SLOTS + slot, layer, slot)
             return carry
 
-        lax.fori_loop(0, LOCAL // SLOTS, body, 0)
+        lax.fori_loop(0, groups, body, 0)
 
     def rounded(other, layer, low, rows):
         start = pl.multiple_of(other * HALF + low, 8)
@@ -332,6 +330,10 @@
     products(0)
     pl.semaphore_wait(barrier, greeted)
     send_wave(0, 0, HEAD)
+    for fetch in fetches(groups, 1):
+        fetch.start()
+    for fetch in fetches(groups, 1):
+        fetch.wait()
     products(1)
     send_wave(1, HEAD, TAIL - HEAD)
     send_wave(2, TAIL, CHUNK - TAIL)
@@ -609,8 +611,8 @@
             VMEM((BLOCK // PANEL, 1, 8, 128), jnp.float32),
             VMEM((BLOCK // PANEL, PANEL, 8, 128), jnp.float32),
             VMEM((BLOCK // PANEL, PANEL, 8, 128), jnp.float32),
-            dma((LAYERS, LOCAL)),
-            dma((LAYERS, LOCAL)),
+            dma((LOCAL // SLOTS + 1,)),
+            dma((LOCAL // SLOTS + 1,)),
             dma,
             dma((3, NY)),
             dma((2,)),

time: 65.5 us -> 65.2 us (level)
  no operation moved by 1% of the time
where the time goes in v17:
time: 65.2 us; the launch traced here: 65 us
  Pallas kernels  64.4 us (99%)
    pallas_call x1, Pallas kernels, main_call(): pl.pallas_call(main_kernel, in_specs=[anywhere, anywhere, whole, whole],...  63 us
    pallas_call x1, Pallas kernels, hand_on(): pl.pallas_call(hand_on_kernel, in_specs=[anywhere, anywhere], out_specs=[...  1.42 us

profile of v17, /device:TPU:1, one launch (start us, length us, event | category | flops | bytes accessed | tf_op | source)
XLA Modules:
  0.0 65.0 jit_solution(7628079110939890595)
XLA Ops:
  0.6 63.0 %shard_map.59 = (f32[2,1152]{1,0:T(2,128)}, f32[1,8]{1,0:T(1,128)}) custom-call(bf16[8,2,64,576]{3,2,1,0:T(8,128)(2,1)} %act_hbm.1, bf16[8,2,64,576]{3,2,1,0:T(8,128)(2,1)} %cot_hbm.1, s32[8,576]{1,0:T(8,128)} %spin_ref.1, f32[1,8]{1,0:T(1,128)} %bitcast.2), custom_call_target="tpu_custom_call" | custom-call | tf_op jit(solution)/shard_map/pallas_call | solution.py:583
  63.6 1.4 %shard_map.60 = (f32[2,1152]{1,0:T(2,128)}, f32[1,8]{1,0:T(1,128)}) custom-call(f32[2,1152]{1,0:T(2,128)} %get-tuple-element.6.update_in, f32[1,8]{1,0:T(1,128)} %get-tuple-element.7.coeff_in), custom_call_target="tpu_custom_call" | custom-call | tf_op jit(solution)/shard_map/pallas_call | solution.py:642

commit v18 on v17

--- a/solution.py
+++ b/solution.py
@@ -75,7 +75,7 @@
 PAIRS = 3 * CH // 2
 HALF = CHUNK // 2
 HEAD = 64
-TAIL = 112
+TAIL = 128
 SLOTS = 2
 CHIPS = 16
 
@@ -111,10 +111,8 @@
         base = panel * PANEL
         last = panel == count - 1
         tile_ref[panel, 0] = tiles[panel]
-        for j in range(PANEL):
-            column_ref[panel, j] = columns[j]
         low = {
-            (i, j): broadcast_row(column_ref, panel, j, i)
+            (i, j): jnp.broadcast_to(columns[j][i : i + 1], (8, 128))
             for i in range(PANEL)
             for j in range(i + 1)
         }

time: 65.2 us -> 65.7 us (level)
  no operation moved by 1% of the time
where the time goes in v18:
time: 65.7 us; the launch traced here: 65.6 us
  Pallas kernels  64.9 us (99%)
    pallas_call x1, Pallas kernels, main_call(): pl.pallas_call(main_kernel, in_specs=[anywhere, anywhere, whole, whole],...  63.5 us
    pallas_call x1, Pallas kernels, hand_on(): pl.pallas_call(hand_on_kernel, in_specs=[anywhere, anywhere], out_specs=[...  1.42 us

profile of v18, /device:TPU:1, one launch (start us, length us, event | category | flops | bytes accessed | tf_op | source)
XLA Modules:
  0.0 65.6 jit_solution(1549620756964520580)
XLA Ops:
  0.6 63.5 %shard_map.59 = (f32[2,1152]{1,0:T(2,128)}, f32[1,8]{1,0:T(1,128)}) custom-call(bf16[8,2,64,576]{3,2,1,0:T(8,128)(2,1)} %act_hbm.1, bf16[8,2,64,576]{3,2,1,0:T(8,128)(2,1)} %cot_hbm.1, s32[8,576]{1,0:T(8,128)} %spin_ref.1, f32[1,8]{1,0:T(1,128)} %bitcast.2), custom_call_target="tpu_custom_call" | custom-call | tf_op jit(solution)/shard_map/pallas_call | solution.py:581
  64.1 1.4 %shard_map.60 = (f32[2,1152]{1,0:T(2,128)}, f32[1,8]{1,0:T(1,128)}) custom-call(f32[2,1152]{1,0:T(2,128)} %get-tuple-element.6.update_in, f32[1,8]{1,0:T(1,128)} %get-tuple-element.7.coeff_in), custom_call_target="tpu_custom_call" | custom-call | tf_op jit(solution)/shard_map/pallas_call | solution.py:640

commit v19 on v17

--- a/solution.py
+++ b/solution.py
@@ -75,8 +75,9 @@
 PAIRS = 3 * CH // 2
 HALF = CHUNK // 2
 HEAD = 64
-TAIL = 112
-SLOTS = 2
+TAIL = 128
+SLOTS = 4
+PAIR = 2
 CHIPS = 16
 
 
@@ -223,7 +224,7 @@
             body(1, NS)
 
     def fetches(group, layer):
-        samples = pl.ds(group * SLOTS, SLOTS) if layer == 0 else pl.ds(0, LOCAL)
+        samples = pl.ds(group * PAIR, PAIR) if layer == 0 else pl.ds(0, LOCAL)
         return [
             pltpu.make_async_copy(
                 hbm.at[samples, layer], local.at[samples, layer], sems.at[group]
@@ -231,7 +232,7 @@
             for hbm, local, sems in ((act_hbm, act_ref, act_sem), (cot_hbm, cot_ref, cot_sem))
         ]
 
-    groups = LOCAL // SLOTS
+    groups = LOCAL // PAIR
     for group in range(groups):
         for fetch in fetches(group, 0):
             fetch.start()
@@ -294,15 +295,15 @@
             wide_rows[layer, pl.ds(down * PAIRS * LOCAL + sample, PAIRS, stride=LOCAL), :] = blocks[down]
 
     def products(layer):
-        def body(group, carry):
-            if layer == 0:
-                for fetch in fetches(group, 0):
-                    fetch.wait()
+        def body(step, carry):
             for slot in range(SLOTS):
-                compute(group * SLOTS + slot, layer, slot)
+                if layer == 0 and slot % PAIR == 0:
+                    for fetch in fetches(step * (SLOTS // PAIR) + slot // PAIR, 0):
+                        fetch.wait()
+                compute(step * SLOTS + slot, layer, slot)
             return carry
 
-        lax.fori_loop(0, groups, body, 0)
+        lax.fori_loop(0, LOCAL // SLOTS, body, 0)
 
     def rounded(other, layer, low, rows):
         start = pl.multiple_of(other * HALF + low, 8)
@@ -611,8 +612,8 @@
             VMEM((BLOCK // PANEL, 1, 8, 128), jnp.float32),
             VMEM((BLOCK // PANEL, PANEL, 8, 128), jnp.float32),
             VMEM((BLOCK // PANEL, PANEL, 8, 128), jnp.float32),
-            dma((LOCAL // SLOTS + 1,)),
-            dma((LOCAL // SLOTS + 1,)),
+            dma((LOCAL // PAIR + 1,)),
+            dma((LOCAL // PAIR + 1,)),
             dma,
             dma((3, NY)),
             dma((2,)),

time: 65.2 us -> 65.4 us (level)
  no operation moved by 1% of the time
where the time goes in v19:
time: 65.4 us; the launch traced here: 65.2 us
  Pallas kernels  64.5 us (99%)
    pallas_call x1, Pallas kernels, main_call(): pl.pallas_call(main_kernel, in_specs=[anywhere, anywhere, whole, whole],...  63.1 us
    pallas_call x1, Pallas kernels, hand_on(): pl.pallas_call(hand_on_kernel, in_specs=[anywhere, anywhere], out_specs=[...  1.42 us

profile of v19, /device:TPU:1, one launch (start us, length us, event | category | flops | bytes accessed | tf_op | source)
XLA Modules:
  0.0 65.2 jit_solution(9957021461211578873)
XLA Ops:
  0.6 63.1 %shard_map.59 = (f32[2,1152]{1,0:T(2,128)}, f32[1,8]{1,0:T(1,128)}) custom-call(bf16[8,2,64,576]{3,2,1,0:T(8,128)(2,1)} %act_hbm.1, bf16[8,2,64,576]{3,2,1,0:T(8,128)(2,1)} %cot_hbm.1, s32[8,576]{1,0:T(8,128)} %spin_ref.1, f32[1,8]{1,0:T(1,128)} %bitcast.2), custom_call_target="tpu_custom_call" | custom-call | tf_op jit(solution)/shard_map/pallas_call | solution.py:584
  63.8 1.4 %shard_map.60 = (f32[2,1152]{1,0:T(2,128)}, f32[1,8]{1,0:T(1,128)}) custom-call(f32[2,1152]{1,0:T(2,128)} %get-tuple-element.6.update_in, f32[1,8]{1,0:T(1,128)} %get-tuple-element.7.coeff_in), custom_call_target="tpu_custom_call" | custom-call | tf_op jit(solution)/shard_map/pallas_call | solution.py:643
